TPU v7x, 32 devices: a whole 2x2x4 slice. The times are simulated.
32 devices in a mesh: tm: 8 (over z, y), head: 4 (over x, core).
Axes of the slice: x: 2, y: 2, z: 4, core: 2. Of those that a mesh axis runs over, the one named last changes fastest.
Arguments:
- queries: bfloat16 [8, 384, 24, 128], P('tm', None, 'head'), may hold values from -40 to 40
- key_vectors: bfloat16 [8, 384, 24, 128], P('tm', None, 'head'), may hold values from -40 to 40
- value_vectors: bfloat16 [8, 384, 24, 128], P('tm', None, 'head'), may hold values from -6 to 6
- head_class: int32 [24], replicated, may hold values from 0 to 1, as said below
- frame_mask: int32 [4, 4], replicated, may hold values from 0 to 1, as said below
Outputs:
- attended: bfloat16 [8, 384, 24, 128], P('tm', None, 'head')
Inputs may be any that keep to these rules, and one draw needn't show every extreme that they name: `head_class`: head group g holds heads g * 6 to g * 6 + 5; each group holds 1 or 5 temporal heads, and groups 2k and 2k + 1 hold 6 temporal heads together. `frame_mask`: the diagonal is all ones.
All inputs are finite; a program needn't handle non-finite values.
Results may differ from a plain program's by a relative error of at most 0.0042.
Values may be sent and summed in bfloat16 or wider, within the bound.
No kernel may reach another device: no remote copies, remote signals or barrier semaphores. Data moves between devices by JAX's collectives and lax.ppermute only.
A program may use at most 64 MiB of HBM per device.

v0:
```python
import jax
import jax.numpy as jnp
from jax import lax
from jax.sharding import PartitionSpec as P


def frame_attend(triple):
    query_block, key_block, value_block = triple
    score_scale = query_block.shape[-1] ** (-0.5)
    scores = (
        jnp.einsum("id,jd->ij", query_block, key_block, preferred_element_type=jnp.float32)
        * score_scale
    )
    peak = jnp.max(scores, axis=-1, keepdims=True)
    exponent = jnp.exp(scores - peak)
    totals = jnp.sum(exponent, axis=-1, keepdims=True)
    blended = jnp.dot(
        exponent.astype(jnp.bfloat16), value_block, preferred_element_type=jnp.float32
    )
    return (blended / totals).astype(jnp.bfloat16)


def run_spatial(triple):
    moved = tuple((jnp.moveaxis(a[0], 1, 0) for a in triple))
    blended = lax.map(frame_attend, moved)
    return jnp.moveaxis(blended, 0, 1)[None]


def run_temporal(triple, frame_mask):
    query_block = lax.all_to_all(triple[0], "tm", split_axis=1, concat_axis=0, tiled=True)
    key_block = lax.all_to_all(triple[1], "tm", split_axis=1, concat_axis=0, tiled=True)
    value_block = lax.all_to_all(triple[2], "tm", split_axis=1, concat_axis=0, tiled=True)
    score_scale = query_block.shape[-1] ** (-0.5)
    frame_total = query_block.shape[0]
    block_total = frame_mask.shape[0]
    frame_block = jnp.arange(frame_total, dtype=jnp.int32) // (frame_total // block_total)
    onehot = (frame_block[:, None] == jnp.arange(block_total, dtype=jnp.int32)[None, :]).astype(
        jnp.float32
    )
    allowed = jnp.dot(jnp.dot(onehot, frame_mask.astype(jnp.float32)), onehot.T) > 0.5
    scores = (
        jnp.einsum("fpmd,gpmd->pmfg", query_block, key_block, preferred_element_type=jnp.float32)
        * score_scale
    )
    scores = jnp.where(allowed, scores, jnp.float32(-1e30))
    peak = jnp.max(scores, axis=-1, keepdims=True)
    exponent = jnp.where(allowed, jnp.exp(scores - peak), jnp.float32(0.0))
    totals = jnp.sum(exponent, axis=-1)
    blended = jnp.einsum(
        "pmfg,gpmd->fpmd",
        exponent.astype(jnp.bfloat16),
        value_block,
        preferred_element_type=jnp.float32,
    )
    result = (blended / jnp.transpose(totals, (2, 0, 1))[..., None]).astype(jnp.bfloat16)
    return lax.all_to_all(result, "tm", split_axis=0, concat_axis=1, tiled=True)


def per_device(queries, key_vectors, value_vectors, head_class, frame_mask):
    group_heads = queries.shape[2]
    moved_heads = group_heads // 3
    half_heads = group_heads // 2
    least_count = half_heads - moved_heads
    most_count = half_heads + moved_heads
    head_group = lax.axis_index("head")
    local_class = lax.dynamic_slice_in_dim(head_class, head_group * group_heads, group_heads)
    sorted_heads = jnp.argsort(local_class, stable=True)
    head_rank = jnp.argsort(sorted_heads)
    temporal_count = jnp.sum(local_class)
    position = jnp.arange(group_heads, dtype=jnp.int32)
    spatial_in = tuple(
        (
            jnp.take(a, sorted_heads[:most_count], axis=2)
            for a in (queries, key_vectors, value_vectors)
        )
    )
    temporal_in = tuple(
        (
            jnp.take(a, sorted_heads[least_count:], axis=2)
            for a in (queries, key_vectors, value_vectors)
        )
    )
    spatial_out = run_spatial(spatial_in)
    temporal_out = run_temporal(temporal_in, frame_mask)
    result_pool = jnp.concatenate([spatial_out, temporal_out], axis=2)
    slot_index = jnp.where(
        position < group_heads - temporal_count, position, most_count + position - least_count
    )
    return jnp.take(result_pool, jnp.take(slot_index, head_rank), axis=2)


def solution(mesh):
    return jax.shard_map(
        per_device,
        mesh=mesh,
        in_specs=(
            P("tm", None, "head", None),
            P("tm", None, "head", None),
            P("tm", None, "head", None),
            P(),
            P(),
        ),
        out_specs=P("tm", None, "head", None),
        check_vma=False,
    )
```

profile of v0, /device:TPU:0, one launch (start us, length us, event | category | flops | bytes accessed | tf_op | source)
XLA Modules:
  0.0 107.3 jit_solution(8365484432126445365)
XLA Ops:
  0.0 0.7 copy-done.7
  0.7 0.7 fusion.40
  1.5 1.0 sort.34
  5.3 1.1 %bitcast_select_fusion.3 = (bf16[1,384,5,128]{3,1,2,0:T(8,128)(2,1)}, bf16[1,384,5,128]{3,1,2,0:T(8,128)(2,1)S(1)}, bf16[1,384,5,128]{3,1,2,0:T(8,128)(2,1)}) fusion(bf16[5,384,128]{2,1,0:T(8,128)(2,1)S(1)} %gather_fusion.5, pred[5]{0:T(512)(128)(4,1)S(1)} %get-tuple-element.63, bf16[5,384,128]{2,1,0:T(8,128)(2,1)S(1)} %gather_fusion.6, ...), kind=kLoop, calls=%fused_computation.38 | loop fusion | flops 737280 | bytes 2949125 | tf_op jit(solution)/shard_map/jit(_take)/select_n | solution.py:79
  6.4 1.2 %copy.65 = bf16[1,384,5,128]{3,2,0,1:T(8,128)(2,1)} copy(bf16[1,384,5,128]{3,1,2,0:T(8,128)(2,1)S(1)} %get-tuple-element.66) | data formatting | bytes 983040 | tf_op jit(solution)/shard_map/jit(_take)/select_n | solution.py:79
  7.7 7.4 %all-to-all-start.1 = ((bf16[1,384,5,128]{3,2,0,1:T(8,128)(2,1)}), bf16[1,384,5,128]{3,2,0,1:T(8,128)(2,1)S(1)}, u32[]{:S(2)}, u32[]{:S(2)}) async-start(bf16[1,384,5,128]{3,2,0,1:T(8,128)(2,1)} %copy.65), calls=%async_computation.1 | async-start | bytes 1572864 | tf_op jit(solution)/shard_map/all_to_all | solution.py:30
  15.1 1.3 %copy.67 = bf16[1,384,5,128]{3,2,0,1:T(8,128)(2,1)} copy(bf16[1,384,5,128]{3,1,2,0:T(8,128)(2,1)S(1)} %copy-done.5) | data formatting | bytes 983040 | tf_op jit(solution)/shard_map/jit(_take)/select_n | solution.py:79
  16.4 18.9 %all-to-all-done.1 = bf16[1,384,5,128]{3,2,0,1:T(8,128)(2,1)S(1)} async-done(((bf16[1,384,5,128]{3,2,0,1:T(8,128)(2,1)}), bf16[1,384,5,128]{3,2,0,1:T(8,128)(2,1)S(1)}, u32[]{:S(2)}, u32[]{:S(2)}) %all-to-all-start.1) | async-done | bytes 491552 | tf_op jit(solution)/shard_map/all_to_all | solution.py:30
  35.3 3.6 %all-to-all-start.2 = ((bf16[1,384,5,128]{3,2,0,1:T(8,128)(2,1)}), bf16[1,384,5,128]{3,2,0,1:T(8,128)(2,1)S(1)}, u32[]{:S(2)}, u32[]{:S(2)}) async-start(bf16[1,384,5,128]{3,2,0,1:T(8,128)(2,1)} %copy.67), calls=%async_computation.2 | async-start | bytes 1572864 | tf_op jit(solution)/shard_map/all_to_all | solution.py:31
  38.8 2.3 %copy.63 = bf16[1,384,5,128]{3,2,0,1:T(8,128)(2,1)} copy(bf16[1,384,5,128]{3,1,2,0:T(8,128)(2,1)} %get-tuple-element.65) | data formatting | bytes 983040 | tf_op jit(solution)/shard_map/jit(_take)/select_n | solution.py:79
  41.1 18.1 %all-to-all-done.2 = bf16[1,384,5,128]{3,2,0,1:T(8,128)(2,1)S(1)} async-done(((bf16[1,384,5,128]{3,2,0,1:T(8,128)(2,1)}), bf16[1,384,5,128]{3,2,0,1:T(8,128)(2,1)S(1)}, u32[]{:S(2)}, u32[]{:S(2)}) %all-to-all-start.2) | async-done | bytes 491552 | tf_op jit(solution)/shard_map/all_to_all | solution.py:31
  59.2 0.9 copy-done.3
  60.1 4.2 %all-to-all-start = ((bf16[1,384,5,128]{3,2,0,1:T(8,128)(2,1)}), bf16[1,384,5,128]{3,2,0,1:T(8,128)(2,1)}, u32[]{:S(2)}, u32[]{:S(2)}) async-start(bf16[1,384,5,128]{3,2,0,1:T(8,128)(2,1)} %copy.63), calls=%async_computation | async-start | bytes 1572864 | tf_op jit(solution)/shard_map/all_to_all | solution.py:32
  66.7 1.2 %fusion.23 = (bf16[5,384,128]{2,1,0:T(8,128)(2,1)}, bf16[5,384,128]{2,1,0:T(8,128)(2,1)}, bf16[5,384,128]{2,1,0:T(8,128)(2,1)}) fusion(bf16[5,384,128]{2,1,0:T(8,128)(2,1)S(1)} %gather_fusion.4, pred[5]{0:T(512)(128)(4,1)S(1)} %get-tuple-element.52, bf16[5,384,128]{2,1,0:T(8,128)(2,1)S(1)} %gather_fusion.3, bf16[5,384,128]{2,1,0:T(8,128)(2,1)S(1)} %gather_fusion.2), kind=kLoop, calls=%fused_computation.40 | loop fusion | flops 737280 | bytes 2949125 | tf_op jit(solution)/shard_map/transpose | solution.py:24
  68.0 0.8 fusion.26
  69.8 14.4 %all-to-all-done = bf16[1,384,5,128]{3,2,0,1:T(8,128)(2,1)} async-done(((bf16[1,384,5,128]{3,2,0,1:T(8,128)(2,1)}), bf16[1,384,5,128]{3,2,0,1:T(8,128)(2,1)}, u32[]{:S(2)}, u32[]{:S(2)}) %all-to-all-start) | async-done | bytes 491552 | tf_op jit(solution)/shard_map/all_to_all | solution.py:32
  84.2 1.7 %fusion.17 = bf16[8,48,5,128]{3,0,2,1:T(8,128)(2,1)S(1)} fusion(bf16[48,5,8,8]{3,2,1,0:T(8,128)(2,1)S(1)} %copy.73, bf16[8,48,5,128]{3,2,1,0:T(8,128)(2,1)} %bitcast.24, f32[8,48,5]{0,2,1:T(8,128)S(1)} %copy.74), kind=kOutput, calls=%fused_computation.28 | convolution fusion | flops 4423680 | bytes 1021440 | tf_op jit(solution)/shard_map/pmfg,gpmd->fpmd/dot_general | solution.py:49
  85.9 0.8 copy.75
  86.7 3.6 %all-to-all-start.3 = ((bf16[8,48,5,128]{3,1,2,0:T(8,128)(2,1)}), bf16[8,48,5,128]{3,1,2,0:T(8,128)(2,1)S(1)}, u32[]{:S(2)}, u32[]{:S(2)}) async-start(bf16[8,48,5,128]{3,1,2,0:T(8,128)(2,1)} %copy.75), calls=%async_computation.3 | async-start | bytes 983040 | tf_op jit(solution)/shard_map/all_to_all | solution.py:56
  90.3 12.8 %while.10 = (s32[]{:T(128)}, bf16[5,384,128]{2,1,0:T(8,128)(2,1)S(1)}, bf16[5,384,128]{2,1,0:T(8,128)(2,1)}, bf16[5,384,128]{2,1,0:T(8,128)(2,1)}, bf16[5,384,128]{2,1,0:T(8,128)(2,1)}, /*index=5*/s32[]{:T(128)}) while((s32[]{:T(128)}, bf16[5,384,128]{2,1,0:T(8,128)(2,1)S(1)}, bf16[5,384,128]{2,1,0:T(8,128)(2,1)}, ...), condition=%wide.region_6.8_spmd, body=%wide.region_3.0_spmd.sunk | while | flops 76479744 | bytes 2173509 | solution.py:25
  90.4 1.2 %fusion.51 = (f32[384]{0:T(512)S(1)}, f32[384,384]{0,1:T(8,128)S(1)}) fusion(bf16[5,384,128]{2,1,0:T(8,128)(2,1)} %get-tuple-element.121, s32[]{:T(128)} %get-tuple-element.112, bf16[5,384,128]{2,1,0:T(8,128)(2,1)} %get-tuple-element.120), kind=kOutput, calls=%fused_computation.77.clone.1 | convolution fusion | flops 38043264 | bytes 788992 | tf_op jit(solution)/shard_map/while/body/eval_jaxpr/id,jd->ij/dot_general | solution.py:11
  91.7 1.2 %fusion.53 = bf16[5,384,128]{2,1,0:T(8,128)(2,1)S(1)} fusion(bf16[5,384,128]{2,1,0:T(8,128)(2,1)S(1)} %get-tuple-element.113, s32[]{:T(128)} %get-tuple-element.112, f32[384,384]{0,1:T(8,128)S(1)} %get-tuple-element.104, f32[384]{0:T(512)S(1)} %get-tuple-element.105, f32[384]{0:T(512)S(1)} %fusion.52, bf16[5,384,128]{2,1,0:T(8,128)(2,1)} %get-tuple-element.122), kind=kOutput, calls=%fused_computation.12.clone.1 | convolution fusion | flops 38141952 | bytes 791552 | tf_op jit(solution)/shard_map/while/body/eval_jaxpr/dot_general | solution.py:17
  92.9 1.2 %fusion.51 = (f32[384]{0:T(512)S(1)}, f32[384,384]{0,1:T(8,128)S(1)}) fusion(bf16[5,384,128]{2,1,0:T(8,128)(2,1)} %get-tuple-element.121, s32[]{:T(128)} %get-tuple-element.112, bf16[5,384,128]{2,1,0:T(8,128)(2,1)} %get-tuple-element.120), kind=kOutput, calls=%fused_computation.77.clone.1 | convolution fusion | flops 38043264 | bytes 788992 | tf_op jit(solution)/shard_map/while/body/eval_jaxpr/id,jd->ij/dot_general | solution.py:11
  94.3 1.2 %fusion.53 = bf16[5,384,128]{2,1,0:T(8,128)(2,1)S(1)} fusion(bf16[5,384,128]{2,1,0:T(8,128)(2,1)S(1)} %get-tuple-element.113, s32[]{:T(128)} %get-tuple-element.112, f32[384,384]{0,1:T(8,128)S(1)} %get-tuple-element.104, f32[384]{0:T(512)S(1)} %get-tuple-element.105, f32[384]{0:T(512)S(1)} %fusion.52, bf16[5,384,128]{2,1,0:T(8,128)(2,1)} %get-tuple-element.122), kind=kOutput, calls=%fused_computation.12.clone.1 | convolution fusion | flops 38141952 | bytes 791552 | tf_op jit(solution)/shard_map/while/body/eval_jaxpr/dot_general | solution.py:17
  95.5 1.2 %fusion.51 = (f32[384]{0:T(512)S(1)}, f32[384,384]{0,1:T(8,128)S(1)}) fusion(bf16[5,384,128]{2,1,0:T(8,128)(2,1)} %get-tuple-element.121, s32[]{:T(128)} %get-tuple-element.112, bf16[5,384,128]{2,1,0:T(8,128)(2,1)} %get-tuple-element.120), kind=kOutput, calls=%fused_computation.77.clone.1 | convolution fusion | flops 38043264 | bytes 788992 | tf_op jit(solution)/shard_map/while/body/eval_jaxpr/id,jd->ij/dot_general | solution.py:11
  96.8 1.2 %fusion.53 = bf16[5,384,128]{2,1,0:T(8,128)(2,1)S(1)} fusion(bf16[5,384,128]{2,1,0:T(8,128)(2,1)S(1)} %get-tuple-element.113, s32[]{:T(128)} %get-tuple-element.112, f32[384,384]{0,1:T(8,128)S(1)} %get-tuple-element.104, f32[384]{0:T(512)S(1)} %get-tuple-element.105, f32[384]{0:T(512)S(1)} %fusion.52, bf16[5,384,128]{2,1,0:T(8,128)(2,1)} %get-tuple-element.122), kind=kOutput, calls=%fused_computation.12.clone.1 | convolution fusion | flops 38141952 | bytes 791552 | tf_op jit(solution)/shard_map/while/body/eval_jaxpr/dot_general | solution.py:17
  98.1 1.2 %fusion.51 = (f32[384]{0:T(512)S(1)}, f32[384,384]{0,1:T(8,128)S(1)}) fusion(bf16[5,384,128]{2,1,0:T(8,128)(2,1)} %get-tuple-element.121, s32[]{:T(128)} %get-tuple-element.112, bf16[5,384,128]{2,1,0:T(8,128)(2,1)} %get-tuple-element.120), kind=kOutput, calls=%fused_computation.77.clone.1 | convolution fusion | flops 38043264 | bytes 788992 | tf_op jit(solution)/shard_map/while/body/eval_jaxpr/id,jd->ij/dot_general | solution.py:11
  99.4 1.2 %fusion.53 = bf16[5,384,128]{2,1,0:T(8,128)(2,1)S(1)} fusion(bf16[5,384,128]{2,1,0:T(8,128)(2,1)S(1)} %get-tuple-element.113, s32[]{:T(128)} %get-tuple-element.112, f32[384,384]{0,1:T(8,128)S(1)} %get-tuple-element.104, f32[384]{0:T(512)S(1)} %get-tuple-element.105, f32[384]{0:T(512)S(1)} %fusion.52, bf16[5,384,128]{2,1,0:T(8,128)(2,1)} %get-tuple-element.122), kind=kOutput, calls=%fused_computation.12.clone.1 | convolution fusion | flops 38141952 | bytes 791552 | tf_op jit(solution)/shard_map/while/body/eval_jaxpr/dot_general | solution.py:17
  100.6 1.2 %fusion.51 = (f32[384]{0:T(512)S(1)}, f32[384,384]{0,1:T(8,128)S(1)}) fusion(bf16[5,384,128]{2,1,0:T(8,128)(2,1)} %get-tuple-element.121, s32[]{:T(128)} %get-tuple-element.112, bf16[5,384,128]{2,1,0:T(8,128)(2,1)} %get-tuple-element.120), kind=kOutput, calls=%fused_computation.77.clone.1 | convolution fusion | flops 38043264 | bytes 788992 | tf_op jit(solution)/shard_map/while/body/eval_jaxpr/id,jd->ij/dot_general | solution.py:11
  102.0 1.2 %fusion.53 = bf16[5,384,128]{2,1,0:T(8,128)(2,1)S(1)} fusion(bf16[5,384,128]{2,1,0:T(8,128)(2,1)S(1)} %get-tuple-element.113, s32[]{:T(128)} %get-tuple-element.112, f32[384,384]{0,1:T(8,128)S(1)} %get-tuple-element.104, f32[384]{0:T(512)S(1)} %get-tuple-element.105, f32[384]{0:T(512)S(1)} %fusion.52, bf16[5,384,128]{2,1,0:T(8,128)(2,1)} %get-tuple-element.122), kind=kOutput, calls=%fused_computation.12.clone.1 | convolution fusion | flops 38141952 | bytes 791552 | tf_op jit(solution)/shard_map/while/body/eval_jaxpr/dot_general | solution.py:17
  103.2 1.0 sort.35
  106.4 0.9 bitcast_select_fusion
  (48 shorter events, 8.4 us)
Async XLA Ops:
  0.0 2.5 %copy-start = (bf16[1,384,6,128]{3,1,2,0:T(8,128)(2,1)S(1)}, bf16[1,384,6,128]{3,1,2,0:T(8,128)(2,1)}, u32[]{:S(2)}) copy-start(bf16[1,384,6,128]{3,1,2,0:T(8,128)(2,1)} %param.11) | copy-start | bytes 1769476
  0.0 0.7 copy-start.7
  2.5 1.1 copy-start.1
  3.6 1.1 copy-start.2
  7.7 7.4 %copy-start.5 = (bf16[1,384,5,128]{3,1,2,0:T(8,128)(2,1)S(1)}, bf16[1,384,5,128]{3,1,2,0:T(8,128)(2,1)}, u32[]{:S(2)}) copy-start(bf16[1,384,5,128]{3,1,2,0:T(8,128)(2,1)} %get-tuple-element.67) | copy-start | bytes 1474564
  7.7 27.6 %all-to-all-start.1 = ((bf16[1,384,5,128]{3,2,0,1:T(8,128)(2,1)}), bf16[1,384,5,128]{3,2,0,1:T(8,128)(2,1)S(1)}, u32[]{:S(2)}, u32[]{:S(2)}) async-start(bf16[1,384,5,128]{3,2,0,1:T(8,128)(2,1)} %copy.65), calls=%async_computation.1 | async-start | bytes 1572864 | tf_op jit(solution)/shard_map/all_to_all | solution.py:30
  35.3 23.9 %all-to-all-start.2 = ((bf16[1,384,5,128]{3,2,0,1:T(8,128)(2,1)}), bf16[1,384,5,128]{3,2,0,1:T(8,128)(2,1)S(1)}, u32[]{:S(2)}, u32[]{:S(2)}) async-start(bf16[1,384,5,128]{3,2,0,1:T(8,128)(2,1)} %copy.67), calls=%async_computation.2 | async-start | bytes 1572864 | tf_op jit(solution)/shard_map/all_to_all | solution.py:31
  41.1 23.2 %copy-start.8 = (s32[4,4]{1,0:T(4,128)S(1)}, s32[4,4]{1,0:T(4,128)}, u32[]{:S(2)}) copy-start(s32[4,4]{1,0:T(4,128)} %param.13) | copy-start | bytes 196
  59.2 0.9 copy-start.3
  60.1 24.1 %all-to-all-start = ((bf16[1,384,5,128]{3,2,0,1:T(8,128)(2,1)}), bf16[1,384,5,128]{3,2,0,1:T(8,128)(2,1)}, u32[]{:S(2)}, u32[]{:S(2)}) async-start(bf16[1,384,5,128]{3,2,0,1:T(8,128)(2,1)} %copy.63), calls=%async_computation | async-start | bytes 1572864 | tf_op jit(solution)/shard_map/all_to_all | solution.py:32
  66.7 1.4 %copy-start.4 = (bf16[1,384,5,128]{3,2,0,1:T(8,128)(2,1)S(1)}, bf16[1,384,5,128]{3,2,0,1:T(8,128)(2,1)}, u32[]{:S(2)}) copy-start(bf16[1,384,5,128]{3,2,0,1:T(8,128)(2,1)} %copy-done.3) | copy-start | bytes 1474564
  86.7 3.6 %copy-start.6 = (bf16[5,384,128]{2,1,0:T(8,128)(2,1)S(1)}, bf16[5,384,128]{2,1,0:T(8,128)(2,1)}, u32[]{:S(2)}) copy-start(bf16[5,384,128]{2,1,0:T(8,128)(2,1)} %custom-call.16) | copy-start | bytes 1474564
  86.7 18.8 %all-to-all-start.3 = ((bf16[8,48,5,128]{3,1,2,0:T(8,128)(2,1)}), bf16[8,48,5,128]{3,1,2,0:T(8,128)(2,1)S(1)}, u32[]{:S(2)}, u32[]{:S(2)}) async-start(bf16[8,48,5,128]{3,1,2,0:T(8,128)(2,1)} %copy.75), calls=%async_computation.3 | async-start | bytes 983040 | tf_op jit(solution)/shard_map/all_to_all | solution.py:56
where the time goes:
time: 108 us; the launch traced here: 107 us
  waiting for transfers between devices  51.4 us (48%)
  starting transfers between devices  18.8 us (17%)
  matrix products  14.9 us (14%)
  local copies, waits for them, and re-layouts  14.2 us (13%)
  other arithmetic  7.07 us (7%)
    all_to_all x1, waiting for transfers between devices, run_temporal(): lax.all_to_all(triple[0], 'tm', split_axis=1, concat_axis=0, tiled=True)  18.9 us
    all_to_all x1, waiting for transfers between devices, run_temporal(): lax.all_to_all(triple[1], 'tm', split_axis=1, concat_axis=0, tiled=True)  18.1 us
    all_to_all x1, waiting for transfers between devices, run_temporal(): lax.all_to_all(triple[2], 'tm', split_axis=1, concat_axis=0, tiled=True)  14.4 us
    all_to_all x1, starting transfers between devices, run_temporal(): lax.all_to_all(triple[0], 'tm', split_axis=1, concat_axis=0, tiled=True)  7.41 us
    dot_general x5, matrix products, frame_attend(): jnp.einsum('id,jd->ij', query_block, key_block, preferred_element_type=jn...  6.09 us
    dot_general x5, matrix products, frame_attend(): jnp.dot(exponent.astype(jnp.bfloat16), value_block, preferred_element_typ...  5.99 us
    select_n x3, local copies, waits for them, and re-layouts, per_device(): jnp.take(a, sorted_heads[least_count:], axis=2)  4.76 us
    all_to_all x1, starting transfers between devices, run_temporal(): lax.all_to_all(triple[2], 'tm', split_axis=1, concat_axis=0, tiled=True)  4.21 us
  transfers between devices with their start and end apart: 4, of which 3 were waited for; matrix products, arithmetic and copies ran while one was open for 22% of the time, Pallas kernels for 0%

commit v1 on v0

v1 whole, which is shorter than its diff:
```python
import functools
import math

import jax
import jax.numpy as jnp
from jax import lax
from jax.experimental import pallas as pl
from jax.experimental.pallas import tpu as pltpu
from jax.sharding import PartitionSpec as P

ROWS = 16
NEGATIVE = -1e30


def rank_heads(class_ref, order_ref, group_heads):
    base = lax.axis_index("head") * group_heads
    temporal = jnp.int32(0)
    for head in range(group_heads):
        is_temporal = class_ref[base + head]
        slot = jnp.where(is_temporal == 1, temporal, group_heads + head - temporal)
        order_ref[slot] = jnp.int32(head)
        temporal = temporal + is_temporal
    return temporal


def softmax_rows(scores):
    peak = jnp.max(scores, axis=-1, keepdims=True)
    exponent = jnp.exp(scores - peak)
    return exponent, jnp.sum(exponent, axis=-1, keepdims=True)


def attend(triples, bias=None):
    factor = triples[0][0].shape[-1] ** -0.5 * math.log2(math.e)
    scores = [
        lax.dot_general(query, key, (((1,), (1,)), ((), ())), preferred_element_type=jnp.float32)
        for query, key, _ in triples
    ]
    if bias is not None:
        scores = [score + bias for score in scores]
    peaks = [jnp.max(score, axis=-1, keepdims=True) for score in scores]
    exponents = [jnp.exp2((score - peak) * factor) for score, peak in zip(scores, peaks)]
    totals = [jnp.sum(exponent, axis=-1, keepdims=True) for exponent in exponents]
    blended = [
        jnp.dot(exponent.astype(jnp.bfloat16), value, preferred_element_type=jnp.float32)
        for exponent, (_, _, value) in zip(exponents, triples)
    ]
    return [(blend / total).astype(jnp.bfloat16) for blend, total in zip(blended, totals)]


def copy_all(copies, sems):
    started = [pltpu.make_async_copy(source, target, sems.at[i]) for i, (source, target) in enumerate(copies)]
    for copy in started:
        copy.start()

    def wait():
        for copy in started:
            copy.wait()

    return wait


def hand_kernel(sizes, class_ref, q_ref, k_ref, v_ref, out_ref, token_ref, order_ref, sems):
    group_heads, most, least = sizes
    handed = (most - least) // 2
    temporal = rank_heads(class_ref, order_ref, group_heads)
    first = jnp.where(temporal == most, most - handed, group_heads)
    copies = []
    for slot in range(handed):
        head = order_ref[first + slot]
        copies += [(ref.at[head], out_ref.at[slot, part]) for part, ref in enumerate((q_ref, k_ref, v_ref))]
    copy_all(copies, sems)()
    token_ref[...] = jnp.zeros_like(token_ref)


def load_kernel(q_ref, k_ref, v_ref, token_ref, q_out, k_out, v_out, sems):
    copies = [
        (ref.at[head], out.at[head])
        for ref, out in ((q_ref, q_out), (k_ref, k_out), (v_ref, v_out))
        for head in range(ref.shape[0])
    ]
    copy_all(copies, sems)()


def spatial_kernel(sizes, class_ref, mask_ref, q_ref, k_ref, v_ref, out_ref, bias_ref, order_ref):
    group_heads, ranks, blocks = sizes
    temporal = rank_heads(class_ref, order_ref, group_heads)

    def body(slot, carry):
        head = order_ref[group_heads + slot]
        (out_ref[head],) = attend([(q_ref[head], k_ref[head], v_ref[head])])
        return carry

    lax.fori_loop(0, group_heads - temporal, body, 0)
    fill_bias(bias_ref, mask_ref, frames_held(ranks), blocks)


def distances(ranks):
    far, near = list(range(ranks // 2, ranks)), list(range(1, ranks // 2))[::-1]
    return [0, *far[:1], *near[-2:-1], *far[1:2], *near[:-2], *near[-1:], *far[2:]]


def pack_kernel(sizes, class_ref, q_ref, k_ref, v_ref, given_ref, *rest):
    group_heads, most, least, ranks, share = sizes
    handed = (most - least) // 2
    out_refs, order_ref = rest[:ranks], rest[ranks]
    temporal = rank_heads(class_ref, order_ref, group_heads)
    me = lax.axis_index("tm")
    rows = [pl.ds(pl.multiple_of((me ^ step) * share, ROWS), share) for step in range(ranks)]

    def put(slot, sources):
        for part, source in enumerate(sources):
            for step in range(ranks):
                out_refs[step][slot, part] = source[rows[step], :]

    def own(slots):
        for slot in slots:
            head = order_ref[slot]
            put(slot, [ref.at[head] for ref in (q_ref, k_ref, v_ref)])

    own(range(least))

    @pl.when(temporal == most)
    def _():
        own(range(least, least + handed))

    @pl.when(temporal != most)
    def _():
        for slot in range(handed):
            put(least + slot, [given_ref.at[slot, part] for part in range(3)])


def frames_held(ranks):
    me = lax.axis_index("tm")
    return [me ^ step for step in distances(ranks)]


def fill_bias(bias_ref, mask_ref, frames, blocks):
    row = lax.broadcasted_iota(jnp.int32, (ROWS, bias_ref.shape[1]), 0)
    column = lax.broadcasted_iota(jnp.int32, (ROWS, bias_ref.shape[1]), 1)
    span = len(frames) // blocks
    for step, own in enumerate(frames):
        strip = jnp.zeros(row.shape, jnp.int32)
        for column_step, other in enumerate(frames):
            strip = jnp.where(column // ROWS == column_step, mask_ref[own // span, other // span], strip)
        kept = jnp.logical_and(column % ROWS == row, strip == 1)
        bias_ref[step * ROWS : (step + 1) * ROWS, :] = jnp.where(kept, jnp.float32(0.0), jnp.float32(NEGATIVE))


def temporal_kernel(sizes, bias_ref, *rest):
    slots, ranks, share = sizes
    in_refs, out_ref = rest[:ranks], rest[ranks]
    frames = frames_held(ranks)
    for slot in range(slots):
        groups = [pl.ds(start, ROWS) for start in range(0, share, ROWS)]
        triples = [
            [jnp.concatenate([ref[slot, part, rows, :] for ref in in_refs], axis=0) for part in range(3)]
            for rows in groups
        ]
        for rows, blended in zip(groups, attend(triples, bias_ref[...])):
            for step, frame in enumerate(frames):
                out_ref[frame, slot, rows, :] = blended[step * ROWS : (step + 1) * ROWS]


def head_copies(ref, out_ref, order_ref, slots, ref_slot):
    return [(ref.at[:, ref_slot(slot)], out_ref.at[order_ref[slot]]) for slot in slots]


def own_kernel(sizes, class_ref, spatial_ref, back_ref, out_ref, order_ref, sems):
    group_heads, most, least = sizes
    temporal = rank_heads(class_ref, order_ref, group_heads)

    def run(count, slots):
        copies = head_copies(back_ref, out_ref, order_ref, slots, lambda slot: slot)
        for slot in range(group_heads - count):
            head = order_ref[group_heads + slot]
            copies.append((spatial_ref.at[head], out_ref.at[head]))
        copy_all(copies, sems)()

    @pl.when(temporal == most)
    def _():
        run(most, range(least + (most - least) // 2))

    @pl.when(temporal != most)
    def _():
        run(least, range(least))


def merge_kernel(sizes, class_ref, back_ref, whole_ref, out_ref, order_ref, sems):
    group_heads, most, least = sizes
    handed = (most - least) // 2
    temporal = rank_heads(class_ref, order_ref, group_heads)

    @pl.when(temporal == most)
    def _():
        slots = range(least + handed, most)
        copy_all(head_copies(back_ref, out_ref, order_ref, slots, lambda slot: slot - handed), sems)()


def per_device(head_total, queries, key_vectors, value_vectors, head_class, frame_mask):
    ranks = lax.axis_size("tm")
    group_heads = queries.shape[2]
    patches, width = queries.shape[1], queries.shape[3]
    share = patches // ranks
    least = group_heads // 2 - group_heads // 3
    most = group_heads // 2 + group_heads // 3
    handed = (most - least) // 2
    slots = least + handed
    blocks = frame_mask.shape[0]
    smem = pl.BlockSpec(memory_space=pltpu.SMEM)
    vmem = pl.BlockSpec(memory_space=pltpu.VMEM)
    hbm = pl.BlockSpec(memory_space=pltpu.HBM)
    params = pltpu.CompilerParams(vmem_limit_bytes=16 * 2**20)

    order = pltpu.SMEM((2 * group_heads,), jnp.int32)
    q, k, v = (jnp.moveaxis(a[0], 1, 0) for a in (queries, key_vectors, value_vectors))
    pairs = [(h, h ^ 1) for h in range(head_total)]
    whole = jax.ShapeDtypeStruct(q.shape, q.dtype)
    steps = distances(ranks)
    by_rank = jax.ShapeDtypeStruct((group_heads, ranks, share, width), q.dtype)
    packed_shape = [jax.ShapeDtypeStruct((slots, 3, share, width), q.dtype)] * ranks
    cost = pl.CostEstimate(
        flops=4 * most * patches * patches * width,
        bytes_accessed=4 * q.size * 2,
        transcendentals=most * patches * patches,
    )

    def swap(array):
        return lax.ppermute(array, "head", pairs)

    def exchange(array):
        return lax.all_to_all(array, "tm", split_axis=0, concat_axis=0, tiled=True)

    def send(array, step):
        return lax.ppermute(array, "tm", [(rank, rank ^ step) for rank in range(ranks)])

    handed_heads, token = pl.pallas_call(
        functools.partial(hand_kernel, (group_heads, most, least)),
        out_shape=[
            jax.ShapeDtypeStruct((handed, 3, patches, width), q.dtype),
            jax.ShapeDtypeStruct((8, width), jnp.float32),
        ],
        in_specs=[smem] + [hbm] * 3,
        out_specs=[vmem] * 2,
        scratch_shapes=[order, pltpu.SemaphoreType.DMA((handed * 3,))],
        compiler_params=pltpu.CompilerParams(vmem_limit_bytes=53 * 2**20),
        name="hand",
    )(head_class, q, k, v)
    given = swap(handed_heads)
    q, k, v = pl.pallas_call(
        load_kernel,
        out_shape=[whole] * 3,
        in_specs=[hbm] * 3 + [vmem],
        out_specs=[vmem] * 3,
        scratch_shapes=[pltpu.SemaphoreType.DMA((3 * group_heads,))],
        compiler_params=pltpu.CompilerParams(vmem_limit_bytes=52 * 2**20),
        name="load",
    )(q, k, v, token)
    packed = pl.pallas_call(
        functools.partial(pack_kernel, (group_heads, most, least, ranks, share)),
        out_shape=packed_shape,
        in_specs=[smem] + [vmem] * 4,
        out_specs=[vmem] * ranks,
        scratch_shapes=[order],
        compiler_params=params,
        name="pack",
    )(head_class, q, k, v, given)
    arrived = [packed[0]] + [send(packed[step], step) for step in steps[1:]]
    spatial, bias = pl.pallas_call(
        functools.partial(spatial_kernel, (group_heads, ranks, blocks)),
        out_shape=[whole, jax.ShapeDtypeStruct((ranks * ROWS, ranks * ROWS), jnp.float32)],
        in_specs=[smem] * 2 + [vmem] * 3,
        out_specs=[vmem] * 2,
        scratch_shapes=[order],
        compiler_params=params,
        cost_estimate=cost,
        name="spatial",
    )(head_class, frame_mask, q, k, v)
    back = exchange(
        pl.pallas_call(
            functools.partial(temporal_kernel, (slots, ranks, share)),
            out_shape=jax.ShapeDtypeStruct((ranks, slots, share, width), q.dtype),
            in_specs=[vmem] * (1 + ranks),
            out_specs=vmem,
            compiler_params=params,
            name="temporal",
        )(bias, *arrived)
    )
    returned = swap(back)
    mostly = pl.pallas_call(
        functools.partial(own_kernel, (group_heads, most, least)),
        out_shape=by_rank,
        in_specs=[smem] + [vmem] * 2,
        out_specs=hbm,
        scratch_shapes=[order, pltpu.SemaphoreType.DMA((slots + group_heads,))],
        compiler_params=params,
        name="own",
    )(head_class, spatial.reshape(by_rank.shape), back)
    merged = pl.pallas_call(
        functools.partial(merge_kernel, (group_heads, most, least)),
        out_shape=by_rank,
        in_specs=[smem, vmem, hbm],
        out_specs=hbm,
        scratch_shapes=[order, pltpu.SemaphoreType.DMA((handed,))],
        input_output_aliases={2: 0},
        compiler_params=params,
        name="merge",
    )(head_class, returned, mostly)
    return jnp.moveaxis(merged.reshape(q.shape), 0, 1)[None]


def frame_attend(triple):
    query_block, key_block, value_block = triple
    scores = lax.dot_general(
        query_block, key_block, (((1,), (1,)), ((), ())), preferred_element_type=jnp.float32
    ) * (query_block.shape[-1] ** -0.5)
    exponent, totals = softmax_rows(scores)
    blended = jnp.dot(
        exponent.astype(jnp.bfloat16), value_block, preferred_element_type=jnp.float32
    )
    return (blended / totals).astype(jnp.bfloat16)


def run_spatial(triple):
    moved = tuple((jnp.moveaxis(a[0], 1, 0) for a in triple))
    blended = lax.map(frame_attend, moved)
    return jnp.moveaxis(blended, 0, 1)[None]


def run_temporal(triple, frame_mask):
    query_block, key_block, value_block = (
        lax.all_to_all(a, "tm", split_axis=1, concat_axis=0, tiled=True) for a in triple
    )
    score_scale = query_block.shape[-1] ** (-0.5)
    frame_total = query_block.shape[0]
    block_total = frame_mask.shape[0]
    frame_block = jnp.arange(frame_total, dtype=jnp.int32) // (frame_total // block_total)
    onehot = (frame_block[:, None] == jnp.arange(block_total, dtype=jnp.int32)[None, :]).astype(
        jnp.float32
    )
    allowed = jnp.dot(jnp.dot(onehot, frame_mask.astype(jnp.float32)), onehot.T) > 0.5
    scores = (
        jnp.einsum("fpmd,gpmd->pmfg", query_block, key_block, preferred_element_type=jnp.float32)
        * score_scale
    )
    scores = jnp.where(allowed, scores, jnp.float32(NEGATIVE))
    peak = jnp.max(scores, axis=-1, keepdims=True)
    exponent = jnp.where(allowed, jnp.exp(scores - peak), jnp.float32(0.0))
    totals = jnp.sum(exponent, axis=-1)
    blended = jnp.einsum(
        "pmfg,gpmd->fpmd",
        exponent.astype(jnp.bfloat16),
        value_block,
        preferred_element_type=jnp.float32,
    )
    result = (blended / jnp.transpose(totals, (2, 0, 1))[..., None]).astype(jnp.bfloat16)
    return lax.all_to_all(result, "tm", split_axis=0, concat_axis=1, tiled=True)


def per_device_many(queries, key_vectors, value_vectors, head_class, frame_mask):
    group_heads = queries.shape[2]
    moved_heads = group_heads // 3
    half_heads = group_heads // 2
    least_count = half_heads - moved_heads
    most_count = half_heads + moved_heads
    head_group = lax.axis_index("head")
    local_class = lax.dynamic_slice_in_dim(head_class, head_group * group_heads, group_heads)
    sorted_heads = jnp.argsort(local_class, stable=True)
    head_rank = jnp.argsort(sorted_heads)
    temporal_count = jnp.sum(local_class)
    position = jnp.arange(group_heads, dtype=jnp.int32)
    triple = (queries, key_vectors, value_vectors)
    spatial_in = tuple((jnp.take(a, sorted_heads[:most_count], axis=2) for a in triple))
    temporal_in = tuple((jnp.take(a, sorted_heads[least_count:], axis=2) for a in triple))
    spatial_out = run_spatial(spatial_in)
    temporal_out = run_temporal(temporal_in, frame_mask)
    result_pool = jnp.concatenate([spatial_out, temporal_out], axis=2)
    slot_index = jnp.where(
        position < group_heads - temporal_count, position, most_count + position - least_count
    )
    return jnp.take(result_pool, jnp.take(slot_index, head_rank), axis=2)


def solution(mesh):
    ranks, head_total = mesh.shape["tm"], mesh.shape["head"]
    spec = P("tm", None, "head", None)

    def whole(queries, key_vectors, value_vectors, head_class, frame_mask):
        few = (
            ranks & (ranks - 1) == 0
            and 2 <= ranks <= 8
            and queries.shape[0] == ranks
            and queries.shape[1] % (ranks * ROWS) == 0
            and head_total % 2 == 0
            and ranks % frame_mask.shape[0] == 0
        )
        body = functools.partial(per_device, head_total) if few else per_device_many
        return jax.shard_map(
            body, mesh=mesh, in_specs=(spec, spec, spec, P(), P()), out_specs=spec, check_vma=False
        )(queries, key_vectors, value_vectors, head_class, frame_mask)

    return whole
```

time: 108 us -> 48.4 us (0.45)
  waiting for transfers between devices: 51.4 us -> 4.17 us
  blocking collectives: 0 us -> 17.3 us
  matrix products: 14.9 us -> 0 us
  local copies, waits for them, and re-layouts: 14.2 us -> 0.66 us
  Pallas kernels: 0 us -> 10.2 us
  other arithmetic: 7.07 us -> 0 us
  starting transfers between devices: 18.8 us -> 15.1 us
    all_to_all x4 -> x0, waiting for transfers between devices: 51.4 us -> none  [the longest x1 18.9 us: run_temporal(): lax.all_to_all(triple[0], 'tm', split_axis=1, concat_axis=0, tiled=True)]
    all_to_all x4 -> x0, starting transfers between devices: 18.8 us -> none  [the longest x1 7.41 us: run_temporal(): lax.all_to_all(triple[0], 'tm', split_axis=1, concat_axis=0, tiled=True)]
    all_to_all x0 -> x1, blocking collectives: none -> 17.3 us  [exchange(): return lax.all_to_all(array, 'tm', split_axis=0, concat_axis=0, tiled=True)]
    ppermute x0 -> x9, starting transfers between devices: none -> 15.1 us  [the longest x7 14.6 us: send(): lax.ppermute(array, 'tm', [(rank, rank ^ step) for rank in range(ranks)])]
    dot_general x13 -> x0, matrix products: 14.9 us -> none  [the longest x5 6.09 us: frame_attend(): jnp.einsum('id,jd->ij', query_block, key_block, preferred_element_type=jn...]
    pallas_call x0 -> x7, Pallas kernels: none -> 10.2 us  [the longest x1 3.17 us: per_device(): pl.pallas_call(functools.partial(spatial_kernel, (group_heads, ranks, blo...]
    gather x8 -> x0, local copies, waits for them, and re-layouts: 5.16 us -> none  [the longest x3 1.94 us: per_device(): jnp.take(a, sorted_heads[:most_count], axis=2)]
    select_n x3 -> x0, local copies, waits for them, and re-layouts: 4.76 us -> none  [per_device(): jnp.take(a, sorted_heads[least_count:], axis=2)]
  transfers between devices with their start and end apart: 4 -> 9, of which waited for: 3 -> 3; matrix products, arithmetic and copies ran while one was open for 22% -> 0% of each run, Pallas kernels for 0% -> 13%
where the time goes in v1:
time: 48.4 us; the launch traced here: 47.6 us
  blocking collectives  17.3 us (36%)
  starting transfers between devices  15.1 us (31%)
  Pallas kernels  10.2 us (21%)
  waiting for transfers between devices  4.17 us (9%)
  local copies, waits for them, and re-layouts  0.66 us (1%)
    all_to_all x1, blocking collectives, exchange(): return lax.all_to_all(array, 'tm', split_axis=0, concat_axis=0, tiled=True)  17.3 us
    ppermute x7, starting transfers between devices, send(): lax.ppermute(array, 'tm', [(rank, rank ^ step) for rank in range(ranks)])  14.6 us
    ppermute x7, waiting for transfers between devices, send(): lax.ppermute(array, 'tm', [(rank, rank ^ step) for rank in range(ranks)])  4.06 us
    pallas_call x1, Pallas kernels, per_device(): pl.pallas_call(functools.partial(spatial_kernel, (group_heads, ranks, blo...  3.17 us
    pallas_call x1, Pallas kernels, per_device(): pl.pallas_call(functools.partial(hand_kernel, (group_heads, most, least))...  1.75 us
    pallas_call x1, Pallas kernels, per_device(): pl.pallas_call(load_kernel, out_shape=[whole] * 3, in_specs=[hbm] * 3 + [...  1.66 us
    pallas_call x1, Pallas kernels, per_device(): pl.pallas_call(functools.partial(own_kernel, (group_heads, most, least)),...  1.46 us
  transfers between devices with their start and end apart: 9, of which 3 were waited for; matrix products, arithmetic and copies ran while one was open for 0% of the time, Pallas kernels for 13%

profile of v1, /device:TPU:0, one launch (start us, length us, event | category | flops | bytes accessed | tf_op | source)
XLA Modules:
  0.0 47.6 jit_solution(132419578579704846)
XLA Ops:
  0.0 0.0 copy-start
  0.0 0.7 %copy-done = s32[24]{0:T(128)S(1)} copy-done((s32[24]{0:T(128)S(1)}, s32[24]{0:T(128)}, u32[]{:S(2)}) %copy-start) | copy-done | bytes 120
  0.7 1.7 %hand.1 = (bf16[2,3,384,128]{3,2,1,0:T(8,128)(2,1)S(1)}, f32[8,128]{1,0:T(8,128)S(1)}) custom-call(s32[24]{0:T(128)S(1)} %copy-done, bf16[6,384,128]{2,1,0:T(8,128)(2,1)} %bitcast.16, bf16[6,384,128]{2,1,0:T(8,128)(2,1)} %bitcast.18, bf16[6,384,128]{2,1,0:T(8,128)(2,1)} %bitcast.20), custom_call_target="tpu_custom_call" | custom-call | tf_op jit(solution)/shard_map/hand/pallas_call | solution.py:236
  2.4 0.5 %collective-permute-start = (bf16[2,3,384,128]{3,2,1,0:T(8,128)(2,1)S(1)}, bf16[2,3,384,128]{3,2,1,0:T(8,128)(2,1)S(1)}, u32[]{:S(2)}, u32[]{:S(2)}) collective-permute-start(bf16[2,3,384,128]{3,2,1,0:T(8,128)(2,1)S(1)} %get-tuple-element.25), channel_id=1, source_target_pairs={{0,1},{1,0},{2,3},{3,2},{4,5},{5,4},{6,7},{7,6},{8,9},{9,8},{10,11... | collective-permute-start | bytes 1769480 | tf_op jit(solution)/shard_map/ppermute | solution.py:228
  2.9 1.7 %load.1 = (bf16[6,384,128]{2,1,0:T(8,128)(2,1)S(1)}, bf16[6,384,128]{2,1,0:T(8,128)(2,1)S(1)}, bf16[6,384,128]{2,1,0:T(8,128)(2,1)S(1)}) custom-call(bf16[6,384,128]{2,1,0:T(8,128)(2,1)} %bitcast.17, bf16[6,384,128]{2,1,0:T(8,128)(2,1)} %bitcast.19, bf16[6,384,128]{2,1,0:T(8,128)(2,1)} %bitcast.21, f32[8,128]{1,0:T(8,128)S(1)} %get-tuple-element.20.token_ref), custom_call_target="tpu_custom_call" | custom-call | tf_op jit(solution)/shard_map/load/pallas_call | solution.py:249
  4.6 0.0 collective-permute-done.given_ref
  4.6 0.6 %pack.1 = (bf16[3,3,48,128]{3,2,1,0:T(8,128)(2,1)S(1)}, bf16[3,3,48,128]{3,2,1,0:T(8,128)(2,1)S(1)}, bf16[3,3,48,128]{3,2,1,0:T(8,128)(2,1)S(1)}, bf16[3,3,48,12...) custom-call(s32[24]{0:T(128)S(1)} %copy-done, ...), custom_call_target="tpu_custom_call" | custom-call | tf_op jit(solution)/shard_map/pack/pallas_call | solution.py:258
  5.3 4.0 %collective-permute-start.1 = (bf16[3,3,48,128]{3,2,1,0:T(8,128)(2,1)S(1)}, bf16[3,3,48,128]{3,2,1,0:T(8,128)(2,1)S(1)}, u32[]{:S(2)}, u32[]{:S(2)}) collective-permute-start(bf16[3,3,48,128]{3,2,1,0:T(8,128)(2,1)S(1)} %get-tuple-element.27), channel_id=1, source_target_pairs={{0,16},{4,20},{8,24},{12,28},{16,0},{20,4},{24,8},{28,12},{1,17},{... | collective-permute-start | bytes 331784 | tf_op jit(solution)/shard_map/ppermute | solution.py:234
  9.2 1.6 %collective-permute-start.2 = (bf16[3,3,48,128]{3,2,1,0:T(8,128)(2,1)S(1)}, bf16[3,3,48,128]{3,2,1,0:T(8,128)(2,1)S(1)}, u32[]{:S(2)}, u32[]{:S(2)}) collective-permute-start(bf16[3,3,48,128]{3,2,1,0:T(8,128)(2,1)S(1)} %get-tuple-element.28), channel_id=1, source_target_pairs={{0,8},{4,12},{8,0},{12,4},{16,24},{20,28},{24,16},{28,20},{1,9},{5... | collective-permute-start | bytes 331784 | tf_op jit(solution)/shard_map/ppermute | solution.py:234
  10.8 1.3 %collective-permute-start.3 = (bf16[3,3,48,128]{3,2,1,0:T(8,128)(2,1)S(1)}, bf16[3,3,48,128]{3,2,1,0:T(8,128)(2,1)S(1)}, u32[]{:S(2)}, u32[]{:S(2)}) collective-permute-start(bf16[3,3,48,128]{3,2,1,0:T(8,128)(2,1)S(1)} %get-tuple-element.29), channel_id=1, source_target_pairs={{0,20},{4,16},{8,28},{12,24},{16,4},{20,0},{24,12},{28,8},{1,21},{... | collective-permute-start | bytes 331784 | tf_op jit(solution)/shard_map/ppermute | solution.py:234
  12.1 0.1 collective-permute-start.4
  12.2 0.0 copy-start.1
  12.2 1.8 %collective-permute-start.5 = (bf16[3,3,48,128]{3,2,1,0:T(8,128)(2,1)S(1)}, bf16[3,3,48,128]{3,2,1,0:T(8,128)(2,1)S(1)}, u32[]{:S(2)}, u32[]{:S(2)}) collective-permute-start(bf16[3,3,48,128]{3,2,1,0:T(8,128)(2,1)S(1)} %get-tuple-element.31), channel_id=1, source_target_pairs={{0,4},{4,0},{8,12},{12,8},{16,20},{20,16},{24,28},{28,24},{1,5},{5... | collective-permute-start | bytes 331784 | tf_op jit(solution)/shard_map/ppermute | solution.py:234
  14.0 1.2 %collective-permute-done.1.rest_1_ = bf16[3,3,48,128]{3,2,1,0:T(8,128)(2,1)S(1)} collective-permute-done((bf16[3,3,48,128]{3,2,1,0:T(8,128)(2,1)S(1)}, bf16[3,3,48,128]{3,2,1,0:T(8,128)(2,1)S(1)}, u32[]{:S(2)}, u32[]{:S(2)}) %collective-permute-start.1) | collective-permute-done | bytes 110624 | tf_op jit(solution)/shard_map/ppermute | solution.py:234
  15.2 4.2 %collective-permute-start.6 = (bf16[3,3,48,128]{3,2,1,0:T(8,128)(2,1)S(1)}, bf16[3,3,48,128]{3,2,1,0:T(8,128)(2,1)S(1)}, u32[]{:S(2)}, u32[]{:S(2)}) collective-permute-start(bf16[3,3,48,128]{3,2,1,0:T(8,128)(2,1)S(1)} %get-tuple-element.32), channel_id=1, source_target_pairs={{0,24},{4,28},{8,16},{12,20},{16,8},{20,12},{24,0},{28,4},{1,25},{... | collective-permute-start | bytes 331784 | tf_op jit(solution)/shard_map/ppermute | solution.py:234
  19.4 0.0 collective-permute-done.2.rest_2_
  19.4 1.6 %collective-permute-start.7 = (bf16[3,3,48,128]{3,2,1,0:T(8,128)(2,1)S(1)}, bf16[3,3,48,128]{3,2,1,0:T(8,128)(2,1)S(1)}, u32[]{:S(2)}, u32[]{:S(2)}) collective-permute-start(bf16[3,3,48,128]{3,2,1,0:T(8,128)(2,1)S(1)} %get-tuple-element.33), channel_id=1, source_target_pairs={{0,28},{4,24},{8,20},{12,16},{16,12},{20,8},{24,4},{28,0},{1,29},{... | collective-permute-start | bytes 331784 | tf_op jit(solution)/shard_map/ppermute | solution.py:234
  21.0 0.0 copy-done.1
  21.0 3.2 %spatial.1 = (bf16[6,384,128]{2,1,0:T(8,128)(2,1)S(1)}, f32[128,128]{1,0:T(8,128)S(1)}) custom-call(s32[24]{0:T(128)S(1)} %copy-done, s32[4,4]{1,0:T(4,128)S(1)} %copy-done.1, bf16[6,384,128]{2,1,0:T(8,128)(2,1)S(1)} %get-tuple-element.21.q_ref, bf16[6,384,128]{2,1,0:T(8,128)(2,1)S(1)} %get-tuple-element.22.k_ref, ...), custom_call_target="tpu_custom_call" | custom-call | flops 377487360 | bytes 2359296 | tf_op jit(solution)/shard_map/spatial/pallas_call | solution.py:268
  24.2 0.0 collective-permute-done.3.rest_3_
  24.2 0.0 collective-permute-done.4.rest_4_
  24.2 0.0 collective-permute-done.5.rest_5_
  24.2 0.0 collective-permute-done.6.rest_6_
  24.2 2.9 %collective-permute-done.7.rest_7_ = bf16[3,3,48,128]{3,2,1,0:T(8,128)(2,1)S(1)} collective-permute-done((bf16[3,3,48,128]{3,2,1,0:T(8,128)(2,1)S(1)}, bf16[3,3,48,128]{3,2,1,0:T(8,128)(2,1)S(1)}, u32[]{:S(2)}, u32[]{:S(2)}) %collective-permute-start.7) | collective-permute-done | bytes 110624 | tf_op jit(solution)/shard_map/ppermute | solution.py:234
  27.1 0.9 %temporal.1 = bf16[8,3,48,128]{3,2,1,0:T(8,128)(2,1)S(1)} custom-call(f32[128,128]{1,0:T(8,128)S(1)} %get-tuple-element.24.bias_ref, bf16[3,3,48,128]{3,2,1,0:T(8,128)(2,1)S(1)} %get-tuple-element.26.rest_0_, bf16[3,3,48,128]{3,2,1,0:T(8,128)(2,1)S(1)} %collective-permute-done.1.rest_1_, bf16[3,3,48,128]{3,2,1,0:T(8,128)(2,1)S(1)} %collective-permute-done.2.rest_2_, ...), custom_call_target="tpu_custom_call" | custom-call | tf_op jit(solution)/shard_map/temporal/pallas_call | solution.py:279
  28.0 17.3 %all_to_all.5.back_ref = bf16[8,3,48,128]{3,2,1,0:T(8,128)(2,1)S(1)} all-to-all(bf16[8,3,48,128]{3,2,1,0:T(8,128)(2,1)S(1)} %temporal.1), channel_id=1, replica_groups=mesh['tm'=8,'head'=4] {'tm'}, dimensions={0} | all-to-all | bytes 589824 | tf_op jit(solution)/shard_map/all_to_all | solution.py:231
  45.4 0.0 collective-permute-start.8
  45.4 1.5 %own.1.whole_ref = bf16[6,8,48,128]{3,2,1,0:T(8,128)(2,1)} custom-call(s32[24]{0:T(128)S(1)} %copy-done, bf16[6,8,48,128]{3,2,1,0:T(8,128)(2,1)S(1)} %bitcast.15, bf16[8,3,48,128]{3,2,1,0:T(8,128)(2,1)S(1)} %all_to_all.5.back_ref), custom_call_target="tpu_custom_call" | custom-call | tf_op jit(solution)/shard_map/own/pallas_call | solution.py:289
  46.9 0.1 collective-permute-done.8.back_ref
  47.0 0.6 %merge.1 = bf16[6,8,48,128]{3,2,1,0:T(8,128)(2,1)} custom-call(s32[24]{0:T(128)S(1)} %copy-done, bf16[8,3,48,128]{3,2,1,0:T(8,128)(2,1)S(1)} %collective-permute-done.8.back_ref, bf16[6,8,48,128]{3,2,1,0:T(8,128)(2,1)} %own.1.whole_ref), custom_call_target="tpu_custom_call", output_to_operand_aliasing={{}: (2, {})} | custom-call | tf_op jit(solution)/shard_map/merge/pallas_call | solution.py:298
Async XLA Ops:
  0.0 0.7 %copy-start = (s32[24]{0:T(128)S(1)}, s32[24]{0:T(128)}, u32[]{:S(2)}) copy-start(s32[24]{0:T(128)} %class_ref.9) | copy-start | bytes 292
  2.4 2.2 %collective-permute-start = (bf16[2,3,384,128]{3,2,1,0:T(8,128)(2,1)S(1)}, bf16[2,3,384,128]{3,2,1,0:T(8,128)(2,1)S(1)}, u32[]{:S(2)}, u32[]{:S(2)}) collective-permute-start(bf16[2,3,384,128]{3,2,1,0:T(8,128)(2,1)S(1)} %get-tuple-element.25), channel_id=1, source_target_pairs={{0,1},{1,0},{2,3},{3,2},{4,5},{5,4},{6,7},{7,6},{8,9},{9,8},{10,11... | collective-permute-start | bytes 1769480 | tf_op jit(solution)/shard_map/ppermute | solution.py:228
  5.3 9.9 %collective-permute-start.1 = (bf16[3,3,48,128]{3,2,1,0:T(8,128)(2,1)S(1)}, bf16[3,3,48,128]{3,2,1,0:T(8,128)(2,1)S(1)}, u32[]{:S(2)}, u32[]{:S(2)}) collective-permute-start(bf16[3,3,48,128]{3,2,1,0:T(8,128)(2,1)S(1)} %get-tuple-element.27), channel_id=1, source_target_pairs={{0,16},{4,20},{8,24},{12,28},{16,0},{20,4},{24,8},{28,12},{1,17},{... | collective-permute-start | bytes 331784 | tf_op jit(solution)/shard_map/ppermute | solution.py:234
  9.2 10.2 %collective-permute-start.2 = (bf16[3,3,48,128]{3,2,1,0:T(8,128)(2,1)S(1)}, bf16[3,3,48,128]{3,2,1,0:T(8,128)(2,1)S(1)}, u32[]{:S(2)}, u32[]{:S(2)}) collective-permute-start(bf16[3,3,48,128]{3,2,1,0:T(8,128)(2,1)S(1)} %get-tuple-element.28), channel_id=1, source_target_pairs={{0,8},{4,12},{8,0},{12,4},{16,24},{20,28},{24,16},{28,20},{1,9},{5... | collective-permute-start | bytes 331784 | tf_op jit(solution)/shard_map/ppermute | solution.py:234
  10.8 13.4 %collective-permute-start.3 = (bf16[3,3,48,128]{3,2,1,0:T(8,128)(2,1)S(1)}, bf16[3,3,48,128]{3,2,1,0:T(8,128)(2,1)S(1)}, u32[]{:S(2)}, u32[]{:S(2)}) collective-permute-start(bf16[3,3,48,128]{3,2,1,0:T(8,128)(2,1)S(1)} %get-tuple-element.29), channel_id=1, source_target_pairs={{0,20},{4,16},{8,28},{12,24},{16,4},{20,0},{24,12},{28,8},{1,21},{... | collective-permute-start | bytes 331784 | tf_op jit(solution)/shard_map/ppermute | solution.py:234
  12.1 12.1 %collective-permute-start.4 = (bf16[3,3,48,128]{3,2,1,0:T(8,128)(2,1)S(1)}, bf16[3,3,48,128]{3,2,1,0:T(8,128)(2,1)S(1)}, u32[]{:S(2)}, u32[]{:S(2)}) collective-permute-start(bf16[3,3,48,128]{3,2,1,0:T(8,128)(2,1)S(1)} %get-tuple-element.30), channel_id=1, source_target_pairs={{0,12},{4,8},{8,4},{12,0},{16,28},{20,24},{24,20},{28,16},{1,13},{... | collective-permute-start | bytes 331784 | tf_op jit(solution)/shard_map/ppermute | solution.py:234
  12.2 8.8 %copy-start.1 = (s32[4,4]{1,0:T(4,128)S(1)}, s32[4,4]{1,0:T(4,128)}, u32[]{:S(2)}) copy-start(s32[4,4]{1,0:T(4,128)} %mask_ref.1) | copy-start | bytes 196
  12.2 12.0 %collective-permute-start.5 = (bf16[3,3,48,128]{3,2,1,0:T(8,128)(2,1)S(1)}, bf16[3,3,48,128]{3,2,1,0:T(8,128)(2,1)S(1)}, u32[]{:S(2)}, u32[]{:S(2)}) collective-permute-start(bf16[3,3,48,128]{3,2,1,0:T(8,128)(2,1)S(1)} %get-tuple-element.31), channel_id=1, source_target_pairs={{0,4},{4,0},{8,12},{12,8},{16,20},{20,16},{24,28},{28,24},{1,5},{5... | collective-permute-start | bytes 331784 | tf_op jit(solution)/shard_map/ppermute | solution.py:234
  15.2 9.0 %collective-permute-start.6 = (bf16[3,3,48,128]{3,2,1,0:T(8,128)(2,1)S(1)}, bf16[3,3,48,128]{3,2,1,0:T(8,128)(2,1)S(1)}, u32[]{:S(2)}, u32[]{:S(2)}) collective-permute-start(bf16[3,3,48,128]{3,2,1,0:T(8,128)(2,1)S(1)} %get-tuple-element.32), channel_id=1, source_target_pairs={{0,24},{4,28},{8,16},{12,20},{16,8},{20,12},{24,0},{28,4},{1,25},{... | collective-permute-start | bytes 331784 | tf_op jit(solution)/shard_map/ppermute | solution.py:234
  19.4 7.7 %collective-permute-start.7 = (bf16[3,3,48,128]{3,2,1,0:T(8,128)(2,1)S(1)}, bf16[3,3,48,128]{3,2,1,0:T(8,128)(2,1)S(1)}, u32[]{:S(2)}, u32[]{:S(2)}) collective-permute-start(bf16[3,3,48,128]{3,2,1,0:T(8,128)(2,1)S(1)} %get-tuple-element.33), channel_id=1, source_target_pairs={{0,28},{4,24},{8,20},{12,16},{16,12},{20,8},{24,4},{28,0},{1,29},{... | collective-permute-start | bytes 331784 | tf_op jit(solution)/shard_map/ppermute | solution.py:234
  45.4 1.6 %collective-permute-start.8 = (bf16[8,3,48,128]{3,2,1,0:T(8,128)(2,1)S(1)}, bf16[8,3,48,128]{3,2,1,0:T(8,128)(2,1)S(1)}, u32[]{:S(2)}, u32[]{:S(2)}) collective-permute-start(bf16[8,3,48,128]{3,2,1,0:T(8,128)(2,1)S(1)} %all_to_all.5.back_ref), channel_id=1, source_target_pairs={{0,1},{1,0},{2,3},{3,2},{4,5},{5,4},{6,7},{7,6},{8,9},{9,8},{10,11... | collective-permute-start | bytes 884744 | tf_op jit(solution)/shard_map/ppermute | solution.py:228

commit v2 on v1

--- a/solution.py
+++ b/solution.py
@@ -12,8 +12,8 @@
 NEGATIVE = -1e30
 
 
-def rank_heads(class_ref, order_ref, group_heads):
-    base = lax.axis_index("head") * group_heads
+def rank_heads(class_ref, order_ref, group_heads, group=None):
+    base = (lax.axis_index("head") if group is None else group) * group_heads
     temporal = jnp.int32(0)
     for head in range(group_heads):
         is_temporal = class_ref[base + head]
@@ -59,20 +59,7 @@
     return wait
 
 
-def hand_kernel(sizes, class_ref, q_ref, k_ref, v_ref, out_ref, token_ref, order_ref, sems):
-    group_heads, most, least = sizes
-    handed = (most - least) // 2
-    temporal = rank_heads(class_ref, order_ref, group_heads)
-    first = jnp.where(temporal == most, most - handed, group_heads)
-    copies = []
-    for slot in range(handed):
-        head = order_ref[first + slot]
-        copies += [(ref.at[head], out_ref.at[slot, part]) for part, ref in enumerate((q_ref, k_ref, v_ref))]
-    copy_all(copies, sems)()
-    token_ref[...] = jnp.zeros_like(token_ref)
-
-
-def load_kernel(q_ref, k_ref, v_ref, token_ref, q_out, k_out, v_out, sems):
+def load_kernel(class_ref, q_ref, k_ref, v_ref, q_out, k_out, v_out, sems):
     copies = [
         (ref.at[head], out.at[head])
         for ref, out in ((q_ref, q_out), (k_ref, k_out), (v_ref, v_out))
@@ -95,38 +82,35 @@
 
 
 def distances(ranks):
-    far, near = list(range(ranks // 2, ranks)), list(range(1, ranks // 2))[::-1]
-    return [0, *far[:1], *near[-2:-1], *far[1:2], *near[:-2], *near[-1:], *far[2:]]
-
-
-def pack_kernel(sizes, class_ref, q_ref, k_ref, v_ref, given_ref, *rest):
+    far, near = [*range(ranks // 2, ranks, 2), *range(ranks // 2 + 1, ranks, 2)], list(range(1, ranks // 2))[::-1]
+    return [0, *far[:1], *near[-2:-1], *far[1:3], *near[:-2], *near[-1:], *far[3:]]
+
+
+def pack_kernel(sizes, class_ref, *refs):
     group_heads, most, least, ranks, share = sizes
     handed = (most - least) // 2
-    out_refs, order_ref = rest[:ranks], rest[ranks]
+    own_refs, other_refs, out_refs, order_ref = refs[:3], refs[3:6], refs[6:-1], refs[-1]
     temporal = rank_heads(class_ref, order_ref, group_heads)
     me = lax.axis_index("tm")
     rows = [pl.ds(pl.multiple_of((me ^ step) * share, ROWS), share) for step in range(ranks)]
 
-    def put(slot, sources):
-        for part, source in enumerate(sources):
-            for step in range(ranks):
-                out_refs[step][slot, part] = source[rows[step], :]
-
-    def own(slots):
+    def put(slots, refs, ref_slot):
         for slot in slots:
-            head = order_ref[slot]
-            put(slot, [ref.at[head] for ref in (q_ref, k_ref, v_ref)])
-
-    own(range(least))
+            head = order_ref[ref_slot(slot)]
+            for part, ref in enumerate(refs):
+                for step in range(ranks):
+                    out_refs[step][slot, part] = ref[head, rows[step], :]
+
+    put(range(least), own_refs, lambda slot: slot)
 
     @pl.when(temporal == most)
     def _():
-        own(range(least, least + handed))
+        put(range(least, least + handed), own_refs, lambda slot: slot)
 
     @pl.when(temporal != most)
     def _():
-        for slot in range(handed):
-            put(least + slot, [given_ref.at[slot, part] for part in range(3)])
+        rank_heads(class_ref, order_ref, group_heads, lax.axis_index("head") ^ 1)
+        put(range(least, least + handed), other_refs, lambda slot: slot - least + most - handed)
 
 
 def frames_held(ranks):
@@ -233,37 +217,25 @@
     def send(array, step):
         return lax.ppermute(array, "tm", [(rank, rank ^ step) for rank in range(ranks)])
 
-    handed_heads, token = pl.pallas_call(
-        functools.partial(hand_kernel, (group_heads, most, least)),
-        out_shape=[
-            jax.ShapeDtypeStruct((handed, 3, patches, width), q.dtype),
-            jax.ShapeDtypeStruct((8, width), jnp.float32),
-        ],
-        in_specs=[smem] + [hbm] * 3,
-        out_specs=[vmem] * 2,
-        scratch_shapes=[order, pltpu.SemaphoreType.DMA((handed * 3,))],
-        compiler_params=pltpu.CompilerParams(vmem_limit_bytes=53 * 2**20),
-        name="hand",
-    )(head_class, q, k, v)
-    given = swap(handed_heads)
+    others = [swap(array) for array in (q, k, v)]
     q, k, v = pl.pallas_call(
         load_kernel,
         out_shape=[whole] * 3,
-        in_specs=[hbm] * 3 + [vmem],
+        in_specs=[smem] + [hbm] * 3,
         out_specs=[vmem] * 3,
         scratch_shapes=[pltpu.SemaphoreType.DMA((3 * group_heads,))],
         compiler_params=pltpu.CompilerParams(vmem_limit_bytes=52 * 2**20),
         name="load",
-    )(q, k, v, token)
+    )(head_class, q, k, v)
     packed = pl.pallas_call(
         functools.partial(pack_kernel, (group_heads, most, least, ranks, share)),
         out_shape=packed_shape,
-        in_specs=[smem] + [vmem] * 4,
+        in_specs=[smem] + [vmem] * 6,
         out_specs=[vmem] * ranks,
         scratch_shapes=[order],
         compiler_params=params,
         name="pack",
-    )(head_class, q, k, v, given)
+    )(head_class, q, k, v, *others)
     arrived = [packed[0]] + [send(packed[step], step) for step in steps[1:]]
     spatial, bias = pl.pallas_call(
         functools.partial(spatial_kernel, (group_heads, ranks, blocks)),

time: 48.4 us -> 47.9 us (0.990); the launches traced: 47.6 us -> 47.7 us
  starting transfers between devices: 15.1 us -> 19.8 us
  Pallas kernels: 10.2 us -> 7.64 us
  blocking collectives: 17.3 us -> 15.8 us
  local copies, waits for them, and re-layouts: 0.66 us -> 0.15 us
    ppermute x7, starting transfers between devices: 14.6 us -> 18.9 us  [send(): lax.ppermute(array, 'tm', [(rank, rank ^ step) for rank in range(ranks)])]
    pallas_call x1, Pallas kernels: 3.17 us -> 1.2 us  [per_device(): pl.pallas_call(functools.partial(spatial_kernel, (group_heads, ranks, blo...]
    all_to_all x1, blocking collectives: 17.3 us -> 15.8 us  [exchange(): return lax.all_to_all(array, 'tm', split_axis=0, concat_axis=0, tiled=True)]
    pallas_call x2 -> x1, Pallas kernels: 3.41 us -> 2.21 us  [per_device(): pl.pallas_call(load_kernel, out_shape=[whole] * 3, in_specs=[smem] + [hbm...]
    ppermute x7, waiting for transfers between devices: 4.06 us -> 3.31 us  [send(): lax.ppermute(array, 'tm', [(rank, rank ^ step) for rank in range(ranks)])]
    ppermute x2 -> x4, waiting for transfers between devices: 0.11 us -> 0.83 us  [swap(): return lax.ppermute(array, 'head', pairs)]
    pallas_call x1, Pallas kernels: 0.59 us -> 1.26 us  [per_device(): pl.pallas_call(functools.partial(merge_kernel, (group_heads, most, least)...]
    unnamed x4, local copies, waits for them, and re-layouts: 0.66 us -> 0.15 us
  transfers between devices with their start and end apart: 9 -> 11, of which waited for: 3 -> 3; matrix products, arithmetic and copies ran while one was open for 0% -> 0% of each run, Pallas kernels for 13% -> 10%
where the time goes in v2:
time: 47.9 us; the launch traced here: 47.7 us
  starting transfers between devices  19.8 us (41%)
  blocking collectives  15.8 us (33%)
  Pallas kernels  7.64 us (16%)
  waiting for transfers between devices  4.14 us (9%)
    ppermute x7, starting transfers between devices, send(): lax.ppermute(array, 'tm', [(rank, rank ^ step) for rank in range(ranks)])  18.9 us
    all_to_all x1, blocking collectives, exchange(): return lax.all_to_all(array, 'tm', split_axis=0, concat_axis=0, tiled=True)  15.8 us
    ppermute x7, waiting for transfers between devices, send(): lax.ppermute(array, 'tm', [(rank, rank ^ step) for rank in range(ranks)])  3.31 us
    pallas_call x1, Pallas kernels, per_device(): pl.pallas_call(load_kernel, out_shape=[whole] * 3, in_specs=[smem] + [hbm...  2.21 us
    pallas_call x1, Pallas kernels, per_device(): pl.pallas_call(functools.partial(own_kernel, (group_heads, most, least)),...  1.38 us
    pallas_call x1, Pallas kernels, per_device(): pl.pallas_call(functools.partial(merge_kernel, (group_heads, most, least)...  1.26 us
    pallas_call x1, Pallas kernels, per_device(): pl.pallas_call(functools.partial(spatial_kernel, (group_heads, ranks, blo...  1.2 us
    ppermute x4, starting transfers between devices, swap(): return lax.ppermute(array, 'head', pairs)  0.97 us
  transfers between devices with their start and end apart: 11, of which 3 were waited for; matrix products, arithmetic and copies ran while one was open for 0% of the time, Pallas kernels for 10%

profile of v2, /device:TPU:0, one launch (start us, length us, event | category | flops | bytes accessed | tf_op | source)
XLA Modules:
  0.0 47.7 jit_solution(2053934142050256020)
XLA Ops:
  0.0 0.5 collective-permute-start
  0.5 0.0 copy-start
  0.5 0.1 collective-permute-start.1
  0.5 0.4 collective-permute-start.2
  1.0 0.1 copy-done
  1.1 2.2 %load.1 = (bf16[6,384,128]{2,1,0:T(8,128)(2,1)S(1)}, bf16[6,384,128]{2,1,0:T(8,128)(2,1)S(1)}, bf16[6,384,128]{2,1,0:T(8,128)(2,1)S(1)}) custom-call(s32[24]{0:T(128)S(1)} %copy-done, bf16[6,384,128]{2,1,0:T(8,128)(2,1)} %bitcast.17, bf16[6,384,128]{2,1,0:T(8,128)(2,1)} %bitcast.19, bf16[6,384,128]{2,1,0:T(8,128)(2,1)} %bitcast.21), custom_call_target="tpu_custom_call" | custom-call | tf_op jit(solution)/shard_map/load/pallas_call | solution.py:221
  3.3 0.0 collective-permute-done.refs_3_
  3.3 0.0 collective-permute-done.1.refs_4_
  3.3 0.6 %collective-permute-done.2.refs_5_ = bf16[6,384,128]{2,1,0:T(8,128)(2,1)S(1)} collective-permute-done((bf16[6,384,128]{2,1,0:T(8,128)(2,1)}, bf16[6,384,128]{2,1,0:T(8,128)(2,1)S(1)}, u32[]{:S(2)}, u32[]{:S(2)}) %collective-permute-start.2) | collective-permute-done | bytes 589856 | tf_op jit(solution)/shard_map/ppermute | solution.py:212
  4.0 0.6 %pack.1 = (bf16[3,3,48,128]{3,2,1,0:T(8,128)(2,1)S(1)}, bf16[3,3,48,128]{3,2,1,0:T(8,128)(2,1)S(1)}, bf16[3,3,48,128]{3,2,1,0:T(8,128)(2,1)S(1)}, bf16[3,3,48,12...) custom-call(s32[24]{0:T(128)S(1)} %copy-done, ...), custom_call_target="tpu_custom_call" | custom-call | tf_op jit(solution)/shard_map/pack/pallas_call | solution.py:230
  4.6 4.0 %collective-permute-start.3 = (bf16[3,3,48,128]{3,2,1,0:T(8,128)(2,1)S(1)}, bf16[3,3,48,128]{3,2,1,0:T(8,128)(2,1)S(1)}, u32[]{:S(2)}, u32[]{:S(2)}) collective-permute-start(bf16[3,3,48,128]{3,2,1,0:T(8,128)(2,1)S(1)} %get-tuple-element.23), channel_id=1, source_target_pairs={{0,16},{4,20},{8,24},{12,28},{16,0},{20,4},{24,8},{28,12},{1,17},{... | collective-permute-start | bytes 331784 | tf_op jit(solution)/shard_map/ppermute | solution.py:218
  8.7 1.6 %collective-permute-start.4 = (bf16[3,3,48,128]{3,2,1,0:T(8,128)(2,1)S(1)}, bf16[3,3,48,128]{3,2,1,0:T(8,128)(2,1)S(1)}, u32[]{:S(2)}, u32[]{:S(2)}) collective-permute-start(bf16[3,3,48,128]{3,2,1,0:T(8,128)(2,1)S(1)} %get-tuple-element.24), channel_id=1, source_target_pairs={{0,8},{4,12},{8,0},{12,4},{16,24},{20,28},{24,16},{28,20},{1,9},{5... | collective-permute-start | bytes 331784 | tf_op jit(solution)/shard_map/ppermute | solution.py:218
  10.2 0.0 collective-permute-start.5
  10.2 2.9 %collective-permute-start.6 = (bf16[3,3,48,128]{3,2,1,0:T(8,128)(2,1)S(1)}, bf16[3,3,48,128]{3,2,1,0:T(8,128)(2,1)S(1)}, u32[]{:S(2)}, u32[]{:S(2)}) collective-permute-start(bf16[3,3,48,128]{3,2,1,0:T(8,128)(2,1)S(1)} %get-tuple-element.26), channel_id=1, source_target_pairs={{0,20},{4,16},{8,28},{12,24},{16,4},{20,0},{24,12},{28,8},{1,21},{... | collective-permute-start | bytes 331784 | tf_op jit(solution)/shard_map/ppermute | solution.py:218
  13.1 2.4 %collective-permute-start.7 = (bf16[3,3,48,128]{3,2,1,0:T(8,128)(2,1)S(1)}, bf16[3,3,48,128]{3,2,1,0:T(8,128)(2,1)S(1)}, u32[]{:S(2)}, u32[]{:S(2)}) collective-permute-start(bf16[3,3,48,128]{3,2,1,0:T(8,128)(2,1)S(1)} %get-tuple-element.27), channel_id=1, source_target_pairs={{0,12},{4,8},{8,4},{12,0},{16,28},{20,24},{24,20},{28,16},{1,13},{... | collective-permute-start | bytes 331784 | tf_op jit(solution)/shard_map/ppermute | solution.py:218
  15.5 0.0 collective-permute-done.3.rest_1_
  15.5 1.7 %collective-permute-start.8 = (bf16[3,3,48,128]{3,2,1,0:T(8,128)(2,1)S(1)}, bf16[3,3,48,128]{3,2,1,0:T(8,128)(2,1)S(1)}, u32[]{:S(2)}, u32[]{:S(2)}) collective-permute-start(bf16[3,3,48,128]{3,2,1,0:T(8,128)(2,1)S(1)} %get-tuple-element.28), channel_id=1, source_target_pairs={{0,4},{4,0},{8,12},{12,8},{16,20},{20,16},{24,28},{28,24},{1,5},{5... | collective-permute-start | bytes 331784 | tf_op jit(solution)/shard_map/ppermute | solution.py:218
  17.3 0.0 collective-permute-done.4.rest_2_
  17.3 6.3 %collective-permute-start.9 = (bf16[3,3,48,128]{3,2,1,0:T(8,128)(2,1)S(1)}, bf16[3,3,48,128]{3,2,1,0:T(8,128)(2,1)S(1)}, u32[]{:S(2)}, u32[]{:S(2)}) collective-permute-start(bf16[3,3,48,128]{3,2,1,0:T(8,128)(2,1)S(1)} %get-tuple-element.29), channel_id=1, source_target_pairs={{0,28},{4,24},{8,20},{12,16},{16,12},{20,8},{24,4},{28,0},{1,29},{... | collective-permute-start | bytes 331784 | tf_op jit(solution)/shard_map/ppermute | solution.py:218
  23.5 0.0 copy-done.1
  23.5 1.2 %spatial.1 = (bf16[6,384,128]{2,1,0:T(8,128)(2,1)S(1)}, f32[128,128]{1,0:T(8,128)S(1)}) custom-call(s32[24]{0:T(128)S(1)} %copy-done, s32[4,4]{1,0:T(4,128)S(1)} %copy-done.1, bf16[6,384,128]{2,1,0:T(8,128)(2,1)S(1)} %get-tuple-element.18.q_ref.refs_0_, bf16[6,384,128]{2,1,0:T(8,128)(2,1)S(1)} %get-tuple-element.19.k_ref.refs_1_, ...), custom_call_target="tpu_custom_call" | custom-call | flops 377487360 | bytes 2359296 | tf_op jit(solution)/shard_map/spatial/pallas_call | solution.py:240
  24.7 0.0 collective-permute-done.5.rest_3_
  24.8 3.3 %collective-permute-done.6.rest_4_ = bf16[3,3,48,128]{3,2,1,0:T(8,128)(2,1)S(1)} collective-permute-done((bf16[3,3,48,128]{3,2,1,0:T(8,128)(2,1)S(1)}, bf16[3,3,48,128]{3,2,1,0:T(8,128)(2,1)S(1)}, u32[]{:S(2)}, u32[]{:S(2)}) %collective-permute-start.6) | collective-permute-done | bytes 110624 | tf_op jit(solution)/shard_map/ppermute | solution.py:218
  28.0 0.0 collective-permute-done.7.rest_5_
  28.0 0.0 collective-permute-done.8.rest_6_
  28.1 0.0 collective-permute-done.9.rest_7_
  28.1 0.9 %temporal.1 = bf16[8,3,48,128]{3,2,1,0:T(8,128)(2,1)S(1)} custom-call(f32[128,128]{1,0:T(8,128)S(1)} %get-tuple-element.21.bias_ref, bf16[3,3,48,128]{3,2,1,0:T(8,128)(2,1)S(1)} %get-tuple-element.22.rest_0_, bf16[3,3,48,128]{3,2,1,0:T(8,128)(2,1)S(1)} %collective-permute-done.3.rest_1_, bf16[3,3,48,128]{3,2,1,0:T(8,128)(2,1)S(1)} %collective-permute-done.4.rest_2_, ...), custom_call_target="tpu_custom_call" | custom-call | tf_op jit(solution)/shard_map/temporal/pallas_call | solution.py:251
  29.0 15.8 %all_to_all.5.back_ref = bf16[8,3,48,128]{3,2,1,0:T(8,128)(2,1)S(1)} all-to-all(bf16[8,3,48,128]{3,2,1,0:T(8,128)(2,1)S(1)} %temporal.1), channel_id=1, replica_groups=mesh['tm'=8,'head'=4] {'tm'}, dimensions={0} | all-to-all | bytes 589824 | tf_op jit(solution)/shard_map/all_to_all | solution.py:215
  44.8 0.0 collective-permute-start.10
  44.8 1.4 %own.1.whole_ref = bf16[6,8,48,128]{3,2,1,0:T(8,128)(2,1)} custom-call(s32[24]{0:T(128)S(1)} %copy-done, bf16[6,8,48,128]{3,2,1,0:T(8,128)(2,1)S(1)} %bitcast.15, bf16[8,3,48,128]{3,2,1,0:T(8,128)(2,1)S(1)} %all_to_all.5.back_ref), custom_call_target="tpu_custom_call" | custom-call | tf_op jit(solution)/shard_map/own/pallas_call | solution.py:261
  46.2 0.2 collective-permute-done.10.back_ref
  46.4 1.3 %merge.1 = bf16[6,8,48,128]{3,2,1,0:T(8,128)(2,1)} custom-call(s32[24]{0:T(128)S(1)} %copy-done, bf16[8,3,48,128]{3,2,1,0:T(8,128)(2,1)S(1)} %collective-permute-done.10.back_ref, bf16[6,8,48,128]{3,2,1,0:T(8,128)(2,1)} %own.1.whole_ref), custom_call_target="tpu_custom_call", output_to_operand_aliasing={{}: (2, {})} | custom-call | tf_op jit(solution)/shard_map/merge/pallas_call | solution.py:270
  (1 shorter events, 0.0 us)
Async XLA Ops:
  0.0 3.3 %collective-permute-start = (bf16[6,384,128]{2,1,0:T(8,128)(2,1)}, bf16[6,384,128]{2,1,0:T(8,128)(2,1)S(1)}, u32[]{:S(2)}, u32[]{:S(2)}) collective-permute-start(bf16[6,384,128]{2,1,0:T(8,128)(2,1)} %bitcast.16), channel_id=1, source_target_pairs={{0,1},{1,0},{2,3},{3,2},{4,5},{5,4},{6,7},{7,6},{8,9},{9,8},{10,11... | collective-permute-start | bytes 1769480 | tf_op jit(solution)/shard_map/ppermute | solution.py:212
  0.5 0.7 %copy-start = (s32[24]{0:T(128)S(1)}, s32[24]{0:T(128)}, u32[]{:S(2)}) copy-start(s32[24]{0:T(128)} %class_ref.9) | copy-start | bytes 292
  0.5 2.9 %collective-permute-start.1 = (bf16[6,384,128]{2,1,0:T(8,128)(2,1)}, bf16[6,384,128]{2,1,0:T(8,128)(2,1)S(1)}, u32[]{:S(2)}, u32[]{:S(2)}) collective-permute-start(bf16[6,384,128]{2,1,0:T(8,128)(2,1)} %bitcast.18), channel_id=1, source_target_pairs={{0,1},{1,0},{2,3},{3,2},{4,5},{5,4},{6,7},{7,6},{8,9},{9,8},{10,11... | collective-permute-start | bytes 1769480 | tf_op jit(solution)/shard_map/ppermute | solution.py:212
  0.5 3.5 %collective-permute-start.2 = (bf16[6,384,128]{2,1,0:T(8,128)(2,1)}, bf16[6,384,128]{2,1,0:T(8,128)(2,1)S(1)}, u32[]{:S(2)}, u32[]{:S(2)}) collective-permute-start(bf16[6,384,128]{2,1,0:T(8,128)(2,1)} %bitcast.20), channel_id=1, source_target_pairs={{0,1},{1,0},{2,3},{3,2},{4,5},{5,4},{6,7},{7,6},{8,9},{9,8},{10,11... | collective-permute-start | bytes 1769480 | tf_op jit(solution)/shard_map/ppermute | solution.py:212
  4.6 10.9 %collective-permute-start.3 = (bf16[3,3,48,128]{3,2,1,0:T(8,128)(2,1)S(1)}, bf16[3,3,48,128]{3,2,1,0:T(8,128)(2,1)S(1)}, u32[]{:S(2)}, u32[]{:S(2)}) collective-permute-start(bf16[3,3,48,128]{3,2,1,0:T(8,128)(2,1)S(1)} %get-tuple-element.23), channel_id=1, source_target_pairs={{0,16},{4,20},{8,24},{12,28},{16,0},{20,4},{24,8},{28,12},{1,17},{... | collective-permute-start | bytes 331784 | tf_op jit(solution)/shard_map/ppermute | solution.py:218
  8.7 8.6 %collective-permute-start.4 = (bf16[3,3,48,128]{3,2,1,0:T(8,128)(2,1)S(1)}, bf16[3,3,48,128]{3,2,1,0:T(8,128)(2,1)S(1)}, u32[]{:S(2)}, u32[]{:S(2)}) collective-permute-start(bf16[3,3,48,128]{3,2,1,0:T(8,128)(2,1)S(1)} %get-tuple-element.24), channel_id=1, source_target_pairs={{0,8},{4,12},{8,0},{12,4},{16,24},{20,28},{24,16},{28,20},{1,9},{5... | collective-permute-start | bytes 331784 | tf_op jit(solution)/shard_map/ppermute | solution.py:218
  10.2 14.5 %collective-permute-start.5 = (bf16[3,3,48,128]{3,2,1,0:T(8,128)(2,1)S(1)}, bf16[3,3,48,128]{3,2,1,0:T(8,128)(2,1)S(1)}, u32[]{:S(2)}, u32[]{:S(2)}) collective-permute-start(bf16[3,3,48,128]{3,2,1,0:T(8,128)(2,1)S(1)} %get-tuple-element.25), channel_id=1, source_target_pairs={{0,24},{4,28},{8,16},{12,20},{16,8},{20,12},{24,0},{28,4},{1,25},{... | collective-permute-start | bytes 331784 | tf_op jit(solution)/shard_map/ppermute | solution.py:218
  10.2 17.8 %collective-permute-start.6 = (bf16[3,3,48,128]{3,2,1,0:T(8,128)(2,1)S(1)}, bf16[3,3,48,128]{3,2,1,0:T(8,128)(2,1)S(1)}, u32[]{:S(2)}, u32[]{:S(2)}) collective-permute-start(bf16[3,3,48,128]{3,2,1,0:T(8,128)(2,1)S(1)} %get-tuple-element.26), channel_id=1, source_target_pairs={{0,20},{4,16},{8,28},{12,24},{16,4},{20,0},{24,12},{28,8},{1,21},{... | collective-permute-start | bytes 331784 | tf_op jit(solution)/shard_map/ppermute | solution.py:218
  13.1 10.4 %copy-start.1 = (s32[4,4]{1,0:T(4,128)S(1)}, s32[4,4]{1,0:T(4,128)}, u32[]{:S(2)}) copy-start(s32[4,4]{1,0:T(4,128)} %mask_ref.1) | copy-start | bytes 196
  13.1 14.9 %collective-permute-start.7 = (bf16[3,3,48,128]{3,2,1,0:T(8,128)(2,1)S(1)}, bf16[3,3,48,128]{3,2,1,0:T(8,128)(2,1)S(1)}, u32[]{:S(2)}, u32[]{:S(2)}) collective-permute-start(bf16[3,3,48,128]{3,2,1,0:T(8,128)(2,1)S(1)} %get-tuple-element.27), channel_id=1, source_target_pairs={{0,12},{4,8},{8,4},{12,0},{16,28},{20,24},{24,20},{28,16},{1,13},{... | collective-permute-start | bytes 331784 | tf_op jit(solution)/shard_map/ppermute | solution.py:218
  15.5 12.5 %collective-permute-start.8 = (bf16[3,3,48,128]{3,2,1,0:T(8,128)(2,1)S(1)}, bf16[3,3,48,128]{3,2,1,0:T(8,128)(2,1)S(1)}, u32[]{:S(2)}, u32[]{:S(2)}) collective-permute-start(bf16[3,3,48,128]{3,2,1,0:T(8,128)(2,1)S(1)} %get-tuple-element.28), channel_id=1, source_target_pairs={{0,4},{4,0},{8,12},{12,8},{16,20},{20,16},{24,28},{28,24},{1,5},{5... | collective-permute-start | bytes 331784 | tf_op jit(solution)/shard_map/ppermute | solution.py:218
  17.3 10.8 %collective-permute-start.9 = (bf16[3,3,48,128]{3,2,1,0:T(8,128)(2,1)S(1)}, bf16[3,3,48,128]{3,2,1,0:T(8,128)(2,1)S(1)}, u32[]{:S(2)}, u32[]{:S(2)}) collective-permute-start(bf16[3,3,48,128]{3,2,1,0:T(8,128)(2,1)S(1)} %get-tuple-element.29), channel_id=1, source_target_pairs={{0,28},{4,24},{8,20},{12,16},{16,12},{20,8},{24,4},{28,0},{1,29},{... | collective-permute-start | bytes 331784 | tf_op jit(solution)/shard_map/ppermute | solution.py:218
  44.8 1.6 %collective-permute-start.10 = (bf16[8,3,48,128]{3,2,1,0:T(8,128)(2,1)S(1)}, bf16[8,3,48,128]{3,2,1,0:T(8,128)(2,1)S(1)}, u32[]{:S(2)}, u32[]{:S(2)}) collective-permute-start(bf16[8,3,48,128]{3,2,1,0:T(8,128)(2,1)S(1)} %all_to_all.5.back_ref), channel_id=1, source_target_pairs={{0,1},{1,0},{2,3},{3,2},{4,5},{5,4},{6,7},{7,6},{8,9},{9,8},{10,11... | collective-permute-start | bytes 884744 | tf_op jit(solution)/shard_map/ppermute | solution.py:212

commit v3 on v2

--- a/solution.py
+++ b/solution.py
@@ -78,12 +78,22 @@
         return carry
 
     lax.fori_loop(0, group_heads - temporal, body, 0)
-    fill_bias(bias_ref, mask_ref, frames_held(ranks), blocks)
+    fill_bias(bias_ref, mask_ref, frames_held(distances(ranks)), blocks)
 
 
 def distances(ranks):
     far, near = [*range(ranks // 2, ranks, 2), *range(ranks // 2 + 1, ranks, 2)], list(range(1, ranks // 2))[::-1]
-    return [0, *far[:1], *near[-2:-1], *far[1:3], *near[:-2], *near[-1:], *far[3:]]
+    return [0, *far[:1], *near[-2:-1], *far[1:2], *near[:-2], *near[-1:], *far[2:]]
+
+
+def back_distances(ranks):
+    far, near = list(range(ranks // 2, ranks)), list(range(1, ranks // 2))
+    cut = len(far) // 2
+    return [0, *far[cut:], *far[:cut], *near[1:], *near[:1]]
+
+
+def block_rows(rank, share):
+    return pl.ds(pl.multiple_of(rank * share, ROWS), share)
 
 
 def pack_kernel(sizes, class_ref, *refs):
@@ -92,7 +102,7 @@
     own_refs, other_refs, out_refs, order_ref = refs[:3], refs[3:6], refs[6:-1], refs[-1]
     temporal = rank_heads(class_ref, order_ref, group_heads)
     me = lax.axis_index("tm")
-    rows = [pl.ds(pl.multiple_of((me ^ step) * share, ROWS), share) for step in range(ranks)]
+    rows = [block_rows(me ^ step, share) for step in range(ranks)]
 
     def put(slots, refs, ref_slot):
         for slot in slots:
@@ -113,9 +123,9 @@
         put(range(least, least + handed), other_refs, lambda slot: slot - least + most - handed)
 
 
-def frames_held(ranks):
+def frames_held(steps):
     me = lax.axis_index("tm")
-    return [me ^ step for step in distances(ranks)]
+    return [me ^ step for step in steps]
 
 
 def fill_bias(bias_ref, mask_ref, frames, blocks):
@@ -132,8 +142,7 @@
 
 def temporal_kernel(sizes, bias_ref, *rest):
     slots, ranks, share = sizes
-    in_refs, out_ref = rest[:ranks], rest[ranks]
-    frames = frames_held(ranks)
+    in_refs, out_refs = rest[:ranks], rest[ranks:]
     for slot in range(slots):
         groups = [pl.ds(start, ROWS) for start in range(0, share, ROWS)]
         triples = [
@@ -141,20 +150,31 @@
             for rows in groups
         ]
         for rows, blended in zip(groups, attend(triples, bias_ref[...])):
-            for step, frame in enumerate(frames):
-                out_ref[frame, slot, rows, :] = blended[step * ROWS : (step + 1) * ROWS]
-
-
-def head_copies(ref, out_ref, order_ref, slots, ref_slot):
-    return [(ref.at[:, ref_slot(slot)], out_ref.at[order_ref[slot]]) for slot in slots]
-
-
-def own_kernel(sizes, class_ref, spatial_ref, back_ref, out_ref, order_ref, sems):
-    group_heads, most, least = sizes
+            for at, out_ref in enumerate(out_refs):
+                out_ref[slot, rows, :] = blended[at * ROWS : (at + 1) * ROWS]
+
+
+def gather_kernel(sizes, *refs):
+    least, ranks, share = sizes
+    *back_refs, out_ref = refs
+    for frame, back_ref in zip(frames_held(back_distances(ranks)), back_refs):
+        for slot in range(out_ref.shape[0]):
+            out_ref[slot, block_rows(frame, share), :] = back_ref[least + slot]
+
+
+def own_kernel(sizes, class_ref, spatial_ref, *rest):
+    group_heads, most, least, ranks, share = sizes
+    back_refs = rest[:ranks]
+    out_ref, order_ref, sems = rest[ranks:]
     temporal = rank_heads(class_ref, order_ref, group_heads)
+    rows = [block_rows(frame, share) for frame in frames_held(back_distances(ranks))]
 
     def run(count, slots):
-        copies = head_copies(back_ref, out_ref, order_ref, slots, lambda slot: slot)
+        copies = [
+            (back_ref.at[slot], out_ref.at[order_ref[slot], block, :])
+            for slot in slots
+            for block, back_ref in zip(rows, back_refs)
+        ]
         for slot in range(group_heads - count):
             head = order_ref[group_heads + slot]
             copies.append((spatial_ref.at[head], out_ref.at[head]))
@@ -169,15 +189,15 @@
         run(least, range(least))
 
 
-def merge_kernel(sizes, class_ref, back_ref, whole_ref, out_ref, order_ref, sems):
+def merge_kernel(sizes, class_ref, given_ref, whole_ref, out_ref, order_ref, sems):
     group_heads, most, least = sizes
     handed = (most - least) // 2
     temporal = rank_heads(class_ref, order_ref, group_heads)
 
     @pl.when(temporal == most)
     def _():
-        slots = range(least + handed, most)
-        copy_all(head_copies(back_ref, out_ref, order_ref, slots, lambda slot: slot - handed), sems)()
+        slots = range(handed)
+        copy_all([(given_ref.at[slot], out_ref.at[order_ref[most - handed + slot]]) for slot in slots], sems)()
 
 
 def per_device(head_total, queries, key_vectors, value_vectors, head_class, frame_mask):
@@ -200,7 +220,6 @@
     pairs = [(h, h ^ 1) for h in range(head_total)]
     whole = jax.ShapeDtypeStruct(q.shape, q.dtype)
     steps = distances(ranks)
-    by_rank = jax.ShapeDtypeStruct((group_heads, ranks, share, width), q.dtype)
     packed_shape = [jax.ShapeDtypeStruct((slots, 3, share, width), q.dtype)] * ranks
     cost = pl.CostEstimate(
         flops=4 * most * patches * patches * width,
@@ -210,9 +229,6 @@
 
     def swap(array):
         return lax.ppermute(array, "head", pairs)
-
-    def exchange(array):
-        return lax.all_to_all(array, "tm", split_axis=0, concat_axis=0, tiled=True)
 
     def send(array, step):
         return lax.ppermute(array, "tm", [(rank, rank ^ step) for rank in range(ranks)])
@@ -247,29 +263,38 @@
         cost_estimate=cost,
         name="spatial",
     )(head_class, frame_mask, q, k, v)
-    back = exchange(
+    blended = pl.pallas_call(
+        functools.partial(temporal_kernel, (slots, ranks, share)),
+        out_shape=[jax.ShapeDtypeStruct((slots, share, width), q.dtype)] * ranks,
+        in_specs=[vmem] * (1 + ranks),
+        out_specs=[vmem] * ranks,
+        compiler_params=params,
+        name="temporal",
+    )(bias, *arrived)
+    by_step = dict(zip(steps, blended))
+    back = [by_step[0]] + [send(by_step[step], step) for step in back_distances(ranks)[1:]]
+    returned = swap(
         pl.pallas_call(
-            functools.partial(temporal_kernel, (slots, ranks, share)),
-            out_shape=jax.ShapeDtypeStruct((ranks, slots, share, width), q.dtype),
-            in_specs=[vmem] * (1 + ranks),
+            functools.partial(gather_kernel, (least, ranks, share)),
+            out_shape=jax.ShapeDtypeStruct((handed, patches, width), q.dtype),
+            in_specs=[vmem] * ranks,
             out_specs=vmem,
             compiler_params=params,
-            name="temporal",
-        )(bias, *arrived)
-    )
-    returned = swap(back)
+            name="gather",
+        )(*back)
+    )
     mostly = pl.pallas_call(
-        functools.partial(own_kernel, (group_heads, most, least)),
-        out_shape=by_rank,
-        in_specs=[smem] + [vmem] * 2,
+        functools.partial(own_kernel, (group_heads, most, least, ranks, share)),
+        out_shape=whole,
+        in_specs=[smem] + [vmem] * (1 + ranks),
         out_specs=hbm,
-        scratch_shapes=[order, pltpu.SemaphoreType.DMA((slots + group_heads,))],
+        scratch_shapes=[order, pltpu.SemaphoreType.DMA((slots * ranks + group_heads,))],
         compiler_params=params,
         name="own",
-    )(head_class, spatial.reshape(by_rank.shape), back)
+    )(head_class, spatial, *back)
     merged = pl.pallas_call(
         functools.partial(merge_kernel, (group_heads, most, least)),
-        out_shape=by_rank,
+        out_shape=whole,
         in_specs=[smem, vmem, hbm],
         out_specs=hbm,
         scratch_shapes=[order, pltpu.SemaphoreType.DMA((handed,))],
@@ -277,7 +302,7 @@
         compiler_params=params,
         name="merge",
     )(head_class, returned, mostly)
-    return jnp.moveaxis(merged.reshape(q.shape), 0, 1)[None]
+    return jnp.moveaxis(merged, 0, 1)[None]
 
 
 def frame_attend(triple):

time: 47.9 us -> 46.1 us (0.962)
  blocking collectives: 15.8 us -> 0 us
  waiting for transfers between devices: 4.14 us -> 12 us
  starting transfers between devices: 19.8 us -> 25.9 us
    all_to_all x1 -> x0, blocking collectives: 15.8 us -> none  [exchange(): return lax.all_to_all(array, 'tm', split_axis=0, concat_axis=0, tiled=True)]
    ppermute x7 -> x14, waiting for transfers between devices: 3.31 us -> 11.3 us  [send(): lax.ppermute(array, 'tm', [(rank, rank ^ step) for rank in range(ranks)])]
    ppermute x7 -> x14, starting transfers between devices: 18.9 us -> 24.9 us  [send(): lax.ppermute(array, 'tm', [(rank, rank ^ step) for rank in range(ranks)])]
    pallas_call x1 -> x2, Pallas kernels: 1.38 us -> 1.6 us  [the longest x1 1.58 us: per_device(): pl.pallas_call(functools.partial(own_kernel, (group_heads, most, least, r...]
  transfers between devices with their start and end apart: 11 -> 18, of which waited for: 3 -> 6; matrix products, arithmetic and copies ran while one was open for 0% -> 0% of each run, Pallas kernels for 10% -> 11%
where the time goes in v3:
time: 46.1 us; the launch traced here: 46 us
  starting transfers between devices  25.9 us (56%)
  waiting for transfers between devices  12 us (26%)
  Pallas kernels  7.86 us (17%)
    ppermute x14, starting transfers between devices, send(): lax.ppermute(array, 'tm', [(rank, rank ^ step) for rank in range(ranks)])  24.9 us
    ppermute x14, waiting for transfers between devices, send(): lax.ppermute(array, 'tm', [(rank, rank ^ step) for rank in range(ranks)])  11.3 us
    pallas_call x1, Pallas kernels, per_device(): pl.pallas_call(load_kernel, out_shape=[whole] * 3, in_specs=[smem] + [hbm...  2.21 us
    pallas_call x1, Pallas kernels, per_device(): pl.pallas_call(functools.partial(own_kernel, (group_heads, most, least, r...  1.58 us
    pallas_call x1, Pallas kernels, per_device(): pl.pallas_call(functools.partial(merge_kernel, (group_heads, most, least)...  1.26 us
    pallas_call x1, Pallas kernels, per_device(): pl.pallas_call(functools.partial(spatial_kernel, (group_heads, ranks, blo...  1.2 us
    ppermute x4, starting transfers between devices, swap(): return lax.ppermute(array, 'head', pairs)  1.03 us
    pallas_call x1, Pallas kernels, per_device(): pl.pallas_call(functools.partial(temporal_kernel, (slots, ranks, share)),...  0.94 us
  transfers between devices with their start and end apart: 18, of which 6 were waited for; matrix products, arithmetic and copies ran while one was open for 0% of the time, Pallas kernels for 11%

profile of v3, /device:TPU:0, one launch (start us, length us, event | category | flops | bytes accessed | tf_op | source)
XLA Modules:
  0.0 46.0 jit_solution(8603256886143411499)
XLA Ops:
  0.0 0.5 collective-permute-start
  0.5 0.1 collective-permute-start.1
  0.5 0.4 collective-permute-start.2
  1.0 0.1 copy-done
  1.1 2.2 %load.1 = (bf16[6,384,128]{2,1,0:T(8,128)(2,1)S(1)}, bf16[6,384,128]{2,1,0:T(8,128)(2,1)S(1)}, bf16[6,384,128]{2,1,0:T(8,128)(2,1)S(1)}) custom-call(s32[24]{0:T(128)S(1)} %copy-done, bf16[6,384,128]{2,1,0:T(8,128)(2,1)} %bitcast.13, bf16[6,384,128]{2,1,0:T(8,128)(2,1)} %bitcast.15, bf16[6,384,128]{2,1,0:T(8,128)(2,1)} %bitcast.17), custom_call_target="tpu_custom_call" | custom-call | tf_op jit(solution)/shard_map/load/pallas_call | solution.py:237
  3.3 0.0 collective-permute-done.1.refs_4_
  3.3 0.6 %collective-permute-done.2.refs_5_ = bf16[6,384,128]{2,1,0:T(8,128)(2,1)S(1)} collective-permute-done((bf16[6,384,128]{2,1,0:T(8,128)(2,1)}, bf16[6,384,128]{2,1,0:T(8,128)(2,1)S(1)}, u32[]{:S(2)}, u32[]{:S(2)}) %collective-permute-start.2) | collective-permute-done | bytes 589856 | tf_op jit(solution)/shard_map/ppermute | solution.py:231
  4.0 0.6 %pack.1 = (bf16[3,3,48,128]{3,2,1,0:T(8,128)(2,1)S(1)}, bf16[3,3,48,128]{3,2,1,0:T(8,128)(2,1)S(1)}, bf16[3,3,48,128]{3,2,1,0:T(8,128)(2,1)S(1)}, bf16[3,3,48,12...) custom-call(s32[24]{0:T(128)S(1)} %copy-done, ...), custom_call_target="tpu_custom_call" | custom-call | tf_op jit(solution)/shard_map/pack/pallas_call | solution.py:246
  4.6 4.0 %collective-permute-start.3 = (bf16[3,3,48,128]{3,2,1,0:T(8,128)(2,1)S(1)}, bf16[3,3,48,128]{3,2,1,0:T(8,128)(2,1)S(1)}, u32[]{:S(2)}, u32[]{:S(2)}) collective-permute-start(bf16[3,3,48,128]{3,2,1,0:T(8,128)(2,1)S(1)} %get-tuple-element.31), channel_id=1, source_target_pairs={{0,16},{4,20},{8,24},{12,28},{16,0},{20,4},{24,8},{28,12},{1,17},{... | collective-permute-start | bytes 331784 | tf_op jit(solution)/shard_map/ppermute | solution.py:234
  8.7 1.6 %collective-permute-start.4 = (bf16[3,3,48,128]{3,2,1,0:T(8,128)(2,1)S(1)}, bf16[3,3,48,128]{3,2,1,0:T(8,128)(2,1)S(1)}, u32[]{:S(2)}, u32[]{:S(2)}) collective-permute-start(bf16[3,3,48,128]{3,2,1,0:T(8,128)(2,1)S(1)} %get-tuple-element.32), channel_id=1, source_target_pairs={{0,8},{4,12},{8,0},{12,4},{16,24},{20,28},{24,16},{28,20},{1,9},{5... | collective-permute-start | bytes 331784 | tf_op jit(solution)/shard_map/ppermute | solution.py:234
  10.2 0.0 collective-permute-start.5
  10.2 1.9 %collective-permute-start.6 = (bf16[3,3,48,128]{3,2,1,0:T(8,128)(2,1)S(1)}, bf16[3,3,48,128]{3,2,1,0:T(8,128)(2,1)S(1)}, u32[]{:S(2)}, u32[]{:S(2)}) collective-permute-start(bf16[3,3,48,128]{3,2,1,0:T(8,128)(2,1)S(1)} %get-tuple-element.34), channel_id=1, source_target_pairs={{0,12},{4,8},{8,4},{12,0},{16,28},{20,24},{24,20},{28,16},{1,13},{... | collective-permute-start | bytes 331784 | tf_op jit(solution)/shard_map/ppermute | solution.py:234
  12.1 0.5 %collective-permute-start.7 = (bf16[3,3,48,128]{3,2,1,0:T(8,128)(2,1)S(1)}, bf16[3,3,48,128]{3,2,1,0:T(8,128)(2,1)S(1)}, u32[]{:S(2)}, u32[]{:S(2)}) collective-permute-start(bf16[3,3,48,128]{3,2,1,0:T(8,128)(2,1)S(1)} %get-tuple-element.35), channel_id=1, source_target_pairs={{0,4},{4,0},{8,12},{12,8},{16,20},{20,16},{24,28},{28,24},{1,5},{5... | collective-permute-start | bytes 331784 | tf_op jit(solution)/shard_map/ppermute | solution.py:234
  12.6 2.4 %collective-permute-done.3.rest_1_ = bf16[3,3,48,128]{3,2,1,0:T(8,128)(2,1)S(1)} collective-permute-done((bf16[3,3,48,128]{3,2,1,0:T(8,128)(2,1)S(1)}, bf16[3,3,48,128]{3,2,1,0:T(8,128)(2,1)S(1)}, u32[]{:S(2)}, u32[]{:S(2)}) %collective-permute-start.3) | collective-permute-done | bytes 110624 | tf_op jit(solution)/shard_map/ppermute | solution.py:234
  15.0 2.0 %collective-permute-start.8 = (bf16[3,3,48,128]{3,2,1,0:T(8,128)(2,1)S(1)}, bf16[3,3,48,128]{3,2,1,0:T(8,128)(2,1)S(1)}, u32[]{:S(2)}, u32[]{:S(2)}) collective-permute-start(bf16[3,3,48,128]{3,2,1,0:T(8,128)(2,1)S(1)} %get-tuple-element.36), channel_id=1, source_target_pairs={{0,20},{4,16},{8,28},{12,24},{16,4},{20,0},{24,12},{28,8},{1,21},{... | collective-permute-start | bytes 331784 | tf_op jit(solution)/shard_map/ppermute | solution.py:234
  17.1 3.7 %collective-permute-start.9 = (bf16[3,3,48,128]{3,2,1,0:T(8,128)(2,1)S(1)}, bf16[3,3,48,128]{3,2,1,0:T(8,128)(2,1)S(1)}, u32[]{:S(2)}, u32[]{:S(2)}) collective-permute-start(bf16[3,3,48,128]{3,2,1,0:T(8,128)(2,1)S(1)} %get-tuple-element.37), channel_id=1, source_target_pairs={{0,28},{4,24},{8,20},{12,16},{16,12},{20,8},{24,4},{28,0},{1,29},{... | collective-permute-start | bytes 331784 | tf_op jit(solution)/shard_map/ppermute | solution.py:234
  20.7 1.2 %spatial.1 = (bf16[6,384,128]{2,1,0:T(8,128)(2,1)S(1)}, f32[128,128]{1,0:T(8,128)S(1)}) custom-call(s32[24]{0:T(128)S(1)} %copy-done, s32[4,4]{1,0:T(4,128)S(1)} %copy-done.1, bf16[6,384,128]{2,1,0:T(8,128)(2,1)S(1)} %get-tuple-element.26.q_ref.refs_0_, bf16[6,384,128]{2,1,0:T(8,128)(2,1)S(1)} %get-tuple-element.27.k_ref.refs_1_, ...), custom_call_target="tpu_custom_call" | custom-call | flops 377487360 | bytes 2359296 | tf_op jit(solution)/shard_map/spatial/pallas_call | solution.py:256
  22.0 6.1 %collective-permute-done.8.rest_6_ = bf16[3,3,48,128]{3,2,1,0:T(8,128)(2,1)S(1)} collective-permute-done((bf16[3,3,48,128]{3,2,1,0:T(8,128)(2,1)S(1)}, bf16[3,3,48,128]{3,2,1,0:T(8,128)(2,1)S(1)}, u32[]{:S(2)}, u32[]{:S(2)}) %collective-permute-start.8) | collective-permute-done | bytes 110624 | tf_op jit(solution)/shard_map/ppermute | solution.py:234
  28.0 0.9 %temporal.1 = (bf16[3,48,128]{2,1,0:T(8,128)(2,1)S(1)}, bf16[3,48,128]{2,1,0:T(8,128)(2,1)S(1)}, bf16[3,48,128]{2,1,0:T(8,128)(2,1)S(1)}, bf16[3,48,128]{2,1,0:T...) custom-call(f32[128,128]{1,0:T(8,128)S(1)} %get-tuple-element.29.bia, ...), custom_call_target="tpu_custom_call" | custom-call | tf_op jit(solution)/shard_map/temporal/pallas_call | solution.py:266
  29.0 2.9 %collective-permute-start.10 = (bf16[3,48,128]{2,1,0:T(8,128)(2,1)S(1)}, bf16[3,48,128]{2,1,0:T(8,128)(2,1)S(1)}, u32[]{:S(2)}, u32[]{:S(2)}) collective-permute-start(bf16[3,48,128]{2,1,0:T(8,128)(2,1)S(1)} %get-tuple-element.39), channel_id=1, source_target_pairs={{0,24},{4,28},{8,16},{12,20},{16,8},{20,12},{24,0},{28,4},{1,25},{... | collective-permute-start | bytes 110600 | tf_op jit(solution)/shard_map/ppermute | solution.py:234
  31.9 1.3 %collective-permute-start.11 = (bf16[3,48,128]{2,1,0:T(8,128)(2,1)S(1)}, bf16[3,48,128]{2,1,0:T(8,128)(2,1)S(1)}, u32[]{:S(2)}, u32[]{:S(2)}) collective-permute-start(bf16[3,48,128]{2,1,0:T(8,128)(2,1)S(1)} %get-tuple-element.40), channel_id=1, source_target_pairs={{0,28},{4,24},{8,20},{12,16},{16,12},{20,8},{24,4},{28,0},{1,29},{... | collective-permute-start | bytes 110600 | tf_op jit(solution)/shard_map/ppermute | solution.py:234
  33.2 2.1 %collective-permute-start.12 = (bf16[3,48,128]{2,1,0:T(8,128)(2,1)S(1)}, bf16[3,48,128]{2,1,0:T(8,128)(2,1)S(1)}, u32[]{:S(2)}, u32[]{:S(2)}) collective-permute-start(bf16[3,48,128]{2,1,0:T(8,128)(2,1)S(1)} %get-tuple-element.41), channel_id=1, source_target_pairs={{0,16},{4,20},{8,24},{12,28},{16,0},{20,4},{24,8},{28,12},{1,17},{... | collective-permute-start | bytes 110600 | tf_op jit(solution)/shard_map/ppermute | solution.py:234
  35.2 1.5 %collective-permute-start.13 = (bf16[3,48,128]{2,1,0:T(8,128)(2,1)S(1)}, bf16[3,48,128]{2,1,0:T(8,128)(2,1)S(1)}, u32[]{:S(2)}, u32[]{:S(2)}) collective-permute-start(bf16[3,48,128]{2,1,0:T(8,128)(2,1)S(1)} %get-tuple-element.42), channel_id=1, source_target_pairs={{0,20},{4,16},{8,28},{12,24},{16,4},{20,0},{24,12},{28,8},{1,21},{... | collective-permute-start | bytes 110600 | tf_op jit(solution)/shard_map/ppermute | solution.py:234
  36.7 1.0 %collective-permute-start.14 = (bf16[3,48,128]{2,1,0:T(8,128)(2,1)S(1)}, bf16[3,48,128]{2,1,0:T(8,128)(2,1)S(1)}, u32[]{:S(2)}, u32[]{:S(2)}) collective-permute-start(bf16[3,48,128]{2,1,0:T(8,128)(2,1)S(1)} %get-tuple-element.43), channel_id=1, source_target_pairs={{0,8},{4,12},{8,0},{12,4},{16,24},{20,28},{24,16},{28,20},{1,9},{5... | collective-permute-start | bytes 110600 | tf_op jit(solution)/shard_map/ppermute | solution.py:234
  37.7 1.3 %collective-permute-start.15 = (bf16[3,48,128]{2,1,0:T(8,128)(2,1)S(1)}, bf16[3,48,128]{2,1,0:T(8,128)(2,1)S(1)}, u32[]{:S(2)}, u32[]{:S(2)}) collective-permute-start(bf16[3,48,128]{2,1,0:T(8,128)(2,1)S(1)} %get-tuple-element.44), channel_id=1, source_target_pairs={{0,12},{4,8},{8,4},{12,0},{16,28},{20,24},{24,20},{28,16},{1,13},{... | collective-permute-start | bytes 110600 | tf_op jit(solution)/shard_map/ppermute | solution.py:234
  39.0 1.2 %collective-permute-start.16 = (bf16[3,48,128]{2,1,0:T(8,128)(2,1)S(1)}, bf16[3,48,128]{2,1,0:T(8,128)(2,1)S(1)}, u32[]{:S(2)}, u32[]{:S(2)}) collective-permute-start(bf16[3,48,128]{2,1,0:T(8,128)(2,1)S(1)} %get-tuple-element.45), channel_id=1, source_target_pairs={{0,4},{4,0},{8,12},{12,8},{16,20},{20,16},{24,28},{28,24},{1,5},{5... | collective-permute-start | bytes 110600 | tf_op jit(solution)/shard_map/ppermute | solution.py:234
  40.2 0.8 %collective-permute-done.13.refs_4_.rest_4_ = bf16[3,48,128]{2,1,0:T(8,128)(2,1)S(1)} collective-permute-done((bf16[3,48,128]{2,1,0:T(8,128)(2,1)S(1)}, bf16[3,48,128]{2,1,0:T(8,128)(2,1)S(1)}, u32[]{:S(2)}, u32[]{:S(2)}) %collective-permute-start.13) | collective-permute-done | bytes 36896 | tf_op jit(solution)/shard_map/ppermute | solution.py:234
  41.0 1.6 %collective-permute-done.15.refs_6_.rest_6_ = bf16[3,48,128]{2,1,0:T(8,128)(2,1)S(1)} collective-permute-done((bf16[3,48,128]{2,1,0:T(8,128)(2,1)S(1)}, bf16[3,48,128]{2,1,0:T(8,128)(2,1)S(1)}, u32[]{:S(2)}, u32[]{:S(2)}) %collective-permute-start.15) | collective-permute-done | bytes 36896 | tf_op jit(solution)/shard_map/ppermute | solution.py:234
  42.6 0.4 collective-permute-done.16.refs_7_.rest_7_
  43.0 0.1 collective-permute-start.17
  43.1 1.6 %own.1.whole_ref = bf16[6,384,128]{2,1,0:T(8,128)(2,1)} custom-call(s32[24]{0:T(128)S(1)} %copy-done, bf16[6,384,128]{2,1,0:T(8,128)(2,1)S(1)} %get-tuple-element.46.spatial_ref, bf16[3,48,128]{2,1,0:T(8,128)(2,1)S(1)} %get-tuple-element.38.refs_0_.rest_0_, bf16[3,48,128]{2,1,0:T(8,128)(2,1)S(1)} %collective-permute-done.10.refs_1_.rest_1_, ...), custom_call_target="tpu_custom_call" | custom-call | tf_op jit(solution)/shard_map/own/pallas_call | solution.py:286
  44.7 1.3 %merge.1 = bf16[6,384,128]{2,1,0:T(8,128)(2,1)} custom-call(s32[24]{0:T(128)S(1)} %copy-done, bf16[2,384,128]{2,1,0:T(8,128)(2,1)S(1)} %collective-permute-done.17.given_ref, bf16[6,384,128]{2,1,0:T(8,128)(2,1)} %own.1.whole_ref), custom_call_target="tpu_custom_call", output_to_operand_aliasing={{}: (2, {})} | custom-call | tf_op jit(solution)/shard_map/merge/pallas_call | solution.py:295
  (15 shorter events, 0.1 us)
Async XLA Ops:
  0.0 3.3 %collective-permute-start = (bf16[6,384,128]{2,1,0:T(8,128)(2,1)}, bf16[6,384,128]{2,1,0:T(8,128)(2,1)S(1)}, u32[]{:S(2)}, u32[]{:S(2)}) collective-permute-start(bf16[6,384,128]{2,1,0:T(8,128)(2,1)} %bitcast.12), channel_id=1, source_target_pairs={{0,1},{1,0},{2,3},{3,2},{4,5},{5,4},{6,7},{7,6},{8,9},{9,8},{10,11... | collective-permute-start | bytes 1769480 | tf_op jit(solution)/shard_map/ppermute | solution.py:231
  0.5 0.7 %copy-start = (s32[24]{0:T(128)S(1)}, s32[24]{0:T(128)}, u32[]{:S(2)}) copy-start(s32[24]{0:T(128)} %class_ref.9) | copy-start | bytes 292
  0.5 2.9 %collective-permute-start.1 = (bf16[6,384,128]{2,1,0:T(8,128)(2,1)}, bf16[6,384,128]{2,1,0:T(8,128)(2,1)S(1)}, u32[]{:S(2)}, u32[]{:S(2)}) collective-permute-start(bf16[6,384,128]{2,1,0:T(8,128)(2,1)} %bitcast.14), channel_id=1, source_target_pairs={{0,1},{1,0},{2,3},{3,2},{4,5},{5,4},{6,7},{7,6},{8,9},{9,8},{10,11... | collective-permute-start | bytes 1769480 | tf_op jit(solution)/shard_map/ppermute | solution.py:231
  0.5 3.5 %collective-permute-start.2 = (bf16[6,384,128]{2,1,0:T(8,128)(2,1)}, bf16[6,384,128]{2,1,0:T(8,128)(2,1)S(1)}, u32[]{:S(2)}, u32[]{:S(2)}) collective-permute-start(bf16[6,384,128]{2,1,0:T(8,128)(2,1)} %bitcast.16), channel_id=1, source_target_pairs={{0,1},{1,0},{2,3},{3,2},{4,5},{5,4},{6,7},{7,6},{8,9},{9,8},{10,11... | collective-permute-start | bytes 1769480 | tf_op jit(solution)/shard_map/ppermute | solution.py:231
  4.6 10.4 %collective-permute-start.3 = (bf16[3,3,48,128]{3,2,1,0:T(8,128)(2,1)S(1)}, bf16[3,3,48,128]{3,2,1,0:T(8,128)(2,1)S(1)}, u32[]{:S(2)}, u32[]{:S(2)}) collective-permute-start(bf16[3,3,48,128]{3,2,1,0:T(8,128)(2,1)S(1)} %get-tuple-element.31), channel_id=1, source_target_pairs={{0,16},{4,20},{8,24},{12,28},{16,0},{20,4},{24,8},{28,12},{1,17},{... | collective-permute-start | bytes 331784 | tf_op jit(solution)/shard_map/ppermute | solution.py:234
  8.7 8.4 %collective-permute-start.4 = (bf16[3,3,48,128]{3,2,1,0:T(8,128)(2,1)S(1)}, bf16[3,3,48,128]{3,2,1,0:T(8,128)(2,1)S(1)}, u32[]{:S(2)}, u32[]{:S(2)}) collective-permute-start(bf16[3,3,48,128]{3,2,1,0:T(8,128)(2,1)S(1)} %get-tuple-element.32), channel_id=1, source_target_pairs={{0,8},{4,12},{8,0},{12,4},{16,24},{20,28},{24,16},{28,20},{1,9},{5... | collective-permute-start | bytes 331784 | tf_op jit(solution)/shard_map/ppermute | solution.py:234
  10.2 11.7 %collective-permute-start.5 = (bf16[3,3,48,128]{3,2,1,0:T(8,128)(2,1)S(1)}, bf16[3,3,48,128]{3,2,1,0:T(8,128)(2,1)S(1)}, u32[]{:S(2)}, u32[]{:S(2)}) collective-permute-start(bf16[3,3,48,128]{3,2,1,0:T(8,128)(2,1)S(1)} %get-tuple-element.33), channel_id=1, source_target_pairs={{0,24},{4,28},{8,16},{12,20},{16,8},{20,12},{24,0},{28,4},{1,25},{... | collective-permute-start | bytes 331784 | tf_op jit(solution)/shard_map/ppermute | solution.py:234
  10.2 11.7 %collective-permute-start.6 = (bf16[3,3,48,128]{3,2,1,0:T(8,128)(2,1)S(1)}, bf16[3,3,48,128]{3,2,1,0:T(8,128)(2,1)S(1)}, u32[]{:S(2)}, u32[]{:S(2)}) collective-permute-start(bf16[3,3,48,128]{3,2,1,0:T(8,128)(2,1)S(1)} %get-tuple-element.34), channel_id=1, source_target_pairs={{0,12},{4,8},{8,4},{12,0},{16,28},{20,24},{24,20},{28,16},{1,13},{... | collective-permute-start | bytes 331784 | tf_op jit(solution)/shard_map/ppermute | solution.py:234
  12.1 8.6 %copy-start.1 = (s32[4,4]{1,0:T(4,128)S(1)}, s32[4,4]{1,0:T(4,128)}, u32[]{:S(2)}) copy-start(s32[4,4]{1,0:T(4,128)} %mask_ref.1) | copy-start | bytes 196
  12.1 9.9 %collective-permute-start.7 = (bf16[3,3,48,128]{3,2,1,0:T(8,128)(2,1)S(1)}, bf16[3,3,48,128]{3,2,1,0:T(8,128)(2,1)S(1)}, u32[]{:S(2)}, u32[]{:S(2)}) collective-permute-start(bf16[3,3,48,128]{3,2,1,0:T(8,128)(2,1)S(1)} %get-tuple-element.35), channel_id=1, source_target_pairs={{0,4},{4,0},{8,12},{12,8},{16,20},{20,16},{24,28},{28,24},{1,5},{5... | collective-permute-start | bytes 331784 | tf_op jit(solution)/shard_map/ppermute | solution.py:234
  15.0 13.0 %collective-permute-start.8 = (bf16[3,3,48,128]{3,2,1,0:T(8,128)(2,1)S(1)}, bf16[3,3,48,128]{3,2,1,0:T(8,128)(2,1)S(1)}, u32[]{:S(2)}, u32[]{:S(2)}) collective-permute-start(bf16[3,3,48,128]{3,2,1,0:T(8,128)(2,1)S(1)} %get-tuple-element.36), channel_id=1, source_target_pairs={{0,20},{4,16},{8,28},{12,24},{16,4},{20,0},{24,12},{28,8},{1,21},{... | collective-permute-start | bytes 331784 | tf_op jit(solution)/shard_map/ppermute | solution.py:234
  17.1 11.0 %collective-permute-start.9 = (bf16[3,3,48,128]{3,2,1,0:T(8,128)(2,1)S(1)}, bf16[3,3,48,128]{3,2,1,0:T(8,128)(2,1)S(1)}, u32[]{:S(2)}, u32[]{:S(2)}) collective-permute-start(bf16[3,3,48,128]{3,2,1,0:T(8,128)(2,1)S(1)} %get-tuple-element.37), channel_id=1, source_target_pairs={{0,28},{4,24},{8,20},{12,16},{16,12},{20,8},{24,4},{28,0},{1,29},{... | collective-permute-start | bytes 331784 | tf_op jit(solution)/shard_map/ppermute | solution.py:234
  29.0 8.7 %collective-permute-start.10 = (bf16[3,48,128]{2,1,0:T(8,128)(2,1)S(1)}, bf16[3,48,128]{2,1,0:T(8,128)(2,1)S(1)}, u32[]{:S(2)}, u32[]{:S(2)}) collective-permute-start(bf16[3,48,128]{2,1,0:T(8,128)(2,1)S(1)} %get-tuple-element.39), channel_id=1, source_target_pairs={{0,24},{4,28},{8,16},{12,20},{16,8},{20,12},{24,0},{28,4},{1,25},{... | collective-permute-start | bytes 110600 | tf_op jit(solution)/shard_map/ppermute | solution.py:234
  31.9 7.1 %collective-permute-start.11 = (bf16[3,48,128]{2,1,0:T(8,128)(2,1)S(1)}, bf16[3,48,128]{2,1,0:T(8,128)(2,1)S(1)}, u32[]{:S(2)}, u32[]{:S(2)}) collective-permute-start(bf16[3,48,128]{2,1,0:T(8,128)(2,1)S(1)} %get-tuple-element.40), channel_id=1, source_target_pairs={{0,28},{4,24},{8,20},{12,16},{16,12},{20,8},{24,4},{28,0},{1,29},{... | collective-permute-start | bytes 110600 | tf_op jit(solution)/shard_map/ppermute | solution.py:234
  33.2 7.1 %collective-permute-start.12 = (bf16[3,48,128]{2,1,0:T(8,128)(2,1)S(1)}, bf16[3,48,128]{2,1,0:T(8,128)(2,1)S(1)}, u32[]{:S(2)}, u32[]{:S(2)}) collective-permute-start(bf16[3,48,128]{2,1,0:T(8,128)(2,1)S(1)} %get-tuple-element.41), channel_id=1, source_target_pairs={{0,16},{4,20},{8,24},{12,28},{16,0},{20,4},{24,8},{28,12},{1,17},{... | collective-permute-start | bytes 110600 | tf_op jit(solution)/shard_map/ppermute | solution.py:234
  35.2 5.8 %collective-permute-start.13 = (bf16[3,48,128]{2,1,0:T(8,128)(2,1)S(1)}, bf16[3,48,128]{2,1,0:T(8,128)(2,1)S(1)}, u32[]{:S(2)}, u32[]{:S(2)}) collective-permute-start(bf16[3,48,128]{2,1,0:T(8,128)(2,1)S(1)} %get-tuple-element.42), channel_id=1, source_target_pairs={{0,20},{4,16},{8,28},{12,24},{16,4},{20,0},{24,12},{28,8},{1,21},{... | collective-permute-start | bytes 110600 | tf_op jit(solution)/shard_map/ppermute | solution.py:234
  36.7 4.3 %collective-permute-start.14 = (bf16[3,48,128]{2,1,0:T(8,128)(2,1)S(1)}, bf16[3,48,128]{2,1,0:T(8,128)(2,1)S(1)}, u32[]{:S(2)}, u32[]{:S(2)}) collective-permute-start(bf16[3,48,128]{2,1,0:T(8,128)(2,1)S(1)} %get-tuple-element.43), channel_id=1, source_target_pairs={{0,8},{4,12},{8,0},{12,4},{16,24},{20,28},{24,16},{28,20},{1,9},{5... | collective-permute-start | bytes 110600 | tf_op jit(solution)/shard_map/ppermute | solution.py:234
  37.7 4.9 %collective-permute-start.15 = (bf16[3,48,128]{2,1,0:T(8,128)(2,1)S(1)}, bf16[3,48,128]{2,1,0:T(8,128)(2,1)S(1)}, u32[]{:S(2)}, u32[]{:S(2)}) collective-permute-start(bf16[3,48,128]{2,1,0:T(8,128)(2,1)S(1)} %get-tuple-element.44), channel_id=1, source_target_pairs={{0,12},{4,8},{8,4},{12,0},{16,28},{20,24},{24,20},{28,16},{1,13},{... | collective-permute-start | bytes 110600 | tf_op jit(solution)/shard_map/ppermute | solution.py:234
  39.0 4.0 %collective-permute-start.16 = (bf16[3,48,128]{2,1,0:T(8,128)(2,1)S(1)}, bf16[3,48,128]{2,1,0:T(8,128)(2,1)S(1)}, u32[]{:S(2)}, u32[]{:S(2)}) collective-permute-start(bf16[3,48,128]{2,1,0:T(8,128)(2,1)S(1)} %get-tuple-element.45), channel_id=1, source_target_pairs={{0,4},{4,0},{8,12},{12,8},{16,20},{20,16},{24,28},{28,24},{1,5},{5... | collective-permute-start | bytes 110600 | tf_op jit(solution)/shard_map/ppermute | solution.py:234
  43.0 1.7 %collective-permute-start.17 = (bf16[2,384,128]{2,1,0:T(8,128)(2,1)S(1)}, bf16[2,384,128]{2,1,0:T(8,128)(2,1)S(1)}, u32[]{:S(2)}, u32[]{:S(2)}) collective-permute-start(bf16[2,384,128]{2,1,0:T(8,128)(2,1)S(1)} %gather.1), channel_id=1, source_target_pairs={{0,1},{1,0},{2,3},{3,2},{4,5},{5,4},{6,7},{7,6},{8,9},{9,8},{10,11... | collective-permute-start | bytes 589832 | tf_op jit(solution)/shard_map/ppermute | solution.py:231

commit v4 on v3

--- a/solution.py
+++ b/solution.py
@@ -140,16 +140,20 @@
         bias_ref[step * ROWS : (step + 1) * ROWS, :] = jnp.where(kept, jnp.float32(0.0), jnp.float32(NEGATIVE))
 
 
-def temporal_kernel(sizes, bias_ref, *rest):
+def temporal_kernel(sizes, wanted, bias_ref, *rest):
     slots, ranks, share = sizes
     in_refs, out_refs = rest[:ranks], rest[ranks:]
+    bias = jnp.concatenate([bias_ref[at * ROWS : (at + 1) * ROWS, :] for at in wanted], axis=0)
     for slot in range(slots):
         groups = [pl.ds(start, ROWS) for start in range(0, share, ROWS)]
         triples = [
-            [jnp.concatenate([ref[slot, part, rows, :] for ref in in_refs], axis=0) for part in range(3)]
+            [
+                jnp.concatenate([ref[slot, part, rows, :] for ref in refs], axis=0)
+                for part, refs in enumerate(([in_refs[at] for at in wanted], in_refs, in_refs))
+            ]
             for rows in groups
         ]
-        for rows, blended in zip(groups, attend(triples, bias_ref[...])):
+        for rows, blended in zip(groups, attend(triples, bias)):
             for at, out_ref in enumerate(out_refs):
                 out_ref[slot, rows, :] = blended[at * ROWS : (at + 1) * ROWS]
 
@@ -263,15 +267,18 @@
         cost_estimate=cost,
         name="spatial",
     )(head_class, frame_mask, q, k, v)
-    blended = pl.pallas_call(
-        functools.partial(temporal_kernel, (slots, ranks, share)),
-        out_shape=[jax.ShapeDtypeStruct((slots, share, width), q.dtype)] * ranks,
-        in_specs=[vmem] * (1 + ranks),
-        out_specs=[vmem] * ranks,
-        compiler_params=params,
-        name="temporal",
-    )(bias, *arrived)
-    by_step = dict(zip(steps, blended))
+    by_step = {}
+    for name, far in (("temporal_far", True), ("temporal_near", False)):
+        wanted = [at for at, step in enumerate(steps) if (step >= ranks // 2) == far]
+        blended = pl.pallas_call(
+            functools.partial(temporal_kernel, (slots, ranks, share), wanted),
+            out_shape=[jax.ShapeDtypeStruct((slots, share, width), q.dtype)] * len(wanted),
+            in_specs=[vmem] * (1 + ranks),
+            out_specs=[vmem] * len(wanted),
+            compiler_params=params,
+            name=name,
+        )(bias, *arrived)
+        by_step.update((steps[at], array) for at, array in zip(wanted, blended))
     back = [by_step[0]] + [send(by_step[step], step) for step in back_distances(ranks)[1:]]
     returned = swap(
         pl.pallas_call(

time: 46.1 us -> 47.1 us (1.022)
  Pallas kernels: 7.86 us -> 8.74 us
    pallas_call x1 -> x2, Pallas kernels: 0.94 us -> 1.82 us  [per_device(): pl.pallas_call(functools.partial(temporal_kernel, (slots, ranks, share),...]
  transfers between devices with their start and end apart: 18 -> 18, of which waited for: 6 -> 6; matrix products, arithmetic and copies ran while one was open for 0% -> 0% of each run, Pallas kernels for 11% -> 13%
where the time goes in v4:
time: 47.1 us; the launch traced here: 46.9 us
  starting transfers between devices  26 us (55%)
  waiting for transfers between devices  12 us (25%)
  Pallas kernels  8.74 us (19%)
    ppermute x14, starting transfers between devices, send(): lax.ppermute(array, 'tm', [(rank, rank ^ step) for rank in range(ranks)])  24.9 us
    ppermute x14, waiting for transfers between devices, send(): lax.ppermute(array, 'tm', [(rank, rank ^ step) for rank in range(ranks)])  11.3 us
    pallas_call x1, Pallas kernels, per_device(): pl.pallas_call(load_kernel, out_shape=[whole] * 3, in_specs=[smem] + [hbm...  2.21 us
    pallas_call x2, Pallas kernels, per_device(): pl.pallas_call(functools.partial(temporal_kernel, (slots, ranks, share),...  1.82 us
    pallas_call x1, Pallas kernels, per_device(): pl.pallas_call(functools.partial(own_kernel, (group_heads, most, least, r...  1.58 us
    pallas_call x1, Pallas kernels, per_device(): pl.pallas_call(functools.partial(merge_kernel, (group_heads, most, least)...  1.26 us
    pallas_call x1, Pallas kernels, per_device(): pl.pallas_call(functools.partial(spatial_kernel, (group_heads, ranks, blo...  1.2 us
    ppermute x4, starting transfers between devices, swap(): return lax.ppermute(array, 'head', pairs)  1.03 us
  transfers between devices with their start and end apart: 18, of which 6 were waited for; matrix products, arithmetic and copies ran while one was open for 0% of the time, Pallas kernels for 13%

profile of v4, /device:TPU:0, one launch (start us, length us, event | category | flops | bytes accessed | tf_op | source)
XLA Modules:
  0.0 46.9 jit_solution(7658796322854371360)
XLA Ops:
  0.0 0.5 collective-permute-start
  0.5 0.1 collective-permute-start.1
  0.5 0.4 collective-permute-start.2
  1.0 0.1 copy-done
  1.1 2.2 %load.1 = (bf16[6,384,128]{2,1,0:T(8,128)(2,1)S(1)}, bf16[6,384,128]{2,1,0:T(8,128)(2,1)S(1)}, bf16[6,384,128]{2,1,0:T(8,128)(2,1)S(1)}) custom-call(s32[24]{0:T(128)S(1)} %copy-done, bf16[6,384,128]{2,1,0:T(8,128)(2,1)} %bitcast.13, bf16[6,384,128]{2,1,0:T(8,128)(2,1)} %bitcast.15, bf16[6,384,128]{2,1,0:T(8,128)(2,1)} %bitcast.17), custom_call_target="tpu_custom_call" | custom-call | tf_op jit(solution)/shard_map/load/pallas_call | solution.py:241
  3.3 0.0 collective-permute-done.refs_3_
  3.3 0.6 %collective-permute-done.2.refs_5_ = bf16[6,384,128]{2,1,0:T(8,128)(2,1)S(1)} collective-permute-done((bf16[6,384,128]{2,1,0:T(8,128)(2,1)}, bf16[6,384,128]{2,1,0:T(8,128)(2,1)S(1)}, u32[]{:S(2)}, u32[]{:S(2)}) %collective-permute-start.2) | collective-permute-done | bytes 589856 | tf_op jit(solution)/shard_map/ppermute | solution.py:235
  4.0 0.6 %pack.1 = (bf16[3,3,48,128]{3,2,1,0:T(8,128)(2,1)S(1)}, bf16[3,3,48,128]{3,2,1,0:T(8,128)(2,1)S(1)}, bf16[3,3,48,128]{3,2,1,0:T(8,128)(2,1)S(1)}, bf16[3,3,48,12...) custom-call(s32[24]{0:T(128)S(1)} %copy-done, ...), custom_call_target="tpu_custom_call" | custom-call | tf_op jit(solution)/shard_map/pack/pallas_call | solution.py:250
  4.6 4.0 %collective-permute-start.3 = (bf16[3,3,48,128]{3,2,1,0:T(8,128)(2,1)S(1)}, bf16[3,3,48,128]{3,2,1,0:T(8,128)(2,1)S(1)}, u32[]{:S(2)}, u32[]{:S(2)}) collective-permute-start(bf16[3,3,48,128]{3,2,1,0:T(8,128)(2,1)S(1)} %get-tuple-element.31), channel_id=1, source_target_pairs={{0,16},{4,20},{8,24},{12,28},{16,0},{20,4},{24,8},{28,12},{1,17},{... | collective-permute-start | bytes 331784 | tf_op jit(solution)/shard_map/ppermute | solution.py:238
  8.7 1.6 %collective-permute-start.4 = (bf16[3,3,48,128]{3,2,1,0:T(8,128)(2,1)S(1)}, bf16[3,3,48,128]{3,2,1,0:T(8,128)(2,1)S(1)}, u32[]{:S(2)}, u32[]{:S(2)}) collective-permute-start(bf16[3,3,48,128]{3,2,1,0:T(8,128)(2,1)S(1)} %get-tuple-element.32), channel_id=1, source_target_pairs={{0,8},{4,12},{8,0},{12,4},{16,24},{20,28},{24,16},{28,20},{1,9},{5... | collective-permute-start | bytes 331784 | tf_op jit(solution)/shard_map/ppermute | solution.py:238
  10.2 1.9 %collective-permute-start.6 = (bf16[3,3,48,128]{3,2,1,0:T(8,128)(2,1)S(1)}, bf16[3,3,48,128]{3,2,1,0:T(8,128)(2,1)S(1)}, u32[]{:S(2)}, u32[]{:S(2)}) collective-permute-start(bf16[3,3,48,128]{3,2,1,0:T(8,128)(2,1)S(1)} %get-tuple-element.34), channel_id=1, source_target_pairs={{0,12},{4,8},{8,4},{12,0},{16,28},{20,24},{24,20},{28,16},{1,13},{... | collective-permute-start | bytes 331784 | tf_op jit(solution)/shard_map/ppermute | solution.py:238
  12.1 0.5 %collective-permute-start.7 = (bf16[3,3,48,128]{3,2,1,0:T(8,128)(2,1)S(1)}, bf16[3,3,48,128]{3,2,1,0:T(8,128)(2,1)S(1)}, u32[]{:S(2)}, u32[]{:S(2)}) collective-permute-start(bf16[3,3,48,128]{3,2,1,0:T(8,128)(2,1)S(1)} %get-tuple-element.35), channel_id=1, source_target_pairs={{0,4},{4,0},{8,12},{12,8},{16,20},{20,16},{24,28},{28,24},{1,5},{5... | collective-permute-start | bytes 331784 | tf_op jit(solution)/shard_map/ppermute | solution.py:238
  12.6 2.4 %collective-permute-done.3.rest_1_ = bf16[3,3,48,128]{3,2,1,0:T(8,128)(2,1)S(1)} collective-permute-done((bf16[3,3,48,128]{3,2,1,0:T(8,128)(2,1)S(1)}, bf16[3,3,48,128]{3,2,1,0:T(8,128)(2,1)S(1)}, u32[]{:S(2)}, u32[]{:S(2)}) %collective-permute-start.3) | collective-permute-done | bytes 110624 | tf_op jit(solution)/shard_map/ppermute | solution.py:238
  15.0 2.0 %collective-permute-start.8 = (bf16[3,3,48,128]{3,2,1,0:T(8,128)(2,1)S(1)}, bf16[3,3,48,128]{3,2,1,0:T(8,128)(2,1)S(1)}, u32[]{:S(2)}, u32[]{:S(2)}) collective-permute-start(bf16[3,3,48,128]{3,2,1,0:T(8,128)(2,1)S(1)} %get-tuple-element.36), channel_id=1, source_target_pairs={{0,20},{4,16},{8,28},{12,24},{16,4},{20,0},{24,12},{28,8},{1,21},{... | collective-permute-start | bytes 331784 | tf_op jit(solution)/shard_map/ppermute | solution.py:238
  17.1 3.7 %collective-permute-start.9 = (bf16[3,3,48,128]{3,2,1,0:T(8,128)(2,1)S(1)}, bf16[3,3,48,128]{3,2,1,0:T(8,128)(2,1)S(1)}, u32[]{:S(2)}, u32[]{:S(2)}) collective-permute-start(bf16[3,3,48,128]{3,2,1,0:T(8,128)(2,1)S(1)} %get-tuple-element.37), channel_id=1, source_target_pairs={{0,28},{4,24},{8,20},{12,16},{16,12},{20,8},{24,4},{28,0},{1,29},{... | collective-permute-start | bytes 331784 | tf_op jit(solution)/shard_map/ppermute | solution.py:238
  20.7 1.2 %spatial.1 = (bf16[6,384,128]{2,1,0:T(8,128)(2,1)S(1)}, f32[128,128]{1,0:T(8,128)S(1)}) custom-call(s32[24]{0:T(128)S(1)} %copy-done, s32[4,4]{1,0:T(4,128)S(1)} %copy-done.1, bf16[6,384,128]{2,1,0:T(8,128)(2,1)S(1)} %get-tuple-element.26.q_ref.refs_0_, bf16[6,384,128]{2,1,0:T(8,128)(2,1)S(1)} %get-tuple-element.27.k_ref.refs_1_, ...), custom_call_target="tpu_custom_call" | custom-call | flops 377487360 | bytes 2359296 | tf_op jit(solution)/shard_map/spatial/pallas_call | solution.py:260
  22.0 6.1 %collective-permute-done.8.rest_6_ = bf16[3,3,48,128]{3,2,1,0:T(8,128)(2,1)S(1)} collective-permute-done((bf16[3,3,48,128]{3,2,1,0:T(8,128)(2,1)S(1)}, bf16[3,3,48,128]{3,2,1,0:T(8,128)(2,1)S(1)}, u32[]{:S(2)}, u32[]{:S(2)}) %collective-permute-start.8) | collective-permute-done | bytes 110624 | tf_op jit(solution)/shard_map/ppermute | solution.py:238
  28.0 0.9 %temporal_far.1 = (bf16[3,48,128]{2,1,0:T(8,128)(2,1)S(1)}, bf16[3,48,128]{2,1,0:T(8,128)(2,1)S(1)}, bf16[3,48,128]{2,1,0:T(8,128)(2,1)S(1)}, bf16[3,48,128]{2,1,0:T(8,128)(2,1)S(1)}) custom-call(f32[128,128]{1,0:T(8,128)S(1)} %get-tuple-element.29.bias_ref, bf16[3,3,48,128]{3,2,1,0:T(8,128)(2,1)S(1)} %get-tuple-element.30.rest_0_, ...), custom_call_target="tpu_custom_call" | custom-call | tf_op jit(solution)/shard_map/temporal_far/pallas_call | solution.py:273
  29.0 2.9 %collective-permute-start.10 = (bf16[3,48,128]{2,1,0:T(8,128)(2,1)S(1)}, bf16[3,48,128]{2,1,0:T(8,128)(2,1)S(1)}, u32[]{:S(2)}, u32[]{:S(2)}) collective-permute-start(bf16[3,48,128]{2,1,0:T(8,128)(2,1)S(1)} %get-tuple-element.39), channel_id=1, source_target_pairs={{0,24},{4,28},{8,16},{12,20},{16,8},{20,12},{24,0},{28,4},{1,25},{... | collective-permute-start | bytes 110600 | tf_op jit(solution)/shard_map/ppermute | solution.py:238
  31.8 1.3 %collective-permute-start.11 = (bf16[3,48,128]{2,1,0:T(8,128)(2,1)S(1)}, bf16[3,48,128]{2,1,0:T(8,128)(2,1)S(1)}, u32[]{:S(2)}, u32[]{:S(2)}) collective-permute-start(bf16[3,48,128]{2,1,0:T(8,128)(2,1)S(1)} %get-tuple-element.40), channel_id=1, source_target_pairs={{0,28},{4,24},{8,20},{12,16},{16,12},{20,8},{24,4},{28,0},{1,29},{... | collective-permute-start | bytes 110600 | tf_op jit(solution)/shard_map/ppermute | solution.py:238
  33.1 2.1 %collective-permute-start.12 = (bf16[3,48,128]{2,1,0:T(8,128)(2,1)S(1)}, bf16[3,48,128]{2,1,0:T(8,128)(2,1)S(1)}, u32[]{:S(2)}, u32[]{:S(2)}) collective-permute-start(bf16[3,48,128]{2,1,0:T(8,128)(2,1)S(1)} %get-tuple-element.41), channel_id=1, source_target_pairs={{0,16},{4,20},{8,24},{12,28},{16,0},{20,4},{24,8},{28,12},{1,17},{... | collective-permute-start | bytes 110600 | tf_op jit(solution)/shard_map/ppermute | solution.py:238
  35.2 1.5 %collective-permute-start.13 = (bf16[3,48,128]{2,1,0:T(8,128)(2,1)S(1)}, bf16[3,48,128]{2,1,0:T(8,128)(2,1)S(1)}, u32[]{:S(2)}, u32[]{:S(2)}) collective-permute-start(bf16[3,48,128]{2,1,0:T(8,128)(2,1)S(1)} %get-tuple-element.42), channel_id=1, source_target_pairs={{0,20},{4,16},{8,28},{12,24},{16,4},{20,0},{24,12},{28,8},{1,21},{... | collective-permute-start | bytes 110600 | tf_op jit(solution)/shard_map/ppermute | solution.py:238
  36.7 0.9 %temporal_near.1 = (bf16[3,48,128]{2,1,0:T(8,128)(2,1)S(1)}, bf16[3,48,128]{2,1,0:T(8,128)(2,1)S(1)}, bf16[3,48,128]{2,1,0:T(8,128)(2,1)S(1)}, bf16[3,48,128]{2,1,0:T(8,128)(2,1)S(1)}) custom-call(f32[128,128]{1,0:T(8,128)S(1)} %get-tuple-element.29.bias_ref, bf16[3,3,48,128]{3,2,1,0:T(8,128)(2,1)S(1)} %get-tuple-element.30.rest_0_, ...), custom_call_target="tpu_custom_call" | custom-call | tf_op jit(solution)/shard_map/temporal_near/pallas_call | solution.py:273
  37.6 1.1 %collective-permute-start.14 = (bf16[3,48,128]{2,1,0:T(8,128)(2,1)S(1)}, bf16[3,48,128]{2,1,0:T(8,128)(2,1)S(1)}, u32[]{:S(2)}, u32[]{:S(2)}) collective-permute-start(bf16[3,48,128]{2,1,0:T(8,128)(2,1)S(1)} %get-tuple-element.43), channel_id=1, source_target_pairs={{0,8},{4,12},{8,0},{12,4},{16,24},{20,28},{24,16},{28,20},{1,9},{5... | collective-permute-start | bytes 110600 | tf_op jit(solution)/shard_map/ppermute | solution.py:238
  38.7 1.3 %collective-permute-start.15 = (bf16[3,48,128]{2,1,0:T(8,128)(2,1)S(1)}, bf16[3,48,128]{2,1,0:T(8,128)(2,1)S(1)}, u32[]{:S(2)}, u32[]{:S(2)}) collective-permute-start(bf16[3,48,128]{2,1,0:T(8,128)(2,1)S(1)} %get-tuple-element.44), channel_id=1, source_target_pairs={{0,12},{4,8},{8,4},{12,0},{16,28},{20,24},{24,20},{28,16},{1,13},{... | collective-permute-start | bytes 110600 | tf_op jit(solution)/shard_map/ppermute | solution.py:238
  40.0 1.2 %collective-permute-start.16 = (bf16[3,48,128]{2,1,0:T(8,128)(2,1)S(1)}, bf16[3,48,128]{2,1,0:T(8,128)(2,1)S(1)}, u32[]{:S(2)}, u32[]{:S(2)}) collective-permute-start(bf16[3,48,128]{2,1,0:T(8,128)(2,1)S(1)} %get-tuple-element.45), channel_id=1, source_target_pairs={{0,4},{4,0},{8,12},{12,8},{16,20},{20,16},{24,28},{28,24},{1,5},{5... | collective-permute-start | bytes 110600 | tf_op jit(solution)/shard_map/ppermute | solution.py:238
  41.2 0.5 collective-permute-done.14.refs_5_.rest_5_
  41.6 1.9 %collective-permute-done.15.refs_6_.rest_6_ = bf16[3,48,128]{2,1,0:T(8,128)(2,1)S(1)} collective-permute-done((bf16[3,48,128]{2,1,0:T(8,128)(2,1)S(1)}, bf16[3,48,128]{2,1,0:T(8,128)(2,1)S(1)}, u32[]{:S(2)}, u32[]{:S(2)}) %collective-permute-start.15) | collective-permute-done | bytes 36896 | tf_op jit(solution)/shard_map/ppermute | solution.py:238
  43.6 0.4 collective-permute-done.16.refs_7_.rest_7_
  44.0 0.1 collective-permute-start.17
  44.1 1.6 %own.1.whole_ref = bf16[6,384,128]{2,1,0:T(8,128)(2,1)} custom-call(s32[24]{0:T(128)S(1)} %copy-done, bf16[6,384,128]{2,1,0:T(8,128)(2,1)S(1)} %get-tuple-element.46.spatial_ref, bf16[3,48,128]{2,1,0:T(8,128)(2,1)S(1)} %get-tuple-element.38.refs_0_.rest_0_, bf16[3,48,128]{2,1,0:T(8,128)(2,1)S(1)} %collective-permute-done.10.refs_1_.rest_1_, ...), custom_call_target="tpu_custom_call" | custom-call | tf_op jit(solution)/shard_map/own/pallas_call | solution.py:293
  45.7 1.3 %merge.1 = bf16[6,384,128]{2,1,0:T(8,128)(2,1)} custom-call(s32[24]{0:T(128)S(1)} %copy-done, bf16[2,384,128]{2,1,0:T(8,128)(2,1)S(1)} %collective-permute-done.17.given_ref, bf16[6,384,128]{2,1,0:T(8,128)(2,1)} %own.1.whole_ref), custom_call_target="tpu_custom_call", output_to_operand_aliasing={{}: (2, {})} | custom-call | tf_op jit(solution)/shard_map/merge/pallas_call | solution.py:302
  (16 shorter events, 0.1 us)
Async XLA Ops:
  0.0 3.3 %collective-permute-start = (bf16[6,384,128]{2,1,0:T(8,128)(2,1)}, bf16[6,384,128]{2,1,0:T(8,128)(2,1)S(1)}, u32[]{:S(2)}, u32[]{:S(2)}) collective-permute-start(bf16[6,384,128]{2,1,0:T(8,128)(2,1)} %bitcast.12), channel_id=1, source_target_pairs={{0,1},{1,0},{2,3},{3,2},{4,5},{5,4},{6,7},{7,6},{8,9},{9,8},{10,11... | collective-permute-start | bytes 1769480 | tf_op jit(solution)/shard_map/ppermute | solution.py:235
  0.5 0.7 %copy-start = (s32[24]{0:T(128)S(1)}, s32[24]{0:T(128)}, u32[]{:S(2)}) copy-start(s32[24]{0:T(128)} %class_ref.9) | copy-start | bytes 292
  0.5 2.9 %collective-permute-start.1 = (bf16[6,384,128]{2,1,0:T(8,128)(2,1)}, bf16[6,384,128]{2,1,0:T(8,128)(2,1)S(1)}, u32[]{:S(2)}, u32[]{:S(2)}) collective-permute-start(bf16[6,384,128]{2,1,0:T(8,128)(2,1)} %bitcast.14), channel_id=1, source_target_pairs={{0,1},{1,0},{2,3},{3,2},{4,5},{5,4},{6,7},{7,6},{8,9},{9,8},{10,11... | collective-permute-start | bytes 1769480 | tf_op jit(solution)/shard_map/ppermute | solution.py:235
  0.5 3.5 %collective-permute-start.2 = (bf16[6,384,128]{2,1,0:T(8,128)(2,1)}, bf16[6,384,128]{2,1,0:T(8,128)(2,1)S(1)}, u32[]{:S(2)}, u32[]{:S(2)}) collective-permute-start(bf16[6,384,128]{2,1,0:T(8,128)(2,1)} %bitcast.16), channel_id=1, source_target_pairs={{0,1},{1,0},{2,3},{3,2},{4,5},{5,4},{6,7},{7,6},{8,9},{9,8},{10,11... | collective-permute-start | bytes 1769480 | tf_op jit(solution)/shard_map/ppermute | solution.py:235
  4.6 10.4 %collective-permute-start.3 = (bf16[3,3,48,128]{3,2,1,0:T(8,128)(2,1)S(1)}, bf16[3,3,48,128]{3,2,1,0:T(8,128)(2,1)S(1)}, u32[]{:S(2)}, u32[]{:S(2)}) collective-permute-start(bf16[3,3,48,128]{3,2,1,0:T(8,128)(2,1)S(1)} %get-tuple-element.31), channel_id=1, source_target_pairs={{0,16},{4,20},{8,24},{12,28},{16,0},{20,4},{24,8},{28,12},{1,17},{... | collective-permute-start | bytes 331784 | tf_op jit(solution)/shard_map/ppermute | solution.py:238
  8.7 8.4 %collective-permute-start.4 = (bf16[3,3,48,128]{3,2,1,0:T(8,128)(2,1)S(1)}, bf16[3,3,48,128]{3,2,1,0:T(8,128)(2,1)S(1)}, u32[]{:S(2)}, u32[]{:S(2)}) collective-permute-start(bf16[3,3,48,128]{3,2,1,0:T(8,128)(2,1)S(1)} %get-tuple-element.32), channel_id=1, source_target_pairs={{0,8},{4,12},{8,0},{12,4},{16,24},{20,28},{24,16},{28,20},{1,9},{5... | collective-permute-start | bytes 331784 | tf_op jit(solution)/shard_map/ppermute | solution.py:238
  10.2 11.7 %collective-permute-start.5 = (bf16[3,3,48,128]{3,2,1,0:T(8,128)(2,1)S(1)}, bf16[3,3,48,128]{3,2,1,0:T(8,128)(2,1)S(1)}, u32[]{:S(2)}, u32[]{:S(2)}) collective-permute-start(bf16[3,3,48,128]{3,2,1,0:T(8,128)(2,1)S(1)} %get-tuple-element.33), channel_id=1, source_target_pairs={{0,24},{4,28},{8,16},{12,20},{16,8},{20,12},{24,0},{28,4},{1,25},{... | collective-permute-start | bytes 331784 | tf_op jit(solution)/shard_map/ppermute | solution.py:238
  10.2 11.7 %collective-permute-start.6 = (bf16[3,3,48,128]{3,2,1,0:T(8,128)(2,1)S(1)}, bf16[3,3,48,128]{3,2,1,0:T(8,128)(2,1)S(1)}, u32[]{:S(2)}, u32[]{:S(2)}) collective-permute-start(bf16[3,3,48,128]{3,2,1,0:T(8,128)(2,1)S(1)} %get-tuple-element.34), channel_id=1, source_target_pairs={{0,12},{4,8},{8,4},{12,0},{16,28},{20,24},{24,20},{28,16},{1,13},{... | collective-permute-start | bytes 331784 | tf_op jit(solution)/shard_map/ppermute | solution.py:238
  12.1 8.6 %copy-start.1 = (s32[4,4]{1,0:T(4,128)S(1)}, s32[4,4]{1,0:T(4,128)}, u32[]{:S(2)}) copy-start(s32[4,4]{1,0:T(4,128)} %mask_ref.1) | copy-start | bytes 196
  12.1 9.9 %collective-permute-start.7 = (bf16[3,3,48,128]{3,2,1,0:T(8,128)(2,1)S(1)}, bf16[3,3,48,128]{3,2,1,0:T(8,128)(2,1)S(1)}, u32[]{:S(2)}, u32[]{:S(2)}) collective-permute-start(bf16[3,3,48,128]{3,2,1,0:T(8,128)(2,1)S(1)} %get-tuple-element.35), channel_id=1, source_target_pairs={{0,4},{4,0},{8,12},{12,8},{16,20},{20,16},{24,28},{28,24},{1,5},{5... | collective-permute-start | bytes 331784 | tf_op jit(solution)/shard_map/ppermute | solution.py:238
  15.0 13.0 %collective-permute-start.8 = (bf16[3,3,48,128]{3,2,1,0:T(8,128)(2,1)S(1)}, bf16[3,3,48,128]{3,2,1,0:T(8,128)(2,1)S(1)}, u32[]{:S(2)}, u32[]{:S(2)}) collective-permute-start(bf16[3,3,48,128]{3,2,1,0:T(8,128)(2,1)S(1)} %get-tuple-element.36), channel_id=1, source_target_pairs={{0,20},{4,16},{8,28},{12,24},{16,4},{20,0},{24,12},{28,8},{1,21},{... | collective-permute-start | bytes 331784 | tf_op jit(solution)/shard_map/ppermute | solution.py:238
  17.1 11.0 %collective-permute-start.9 = (bf16[3,3,48,128]{3,2,1,0:T(8,128)(2,1)S(1)}, bf16[3,3,48,128]{3,2,1,0:T(8,128)(2,1)S(1)}, u32[]{:S(2)}, u32[]{:S(2)}) collective-permute-start(bf16[3,3,48,128]{3,2,1,0:T(8,128)(2,1)S(1)} %get-tuple-element.37), channel_id=1, source_target_pairs={{0,28},{4,24},{8,20},{12,16},{16,12},{20,8},{24,4},{28,0},{1,29},{... | collective-permute-start | bytes 331784 | tf_op jit(solution)/shard_map/ppermute | solution.py:238
  29.0 9.7 %collective-permute-start.10 = (bf16[3,48,128]{2,1,0:T(8,128)(2,1)S(1)}, bf16[3,48,128]{2,1,0:T(8,128)(2,1)S(1)}, u32[]{:S(2)}, u32[]{:S(2)}) collective-permute-start(bf16[3,48,128]{2,1,0:T(8,128)(2,1)S(1)} %get-tuple-element.39), channel_id=1, source_target_pairs={{0,24},{4,28},{8,16},{12,20},{16,8},{20,12},{24,0},{28,4},{1,25},{... | collective-permute-start | bytes 110600 | tf_op jit(solution)/shard_map/ppermute | solution.py:238
  31.8 8.1 %collective-permute-start.11 = (bf16[3,48,128]{2,1,0:T(8,128)(2,1)S(1)}, bf16[3,48,128]{2,1,0:T(8,128)(2,1)S(1)}, u32[]{:S(2)}, u32[]{:S(2)}) collective-permute-start(bf16[3,48,128]{2,1,0:T(8,128)(2,1)S(1)} %get-tuple-element.40), channel_id=1, source_target_pairs={{0,28},{4,24},{8,20},{12,16},{16,12},{20,8},{24,4},{28,0},{1,29},{... | collective-permute-start | bytes 110600 | tf_op jit(solution)/shard_map/ppermute | solution.py:238
  33.1 8.0 %collective-permute-start.12 = (bf16[3,48,128]{2,1,0:T(8,128)(2,1)S(1)}, bf16[3,48,128]{2,1,0:T(8,128)(2,1)S(1)}, u32[]{:S(2)}, u32[]{:S(2)}) collective-permute-start(bf16[3,48,128]{2,1,0:T(8,128)(2,1)S(1)} %get-tuple-element.41), channel_id=1, source_target_pairs={{0,16},{4,20},{8,24},{12,28},{16,0},{20,4},{24,8},{28,12},{1,17},{... | collective-permute-start | bytes 110600 | tf_op jit(solution)/shard_map/ppermute | solution.py:238
  35.2 6.0 %collective-permute-start.13 = (bf16[3,48,128]{2,1,0:T(8,128)(2,1)S(1)}, bf16[3,48,128]{2,1,0:T(8,128)(2,1)S(1)}, u32[]{:S(2)}, u32[]{:S(2)}) collective-permute-start(bf16[3,48,128]{2,1,0:T(8,128)(2,1)S(1)} %get-tuple-element.42), channel_id=1, source_target_pairs={{0,20},{4,16},{8,28},{12,24},{16,4},{20,0},{24,12},{28,8},{1,21},{... | collective-permute-start | bytes 110600 | tf_op jit(solution)/shard_map/ppermute | solution.py:238
  37.6 4.0 %collective-permute-start.14 = (bf16[3,48,128]{2,1,0:T(8,128)(2,1)S(1)}, bf16[3,48,128]{2,1,0:T(8,128)(2,1)S(1)}, u32[]{:S(2)}, u32[]{:S(2)}) collective-permute-start(bf16[3,48,128]{2,1,0:T(8,128)(2,1)S(1)} %get-tuple-element.43), channel_id=1, source_target_pairs={{0,8},{4,12},{8,0},{12,4},{16,24},{20,28},{24,16},{28,20},{1,9},{5... | collective-permute-start | bytes 110600 | tf_op jit(solution)/shard_map/ppermute | solution.py:238
  38.7 4.9 %collective-permute-start.15 = (bf16[3,48,128]{2,1,0:T(8,128)(2,1)S(1)}, bf16[3,48,128]{2,1,0:T(8,128)(2,1)S(1)}, u32[]{:S(2)}, u32[]{:S(2)}) collective-permute-start(bf16[3,48,128]{2,1,0:T(8,128)(2,1)S(1)} %get-tuple-element.44), channel_id=1, source_target_pairs={{0,12},{4,8},{8,4},{12,0},{16,28},{20,24},{24,20},{28,16},{1,13},{... | collective-permute-start | bytes 110600 | tf_op jit(solution)/shard_map/ppermute | solution.py:238
  40.0 4.0 %collective-permute-start.16 = (bf16[3,48,128]{2,1,0:T(8,128)(2,1)S(1)}, bf16[3,48,128]{2,1,0:T(8,128)(2,1)S(1)}, u32[]{:S(2)}, u32[]{:S(2)}) collective-permute-start(bf16[3,48,128]{2,1,0:T(8,128)(2,1)S(1)} %get-tuple-element.45), channel_id=1, source_target_pairs={{0,4},{4,0},{8,12},{12,8},{16,20},{20,16},{24,28},{28,24},{1,5},{5... | collective-permute-start | bytes 110600 | tf_op jit(solution)/shard_map/ppermute | solution.py:238
  44.0 1.7 %collective-permute-start.17 = (bf16[2,384,128]{2,1,0:T(8,128)(2,1)S(1)}, bf16[2,384,128]{2,1,0:T(8,128)(2,1)S(1)}, u32[]{:S(2)}, u32[]{:S(2)}) collective-permute-start(bf16[2,384,128]{2,1,0:T(8,128)(2,1)S(1)} %gather.1), channel_id=1, source_target_pairs={{0,1},{1,0},{2,3},{3,2},{4,5},{5,4},{6,7},{7,6},{8,9},{9,8},{10,11... | collective-permute-start | bytes 589832 | tf_op jit(solution)/shard_map/ppermute | solution.py:235

commit v5 on v3

--- a/solution.py
+++ b/solution.py
@@ -89,7 +89,7 @@
 def back_distances(ranks):
     far, near = list(range(ranks // 2, ranks)), list(range(1, ranks // 2))
     cut = len(far) // 2
-    return [0, *far[cut:], *far[:cut], *near[1:], *near[:1]]
+    return [0, *far[cut:], *far[:cut], *near[::-1]]
 
 
 def block_rows(rank, share):

time: 46.1 us -> 46.1 us (level); the launches traced: 46 us -> 45.3 us
  waiting for transfers between devices: 12 us -> 10.1 us
  Pallas kernels: 7.86 us -> 9.25 us
    pallas_call x1, Pallas kernels: 1.2 us -> 3.17 us  [per_device(): pl.pallas_call(functools.partial(spatial_kernel, (group_heads, ranks, blo...]
    ppermute x14, waiting for transfers between devices: 11.3 us -> 9.42 us  [send(): lax.ppermute(array, 'tm', [(rank, rank ^ step) for rank in range(ranks)])]
    pallas_call x1, Pallas kernels: 1.26 us -> 0.59 us  [per_device(): pl.pallas_call(functools.partial(merge_kernel, (group_heads, most, least)...]
  transfers between devices with their start and end apart: 18 -> 18, of which waited for: 6 -> 7; matrix products, arithmetic and copies ran while one was open for 0% -> 0% of each run, Pallas kernels for 11% -> 16%
where the time goes in v5:
time: 46.1 us; the launch traced here: 45.3 us
  starting transfers between devices  25.8 us (56%)
  waiting for transfers between devices  10.1 us (22%)
  Pallas kernels  9.25 us (20%)
    ppermute x14, starting transfers between devices, send(): lax.ppermute(array, 'tm', [(rank, rank ^ step) for rank in range(ranks)])  24.7 us
    ppermute x14, waiting for transfers between devices, send(): lax.ppermute(array, 'tm', [(rank, rank ^ step) for rank in range(ranks)])  9.42 us
    pallas_call x1, Pallas kernels, per_device(): pl.pallas_call(functools.partial(spatial_kernel, (group_heads, ranks, blo...  3.17 us
    pallas_call x1, Pallas kernels, per_device(): pl.pallas_call(load_kernel, out_shape=[whole] * 3, in_specs=[smem] + [hbm...  2.21 us
    pallas_call x1, Pallas kernels, per_device(): pl.pallas_call(functools.partial(own_kernel, (group_heads, most, least, r...  1.65 us
    ppermute x4, starting transfers between devices, swap(): return lax.ppermute(array, 'head', pairs)  1.03 us
    pallas_call x1, Pallas kernels, per_device(): pl.pallas_call(functools.partial(temporal_kernel, (slots, ranks, share)),...  0.94 us
  transfers between devices with their start and end apart: 18, of which 7 were waited for; matrix products, arithmetic and copies ran while one was open for 0% of the time, Pallas kernels for 16%

profile of v5, /device:TPU:0, one launch (start us, length us, event | category | flops | bytes accessed | tf_op | source)
XLA Modules:
  0.0 45.3 jit_solution(5776056730911160148)
XLA Ops:
  0.0 0.5 collective-permute-start
  0.5 0.1 collective-permute-start.1
  0.5 0.4 collective-permute-start.2
  1.0 0.1 copy-done
  1.1 2.2 %load.1 = (bf16[6,384,128]{2,1,0:T(8,128)(2,1)S(1)}, bf16[6,384,128]{2,1,0:T(8,128)(2,1)S(1)}, bf16[6,384,128]{2,1,0:T(8,128)(2,1)S(1)}) custom-call(s32[24]{0:T(128)S(1)} %copy-done, bf16[6,384,128]{2,1,0:T(8,128)(2,1)} %bitcast.13, bf16[6,384,128]{2,1,0:T(8,128)(2,1)} %bitcast.15, bf16[6,384,128]{2,1,0:T(8,128)(2,1)} %bitcast.17), custom_call_target="tpu_custom_call" | custom-call | tf_op jit(solution)/shard_map/load/pallas_call | solution.py:237
  3.3 0.0 collective-permute-done.refs_3_
  3.3 0.6 %collective-permute-done.2.refs_5_ = bf16[6,384,128]{2,1,0:T(8,128)(2,1)S(1)} collective-permute-done((bf16[6,384,128]{2,1,0:T(8,128)(2,1)}, bf16[6,384,128]{2,1,0:T(8,128)(2,1)S(1)}, u32[]{:S(2)}, u32[]{:S(2)}) %collective-permute-start.2) | collective-permute-done | bytes 589856 | tf_op jit(solution)/shard_map/ppermute | solution.py:231
  4.0 0.7 %pack.1 = (bf16[3,3,48,128]{3,2,1,0:T(8,128)(2,1)S(1)}, bf16[3,3,48,128]{3,2,1,0:T(8,128)(2,1)S(1)}, bf16[3,3,48,128]{3,2,1,0:T(8,128)(2,1)S(1)}, bf16[3,3,48,12...) custom-call(s32[24]{0:T(128)S(1)} %copy-done, ...), custom_call_target="tpu_custom_call" | custom-call | tf_op jit(solution)/shard_map/pack/pallas_call | solution.py:246
  4.7 4.0 %collective-permute-start.3 = (bf16[3,3,48,128]{3,2,1,0:T(8,128)(2,1)S(1)}, bf16[3,3,48,128]{3,2,1,0:T(8,128)(2,1)S(1)}, u32[]{:S(2)}, u32[]{:S(2)}) collective-permute-start(bf16[3,3,48,128]{3,2,1,0:T(8,128)(2,1)S(1)} %get-tuple-element.31), channel_id=1, source_target_pairs={{0,16},{4,20},{8,24},{12,28},{16,0},{20,4},{24,8},{28,12},{1,17},{... | collective-permute-start | bytes 331784 | tf_op jit(solution)/shard_map/ppermute | solution.py:234
  8.7 1.6 %collective-permute-start.4 = (bf16[3,3,48,128]{3,2,1,0:T(8,128)(2,1)S(1)}, bf16[3,3,48,128]{3,2,1,0:T(8,128)(2,1)S(1)}, u32[]{:S(2)}, u32[]{:S(2)}) collective-permute-start(bf16[3,3,48,128]{3,2,1,0:T(8,128)(2,1)S(1)} %get-tuple-element.32), channel_id=1, source_target_pairs={{0,8},{4,12},{8,0},{12,4},{16,24},{20,28},{24,16},{28,20},{1,9},{5... | collective-permute-start | bytes 331784 | tf_op jit(solution)/shard_map/ppermute | solution.py:234
  10.3 1.9 %collective-permute-start.6 = (bf16[3,3,48,128]{3,2,1,0:T(8,128)(2,1)S(1)}, bf16[3,3,48,128]{3,2,1,0:T(8,128)(2,1)S(1)}, u32[]{:S(2)}, u32[]{:S(2)}) collective-permute-start(bf16[3,3,48,128]{3,2,1,0:T(8,128)(2,1)S(1)} %get-tuple-element.34), channel_id=1, source_target_pairs={{0,12},{4,8},{8,4},{12,0},{16,28},{20,24},{24,20},{28,16},{1,13},{... | collective-permute-start | bytes 331784 | tf_op jit(solution)/shard_map/ppermute | solution.py:234
  12.1 0.5 %collective-permute-start.7 = (bf16[3,3,48,128]{3,2,1,0:T(8,128)(2,1)S(1)}, bf16[3,3,48,128]{3,2,1,0:T(8,128)(2,1)S(1)}, u32[]{:S(2)}, u32[]{:S(2)}) collective-permute-start(bf16[3,3,48,128]{3,2,1,0:T(8,128)(2,1)S(1)} %get-tuple-element.35), channel_id=1, source_target_pairs={{0,4},{4,0},{8,12},{12,8},{16,20},{20,16},{24,28},{28,24},{1,5},{5... | collective-permute-start | bytes 331784 | tf_op jit(solution)/shard_map/ppermute | solution.py:234
  12.6 2.5 %collective-permute-done.3.rest_1_ = bf16[3,3,48,128]{3,2,1,0:T(8,128)(2,1)S(1)} collective-permute-done((bf16[3,3,48,128]{3,2,1,0:T(8,128)(2,1)S(1)}, bf16[3,3,48,128]{3,2,1,0:T(8,128)(2,1)S(1)}, u32[]{:S(2)}, u32[]{:S(2)}) %collective-permute-start.3) | collective-permute-done | bytes 110624 | tf_op jit(solution)/shard_map/ppermute | solution.py:234
  15.1 2.0 %collective-permute-start.8 = (bf16[3,3,48,128]{3,2,1,0:T(8,128)(2,1)S(1)}, bf16[3,3,48,128]{3,2,1,0:T(8,128)(2,1)S(1)}, u32[]{:S(2)}, u32[]{:S(2)}) collective-permute-start(bf16[3,3,48,128]{3,2,1,0:T(8,128)(2,1)S(1)} %get-tuple-element.36), channel_id=1, source_target_pairs={{0,20},{4,16},{8,28},{12,24},{16,4},{20,0},{24,12},{28,8},{1,21},{... | collective-permute-start | bytes 331784 | tf_op jit(solution)/shard_map/ppermute | solution.py:234
  17.1 3.6 %collective-permute-start.9 = (bf16[3,3,48,128]{3,2,1,0:T(8,128)(2,1)S(1)}, bf16[3,3,48,128]{3,2,1,0:T(8,128)(2,1)S(1)}, u32[]{:S(2)}, u32[]{:S(2)}) collective-permute-start(bf16[3,3,48,128]{3,2,1,0:T(8,128)(2,1)S(1)} %get-tuple-element.37), channel_id=1, source_target_pairs={{0,28},{4,24},{8,20},{12,16},{16,12},{20,8},{24,4},{28,0},{1,29},{... | collective-permute-start | bytes 331784 | tf_op jit(solution)/shard_map/ppermute | solution.py:234
  20.7 3.2 %spatial.1 = (bf16[6,384,128]{2,1,0:T(8,128)(2,1)S(1)}, f32[128,128]{1,0:T(8,128)S(1)}) custom-call(s32[24]{0:T(128)S(1)} %copy-done, s32[4,4]{1,0:T(4,128)S(1)} %copy-done.1, bf16[6,384,128]{2,1,0:T(8,128)(2,1)S(1)} %get-tuple-element.26.q_ref.refs_0_, bf16[6,384,128]{2,1,0:T(8,128)(2,1)S(1)} %get-tuple-element.27.k_ref.refs_1_, ...), custom_call_target="tpu_custom_call" | custom-call | flops 377487360 | bytes 2359296 | tf_op jit(solution)/shard_map/spatial/pallas_call | solution.py:256
  23.9 4.2 %collective-permute-done.8.rest_6_ = bf16[3,3,48,128]{3,2,1,0:T(8,128)(2,1)S(1)} collective-permute-done((bf16[3,3,48,128]{3,2,1,0:T(8,128)(2,1)S(1)}, bf16[3,3,48,128]{3,2,1,0:T(8,128)(2,1)S(1)}, u32[]{:S(2)}, u32[]{:S(2)}) %collective-permute-start.8) | collective-permute-done | bytes 110624 | tf_op jit(solution)/shard_map/ppermute | solution.py:234
  28.1 0.9 %temporal.1 = (bf16[3,48,128]{2,1,0:T(8,128)(2,1)S(1)}, bf16[3,48,128]{2,1,0:T(8,128)(2,1)S(1)}, bf16[3,48,128]{2,1,0:T(8,128)(2,1)S(1)}, bf16[3,48,128]{2,1,0:T...) custom-call(f32[128,128]{1,0:T(8,128)S(1)} %get-tuple-element.29.bia, ...), custom_call_target="tpu_custom_call" | custom-call | tf_op jit(solution)/shard_map/temporal/pallas_call | solution.py:266
  29.0 2.9 %collective-permute-start.10 = (bf16[3,48,128]{2,1,0:T(8,128)(2,1)S(1)}, bf16[3,48,128]{2,1,0:T(8,128)(2,1)S(1)}, u32[]{:S(2)}, u32[]{:S(2)}) collective-permute-start(bf16[3,48,128]{2,1,0:T(8,128)(2,1)S(1)} %get-tuple-element.39), channel_id=1, source_target_pairs={{0,24},{4,28},{8,16},{12,20},{16,8},{20,12},{24,0},{28,4},{1,25},{... | collective-permute-start | bytes 110600 | tf_op jit(solution)/shard_map/ppermute | solution.py:234
  31.9 1.3 %collective-permute-start.11 = (bf16[3,48,128]{2,1,0:T(8,128)(2,1)S(1)}, bf16[3,48,128]{2,1,0:T(8,128)(2,1)S(1)}, u32[]{:S(2)}, u32[]{:S(2)}) collective-permute-start(bf16[3,48,128]{2,1,0:T(8,128)(2,1)S(1)} %get-tuple-element.40), channel_id=1, source_target_pairs={{0,28},{4,24},{8,20},{12,16},{16,12},{20,8},{24,4},{28,0},{1,29},{... | collective-permute-start | bytes 110600 | tf_op jit(solution)/shard_map/ppermute | solution.py:234
  33.1 2.1 %collective-permute-start.12 = (bf16[3,48,128]{2,1,0:T(8,128)(2,1)S(1)}, bf16[3,48,128]{2,1,0:T(8,128)(2,1)S(1)}, u32[]{:S(2)}, u32[]{:S(2)}) collective-permute-start(bf16[3,48,128]{2,1,0:T(8,128)(2,1)S(1)} %get-tuple-element.41), channel_id=1, source_target_pairs={{0,16},{4,20},{8,24},{12,28},{16,0},{20,4},{24,8},{28,12},{1,17},{... | collective-permute-start | bytes 110600 | tf_op jit(solution)/shard_map/ppermute | solution.py:234
  35.2 1.5 %collective-permute-start.13 = (bf16[3,48,128]{2,1,0:T(8,128)(2,1)S(1)}, bf16[3,48,128]{2,1,0:T(8,128)(2,1)S(1)}, u32[]{:S(2)}, u32[]{:S(2)}) collective-permute-start(bf16[3,48,128]{2,1,0:T(8,128)(2,1)S(1)} %get-tuple-element.42), channel_id=1, source_target_pairs={{0,20},{4,16},{8,28},{12,24},{16,4},{20,0},{24,12},{28,8},{1,21},{... | collective-permute-start | bytes 110600 | tf_op jit(solution)/shard_map/ppermute | solution.py:234
  36.7 0.9 %collective-permute-start.14 = (bf16[3,48,128]{2,1,0:T(8,128)(2,1)S(1)}, bf16[3,48,128]{2,1,0:T(8,128)(2,1)S(1)}, u32[]{:S(2)}, u32[]{:S(2)}) collective-permute-start(bf16[3,48,128]{2,1,0:T(8,128)(2,1)S(1)} %get-tuple-element.43), channel_id=1, source_target_pairs={{0,12},{4,8},{8,4},{12,0},{16,28},{20,24},{24,20},{28,16},{1,13},{... | collective-permute-start | bytes 110600 | tf_op jit(solution)/shard_map/ppermute | solution.py:234
  37.7 1.3 %collective-permute-start.15 = (bf16[3,48,128]{2,1,0:T(8,128)(2,1)S(1)}, bf16[3,48,128]{2,1,0:T(8,128)(2,1)S(1)}, u32[]{:S(2)}, u32[]{:S(2)}) collective-permute-start(bf16[3,48,128]{2,1,0:T(8,128)(2,1)S(1)} %get-tuple-element.44), channel_id=1, source_target_pairs={{0,8},{4,12},{8,0},{12,4},{16,24},{20,28},{24,16},{28,20},{1,9},{5... | collective-permute-start | bytes 110600 | tf_op jit(solution)/shard_map/ppermute | solution.py:234
  39.0 1.2 %collective-permute-start.16 = (bf16[3,48,128]{2,1,0:T(8,128)(2,1)S(1)}, bf16[3,48,128]{2,1,0:T(8,128)(2,1)S(1)}, u32[]{:S(2)}, u32[]{:S(2)}) collective-permute-start(bf16[3,48,128]{2,1,0:T(8,128)(2,1)S(1)} %get-tuple-element.45), channel_id=1, source_target_pairs={{0,4},{4,0},{8,12},{12,8},{16,20},{20,16},{24,28},{28,24},{1,5},{5... | collective-permute-start | bytes 110600 | tf_op jit(solution)/shard_map/ppermute | solution.py:234
  40.2 0.8 %collective-permute-done.13.refs_4_.rest_4_ = bf16[3,48,128]{2,1,0:T(8,128)(2,1)S(1)} collective-permute-done((bf16[3,48,128]{2,1,0:T(8,128)(2,1)S(1)}, bf16[3,48,128]{2,1,0:T(8,128)(2,1)S(1)}, u32[]{:S(2)}, u32[]{:S(2)}) %collective-permute-start.13) | collective-permute-done | bytes 36896 | tf_op jit(solution)/shard_map/ppermute | solution.py:234
  41.0 0.6 %collective-permute-done.14.refs_5_.rest_5_ = bf16[3,48,128]{2,1,0:T(8,128)(2,1)S(1)} collective-permute-done((bf16[3,48,128]{2,1,0:T(8,128)(2,1)S(1)}, bf16[3,48,128]{2,1,0:T(8,128)(2,1)S(1)}, u32[]{:S(2)}, u32[]{:S(2)}) %collective-permute-start.14) | collective-permute-done | bytes 36896 | tf_op jit(solution)/shard_map/ppermute | solution.py:234
  41.6 0.1 collective-permute-done.15.refs_6_.rest_6_
  41.7 1.2 %collective-permute-done.16.refs_7_.rest_7_ = bf16[3,48,128]{2,1,0:T(8,128)(2,1)S(1)} collective-permute-done((bf16[3,48,128]{2,1,0:T(8,128)(2,1)S(1)}, bf16[3,48,128]{2,1,0:T(8,128)(2,1)S(1)}, u32[]{:S(2)}, u32[]{:S(2)}) %collective-permute-start.16) | collective-permute-done | bytes 36896 | tf_op jit(solution)/shard_map/ppermute | solution.py:234
  43.0 0.1 collective-permute-start.17
  43.1 1.7 %own.1.whole_ref = bf16[6,384,128]{2,1,0:T(8,128)(2,1)} custom-call(s32[24]{0:T(128)S(1)} %copy-done, bf16[6,384,128]{2,1,0:T(8,128)(2,1)S(1)} %get-tuple-element.46.spatial_ref, bf16[3,48,128]{2,1,0:T(8,128)(2,1)S(1)} %get-tuple-element.38.refs_0_.rest_0_, bf16[3,48,128]{2,1,0:T(8,128)(2,1)S(1)} %collective-permute-done.10.refs_1_.rest_1_, ...), custom_call_target="tpu_custom_call" | custom-call | tf_op jit(solution)/shard_map/own/pallas_call | solution.py:286
  44.7 0.6 %merge.1 = bf16[6,384,128]{2,1,0:T(8,128)(2,1)} custom-call(s32[24]{0:T(128)S(1)} %copy-done, bf16[2,384,128]{2,1,0:T(8,128)(2,1)S(1)} %collective-permute-done.17.given_ref, bf16[6,384,128]{2,1,0:T(8,128)(2,1)} %own.1.whole_ref), custom_call_target="tpu_custom_call", output_to_operand_aliasing={{}: (2, {})} | custom-call | tf_op jit(solution)/shard_map/merge/pallas_call | solution.py:295
  (15 shorter events, 0.1 us)
Async XLA Ops:
  0.0 3.3 %collective-permute-start = (bf16[6,384,128]{2,1,0:T(8,128)(2,1)}, bf16[6,384,128]{2,1,0:T(8,128)(2,1)S(1)}, u32[]{:S(2)}, u32[]{:S(2)}) collective-permute-start(bf16[6,384,128]{2,1,0:T(8,128)(2,1)} %bitcast.12), channel_id=1, source_target_pairs={{0,1},{1,0},{2,3},{3,2},{4,5},{5,4},{6,7},{7,6},{8,9},{9,8},{10,11... | collective-permute-start | bytes 1769480 | tf_op jit(solution)/shard_map/ppermute | solution.py:231
  0.5 0.7 %copy-start = (s32[24]{0:T(128)S(1)}, s32[24]{0:T(128)}, u32[]{:S(2)}) copy-start(s32[24]{0:T(128)} %class_ref.9) | copy-start | bytes 292
  0.5 2.9 %collective-permute-start.1 = (bf16[6,384,128]{2,1,0:T(8,128)(2,1)}, bf16[6,384,128]{2,1,0:T(8,128)(2,1)S(1)}, u32[]{:S(2)}, u32[]{:S(2)}) collective-permute-start(bf16[6,384,128]{2,1,0:T(8,128)(2,1)} %bitcast.14), channel_id=1, source_target_pairs={{0,1},{1,0},{2,3},{3,2},{4,5},{5,4},{6,7},{7,6},{8,9},{9,8},{10,11... | collective-permute-start | bytes 1769480 | tf_op jit(solution)/shard_map/ppermute | solution.py:231
  0.5 3.5 %collective-permute-start.2 = (bf16[6,384,128]{2,1,0:T(8,128)(2,1)}, bf16[6,384,128]{2,1,0:T(8,128)(2,1)S(1)}, u32[]{:S(2)}, u32[]{:S(2)}) collective-permute-start(bf16[6,384,128]{2,1,0:T(8,128)(2,1)} %bitcast.16), channel_id=1, source_target_pairs={{0,1},{1,0},{2,3},{3,2},{4,5},{5,4},{6,7},{7,6},{8,9},{9,8},{10,11... | collective-permute-start | bytes 1769480 | tf_op jit(solution)/shard_map/ppermute | solution.py:231
  4.7 10.5 %collective-permute-start.3 = (bf16[3,3,48,128]{3,2,1,0:T(8,128)(2,1)S(1)}, bf16[3,3,48,128]{3,2,1,0:T(8,128)(2,1)S(1)}, u32[]{:S(2)}, u32[]{:S(2)}) collective-permute-start(bf16[3,3,48,128]{3,2,1,0:T(8,128)(2,1)S(1)} %get-tuple-element.31), channel_id=1, source_target_pairs={{0,16},{4,20},{8,24},{12,28},{16,0},{20,4},{24,8},{28,12},{1,17},{... | collective-permute-start | bytes 331784 | tf_op jit(solution)/shard_map/ppermute | solution.py:234
  8.7 8.4 %collective-permute-start.4 = (bf16[3,3,48,128]{3,2,1,0:T(8,128)(2,1)S(1)}, bf16[3,3,48,128]{3,2,1,0:T(8,128)(2,1)S(1)}, u32[]{:S(2)}, u32[]{:S(2)}) collective-permute-start(bf16[3,3,48,128]{3,2,1,0:T(8,128)(2,1)S(1)} %get-tuple-element.32), channel_id=1, source_target_pairs={{0,8},{4,12},{8,0},{12,4},{16,24},{20,28},{24,16},{28,20},{1,9},{5... | collective-permute-start | bytes 331784 | tf_op jit(solution)/shard_map/ppermute | solution.py:234
  10.3 13.6 %collective-permute-start.5 = (bf16[3,3,48,128]{3,2,1,0:T(8,128)(2,1)S(1)}, bf16[3,3,48,128]{3,2,1,0:T(8,128)(2,1)S(1)}, u32[]{:S(2)}, u32[]{:S(2)}) collective-permute-start(bf16[3,3,48,128]{3,2,1,0:T(8,128)(2,1)S(1)} %get-tuple-element.33), channel_id=1, source_target_pairs={{0,24},{4,28},{8,16},{12,20},{16,8},{20,12},{24,0},{28,4},{1,25},{... | collective-permute-start | bytes 331784 | tf_op jit(solution)/shard_map/ppermute | solution.py:234
  10.3 13.6 %collective-permute-start.6 = (bf16[3,3,48,128]{3,2,1,0:T(8,128)(2,1)S(1)}, bf16[3,3,48,128]{3,2,1,0:T(8,128)(2,1)S(1)}, u32[]{:S(2)}, u32[]{:S(2)}) collective-permute-start(bf16[3,3,48,128]{3,2,1,0:T(8,128)(2,1)S(1)} %get-tuple-element.34), channel_id=1, source_target_pairs={{0,12},{4,8},{8,4},{12,0},{16,28},{20,24},{24,20},{28,16},{1,13},{... | collective-permute-start | bytes 331784 | tf_op jit(solution)/shard_map/ppermute | solution.py:234
  12.1 8.6 %copy-start.1 = (s32[4,4]{1,0:T(4,128)S(1)}, s32[4,4]{1,0:T(4,128)}, u32[]{:S(2)}) copy-start(s32[4,4]{1,0:T(4,128)} %mask_ref.1) | copy-start | bytes 196
  12.1 11.8 %collective-permute-start.7 = (bf16[3,3,48,128]{3,2,1,0:T(8,128)(2,1)S(1)}, bf16[3,3,48,128]{3,2,1,0:T(8,128)(2,1)S(1)}, u32[]{:S(2)}, u32[]{:S(2)}) collective-permute-start(bf16[3,3,48,128]{3,2,1,0:T(8,128)(2,1)S(1)} %get-tuple-element.35), channel_id=1, source_target_pairs={{0,4},{4,0},{8,12},{12,8},{16,20},{20,16},{24,28},{28,24},{1,5},{5... | collective-permute-start | bytes 331784 | tf_op jit(solution)/shard_map/ppermute | solution.py:234
  15.1 13.0 %collective-permute-start.8 = (bf16[3,3,48,128]{3,2,1,0:T(8,128)(2,1)S(1)}, bf16[3,3,48,128]{3,2,1,0:T(8,128)(2,1)S(1)}, u32[]{:S(2)}, u32[]{:S(2)}) collective-permute-start(bf16[3,3,48,128]{3,2,1,0:T(8,128)(2,1)S(1)} %get-tuple-element.36), channel_id=1, source_target_pairs={{0,20},{4,16},{8,28},{12,24},{16,4},{20,0},{24,12},{28,8},{1,21},{... | collective-permute-start | bytes 331784 | tf_op jit(solution)/shard_map/ppermute | solution.py:234
  17.1 11.0 %collective-permute-start.9 = (bf16[3,3,48,128]{3,2,1,0:T(8,128)(2,1)S(1)}, bf16[3,3,48,128]{3,2,1,0:T(8,128)(2,1)S(1)}, u32[]{:S(2)}, u32[]{:S(2)}) collective-permute-start(bf16[3,3,48,128]{3,2,1,0:T(8,128)(2,1)S(1)} %get-tuple-element.37), channel_id=1, source_target_pairs={{0,28},{4,24},{8,20},{12,16},{16,12},{20,8},{24,4},{28,0},{1,29},{... | collective-permute-start | bytes 331784 | tf_op jit(solution)/shard_map/ppermute | solution.py:234
  29.0 8.6 %collective-permute-start.10 = (bf16[3,48,128]{2,1,0:T(8,128)(2,1)S(1)}, bf16[3,48,128]{2,1,0:T(8,128)(2,1)S(1)}, u32[]{:S(2)}, u32[]{:S(2)}) collective-permute-start(bf16[3,48,128]{2,1,0:T(8,128)(2,1)S(1)} %get-tuple-element.39), channel_id=1, source_target_pairs={{0,24},{4,28},{8,16},{12,20},{16,8},{20,12},{24,0},{28,4},{1,25},{... | collective-permute-start | bytes 110600 | tf_op jit(solution)/shard_map/ppermute | solution.py:234
  31.9 7.1 %collective-permute-start.11 = (bf16[3,48,128]{2,1,0:T(8,128)(2,1)S(1)}, bf16[3,48,128]{2,1,0:T(8,128)(2,1)S(1)}, u32[]{:S(2)}, u32[]{:S(2)}) collective-permute-start(bf16[3,48,128]{2,1,0:T(8,128)(2,1)S(1)} %get-tuple-element.40), channel_id=1, source_target_pairs={{0,28},{4,24},{8,20},{12,16},{16,12},{20,8},{24,4},{28,0},{1,29},{... | collective-permute-start | bytes 110600 | tf_op jit(solution)/shard_map/ppermute | solution.py:234
  33.1 7.1 %collective-permute-start.12 = (bf16[3,48,128]{2,1,0:T(8,128)(2,1)S(1)}, bf16[3,48,128]{2,1,0:T(8,128)(2,1)S(1)}, u32[]{:S(2)}, u32[]{:S(2)}) collective-permute-start(bf16[3,48,128]{2,1,0:T(8,128)(2,1)S(1)} %get-tuple-element.41), channel_id=1, source_target_pairs={{0,16},{4,20},{8,24},{12,28},{16,0},{20,4},{24,8},{28,12},{1,17},{... | collective-permute-start | bytes 110600 | tf_op jit(solution)/shard_map/ppermute | solution.py:234
  35.2 5.8 %collective-permute-start.13 = (bf16[3,48,128]{2,1,0:T(8,128)(2,1)S(1)}, bf16[3,48,128]{2,1,0:T(8,128)(2,1)S(1)}, u32[]{:S(2)}, u32[]{:S(2)}) collective-permute-start(bf16[3,48,128]{2,1,0:T(8,128)(2,1)S(1)} %get-tuple-element.42), channel_id=1, source_target_pairs={{0,20},{4,16},{8,28},{12,24},{16,4},{20,0},{24,12},{28,8},{1,21},{... | collective-permute-start | bytes 110600 | tf_op jit(solution)/shard_map/ppermute | solution.py:234
  36.7 4.9 %collective-permute-start.14 = (bf16[3,48,128]{2,1,0:T(8,128)(2,1)S(1)}, bf16[3,48,128]{2,1,0:T(8,128)(2,1)S(1)}, u32[]{:S(2)}, u32[]{:S(2)}) collective-permute-start(bf16[3,48,128]{2,1,0:T(8,128)(2,1)S(1)} %get-tuple-element.43), channel_id=1, source_target_pairs={{0,12},{4,8},{8,4},{12,0},{16,28},{20,24},{24,20},{28,16},{1,13},{... | collective-permute-start | bytes 110600 | tf_op jit(solution)/shard_map/ppermute | solution.py:234
  37.7 4.1 %collective-permute-start.15 = (bf16[3,48,128]{2,1,0:T(8,128)(2,1)S(1)}, bf16[3,48,128]{2,1,0:T(8,128)(2,1)S(1)}, u32[]{:S(2)}, u32[]{:S(2)}) collective-permute-start(bf16[3,48,128]{2,1,0:T(8,128)(2,1)S(1)} %get-tuple-element.44), channel_id=1, source_target_pairs={{0,8},{4,12},{8,0},{12,4},{16,24},{20,28},{24,16},{28,20},{1,9},{5... | collective-permute-start | bytes 110600 | tf_op jit(solution)/shard_map/ppermute | solution.py:234
  39.0 4.0 %collective-permute-start.16 = (bf16[3,48,128]{2,1,0:T(8,128)(2,1)S(1)}, bf16[3,48,128]{2,1,0:T(8,128)(2,1)S(1)}, u32[]{:S(2)}, u32[]{:S(2)}) collective-permute-start(bf16[3,48,128]{2,1,0:T(8,128)(2,1)S(1)} %get-tuple-element.45), channel_id=1, source_target_pairs={{0,4},{4,0},{8,12},{12,8},{16,20},{20,16},{24,28},{28,24},{1,5},{5... | collective-permute-start | bytes 110600 | tf_op jit(solution)/shard_map/ppermute | solution.py:234
  43.0 1.7 %collective-permute-start.17 = (bf16[2,384,128]{2,1,0:T(8,128)(2,1)S(1)}, bf16[2,384,128]{2,1,0:T(8,128)(2,1)S(1)}, u32[]{:S(2)}, u32[]{:S(2)}) collective-permute-start(bf16[2,384,128]{2,1,0:T(8,128)(2,1)S(1)} %gather.1), channel_id=1, source_target_pairs={{0,1},{1,0},{2,3},{3,2},{4,5},{5,4},{6,7},{7,6},{8,9},{9,8},{10,11... | collective-permute-start | bytes 589832 | tf_op jit(solution)/shard_map/ppermute | solution.py:231

commit v6 on v5

--- a/solution.py
+++ b/solution.py
@@ -82,7 +82,7 @@
 
 
 def distances(ranks):
-    far, near = [*range(ranks // 2, ranks, 2), *range(ranks // 2 + 1, ranks, 2)], list(range(1, ranks // 2))[::-1]
+    far, near = list(range(ranks // 2, ranks)), list(range(1, ranks // 2))[::-1]
     return [0, *far[:1], *near[-2:-1], *far[1:2], *near[:-2], *near[-1:], *far[2:]]
 
 

time: 46.1 us -> 45.3 us (0.983)
  waiting for transfers between devices: 10.1 us -> 6.74 us
  starting transfers between devices: 25.8 us -> 28.3 us
    ppermute x14, waiting for transfers between devices: 9.42 us -> 6.09 us  [send(): lax.ppermute(array, 'tm', [(rank, rank ^ step) for rank in range(ranks)])]
    ppermute x14, starting transfers between devices: 24.7 us -> 27.2 us  [send(): lax.ppermute(array, 'tm', [(rank, rank ^ step) for rank in range(ranks)])]
where the time goes in v6:
time: 45.3 us; the launch traced here: 44.5 us
  starting transfers between devices  28.3 us (62%)
  Pallas kernels  9.25 us (20%)
  waiting for transfers between devices  6.74 us (15%)
    ppermute x14, starting transfers between devices, send(): lax.ppermute(array, 'tm', [(rank, rank ^ step) for rank in range(ranks)])  27.2 us
    ppermute x14, waiting for transfers between devices, send(): lax.ppermute(array, 'tm', [(rank, rank ^ step) for rank in range(ranks)])  6.09 us
    pallas_call x1, Pallas kernels, per_device(): pl.pallas_call(functools.partial(spatial_kernel, (group_heads, ranks, blo...  3.17 us
    pallas_call x1, Pallas kernels, per_device(): pl.pallas_call(load_kernel, out_shape=[whole] * 3, in_specs=[smem] + [hbm...  2.21 us
    pallas_call x1, Pallas kernels, per_device(): pl.pallas_call(functools.partial(own_kernel, (group_heads, most, least, r...  1.65 us
    ppermute x4, starting transfers between devices, swap(): return lax.ppermute(array, 'head', pairs)  1.03 us
    pallas_call x1, Pallas kernels, per_device(): pl.pallas_call(functools.partial(temporal_kernel, (slots, ranks, share)),...  0.94 us
  transfers between devices with their start and end apart: 18, of which 7 were waited for; matrix products, arithmetic and copies ran while one was open for 0% of the time, Pallas kernels for 16%

profile of v6, /device:TPU:0, one launch (start us, length us, event | category | flops | bytes accessed | tf_op | source)
XLA Modules:
  0.0 44.5 jit_solution(17325616063516177057)
XLA Ops:
  0.0 0.5 %collective-permute-start = (bf16[6,384,128]{2,1,0:T(8,128)(2,1)}, bf16[6,384,128]{2,1,0:T(8,128)(2,1)S(1)}, u32[]{:S(2)}, u32[]{:S(2)}) collective-permute-start(bf16[6,384,128]{2,1,0:T(8,128)(2,1)} %bitcast.12), channel_id=1, source_target_pairs={{0,1},{1,0},{2,3},{3,2},{4,5},{5,4},{6,7},{7,6},{8,9},{9,8},{10,11... | collective-permute-start | bytes 1769480 | tf_op jit(solution)/shard_map/ppermute | solution.py:231
  0.5 0.1 collective-permute-start.1
  0.5 0.4 %collective-permute-start.2 = (bf16[6,384,128]{2,1,0:T(8,128)(2,1)}, bf16[6,384,128]{2,1,0:T(8,128)(2,1)S(1)}, u32[]{:S(2)}, u32[]{:S(2)}) collective-permute-start(bf16[6,384,128]{2,1,0:T(8,128)(2,1)} %bitcast.16), channel_id=1, source_target_pairs={{0,1},{1,0},{2,3},{3,2},{4,5},{5,4},{6,7},{7,6},{8,9},{9,8},{10,11... | collective-permute-start | bytes 1769480 | tf_op jit(solution)/shard_map/ppermute | solution.py:231
  1.0 0.1 copy-done
  1.1 2.2 %load.1 = (bf16[6,384,128]{2,1,0:T(8,128)(2,1)S(1)}, bf16[6,384,128]{2,1,0:T(8,128)(2,1)S(1)}, bf16[6,384,128]{2,1,0:T(8,128)(2,1)S(1)}) custom-call(s32[24]{0:T(128)S(1)} %copy-done, bf16[6,384,128]{2,1,0:T(8,128)(2,1)} %bitcast.13, bf16[6,384,128]{2,1,0:T(8,128)(2,1)} %bitcast.15, bf16[6,384,128]{2,1,0:T(8,128)(2,1)} %bitcast.17), custom_call_target="tpu_custom_call" | custom-call | tf_op jit(solution)/shard_map/load/pallas_call | solution.py:237
  3.3 0.6 %collective-permute-done.2.refs_5_ = bf16[6,384,128]{2,1,0:T(8,128)(2,1)S(1)} collective-permute-done((bf16[6,384,128]{2,1,0:T(8,128)(2,1)}, bf16[6,384,128]{2,1,0:T(8,128)(2,1)S(1)}, u32[]{:S(2)}, u32[]{:S(2)}) %collective-permute-start.2) | collective-permute-done | bytes 589856 | tf_op jit(solution)/shard_map/ppermute | solution.py:231
  4.0 0.7 %pack.1 = (bf16[3,3,48,128]{3,2,1,0:T(8,128)(2,1)S(1)}, bf16[3,3,48,128]{3,2,1,0:T(8,128)(2,1)S(1)}, bf16[3,3,48,128]{3,2,1,0:T(8,128)(2,1)S(1)}, bf16[3,3,48,12...) custom-call(s32[24]{0:T(128)S(1)} %copy-done, ...), custom_call_target="tpu_custom_call" | custom-call | tf_op jit(solution)/shard_map/pack/pallas_call | solution.py:246
  4.7 4.0 %collective-permute-start.3 = (bf16[3,3,48,128]{3,2,1,0:T(8,128)(2,1)S(1)}, bf16[3,3,48,128]{3,2,1,0:T(8,128)(2,1)S(1)}, u32[]{:S(2)}, u32[]{:S(2)}) collective-permute-start(bf16[3,3,48,128]{3,2,1,0:T(8,128)(2,1)S(1)} %get-tuple-element.31), channel_id=1, source_target_pairs={{0,16},{4,20},{8,24},{12,28},{16,0},{20,4},{24,8},{28,12},{1,17},{... | collective-permute-start | bytes 331784 | tf_op jit(solution)/shard_map/ppermute | solution.py:234
  8.7 1.6 %collective-permute-start.4 = (bf16[3,3,48,128]{3,2,1,0:T(8,128)(2,1)S(1)}, bf16[3,3,48,128]{3,2,1,0:T(8,128)(2,1)S(1)}, u32[]{:S(2)}, u32[]{:S(2)}) collective-permute-start(bf16[3,3,48,128]{3,2,1,0:T(8,128)(2,1)S(1)} %get-tuple-element.32), channel_id=1, source_target_pairs={{0,8},{4,12},{8,0},{12,4},{16,24},{20,28},{24,16},{28,20},{1,9},{5... | collective-permute-start | bytes 331784 | tf_op jit(solution)/shard_map/ppermute | solution.py:234
  10.3 1.3 %collective-permute-start.5 = (bf16[3,3,48,128]{3,2,1,0:T(8,128)(2,1)S(1)}, bf16[3,3,48,128]{3,2,1,0:T(8,128)(2,1)S(1)}, u32[]{:S(2)}, u32[]{:S(2)}) collective-permute-start(bf16[3,3,48,128]{3,2,1,0:T(8,128)(2,1)S(1)} %get-tuple-element.33), channel_id=1, source_target_pairs={{0,20},{4,16},{8,28},{12,24},{16,4},{20,0},{24,12},{28,8},{1,21},{... | collective-permute-start | bytes 331784 | tf_op jit(solution)/shard_map/ppermute | solution.py:234
  11.5 0.1 collective-permute-start.6
  11.7 1.8 %collective-permute-start.7 = (bf16[3,3,48,128]{3,2,1,0:T(8,128)(2,1)S(1)}, bf16[3,3,48,128]{3,2,1,0:T(8,128)(2,1)S(1)}, u32[]{:S(2)}, u32[]{:S(2)}) collective-permute-start(bf16[3,3,48,128]{3,2,1,0:T(8,128)(2,1)S(1)} %get-tuple-element.35), channel_id=1, source_target_pairs={{0,4},{4,0},{8,12},{12,8},{16,20},{20,16},{24,28},{28,24},{1,5},{5... | collective-permute-start | bytes 331784 | tf_op jit(solution)/shard_map/ppermute | solution.py:234
  13.5 1.1 %collective-permute-done.3.rest_1_ = bf16[3,3,48,128]{3,2,1,0:T(8,128)(2,1)S(1)} collective-permute-done((bf16[3,3,48,128]{3,2,1,0:T(8,128)(2,1)S(1)}, bf16[3,3,48,128]{3,2,1,0:T(8,128)(2,1)S(1)}, u32[]{:S(2)}, u32[]{:S(2)}) %collective-permute-start.3) | collective-permute-done | bytes 110624 | tf_op jit(solution)/shard_map/ppermute | solution.py:234
  14.6 4.3 %collective-permute-start.8 = (bf16[3,3,48,128]{3,2,1,0:T(8,128)(2,1)S(1)}, bf16[3,3,48,128]{3,2,1,0:T(8,128)(2,1)S(1)}, u32[]{:S(2)}, u32[]{:S(2)}) collective-permute-start(bf16[3,3,48,128]{3,2,1,0:T(8,128)(2,1)S(1)} %get-tuple-element.36), channel_id=1, source_target_pairs={{0,24},{4,28},{8,16},{12,20},{16,8},{20,12},{24,0},{28,4},{1,25},{... | collective-permute-start | bytes 331784 | tf_op jit(solution)/shard_map/ppermute | solution.py:234
  18.8 1.8 %collective-permute-start.9 = (bf16[3,3,48,128]{3,2,1,0:T(8,128)(2,1)S(1)}, bf16[3,3,48,128]{3,2,1,0:T(8,128)(2,1)S(1)}, u32[]{:S(2)}, u32[]{:S(2)}) collective-permute-start(bf16[3,3,48,128]{3,2,1,0:T(8,128)(2,1)S(1)} %get-tuple-element.37), channel_id=1, source_target_pairs={{0,28},{4,24},{8,20},{12,16},{16,12},{20,8},{24,4},{28,0},{1,29},{... | collective-permute-start | bytes 331784 | tf_op jit(solution)/shard_map/ppermute | solution.py:234
  20.6 3.2 %spatial.1 = (bf16[6,384,128]{2,1,0:T(8,128)(2,1)S(1)}, f32[128,128]{1,0:T(8,128)S(1)}) custom-call(s32[24]{0:T(128)S(1)} %copy-done, s32[4,4]{1,0:T(4,128)S(1)} %copy-done.1, bf16[6,384,128]{2,1,0:T(8,128)(2,1)S(1)} %get-tuple-element.26.q_ref.refs_0_, bf16[6,384,128]{2,1,0:T(8,128)(2,1)S(1)} %get-tuple-element.27.k_ref.refs_1_, ...), custom_call_target="tpu_custom_call" | custom-call | flops 377487360 | bytes 2359296 | tf_op jit(solution)/shard_map/spatial/pallas_call | solution.py:256
  23.9 2.5 %collective-permute-done.9.rest_7_ = bf16[3,3,48,128]{3,2,1,0:T(8,128)(2,1)S(1)} collective-permute-done((bf16[3,3,48,128]{3,2,1,0:T(8,128)(2,1)S(1)}, bf16[3,3,48,128]{3,2,1,0:T(8,128)(2,1)S(1)}, u32[]{:S(2)}, u32[]{:S(2)}) %collective-permute-start.9) | collective-permute-done | bytes 110624 | tf_op jit(solution)/shard_map/ppermute | solution.py:234
  26.3 0.9 %temporal.1 = (bf16[3,48,128]{2,1,0:T(8,128)(2,1)S(1)}, bf16[3,48,128]{2,1,0:T(8,128)(2,1)S(1)}, bf16[3,48,128]{2,1,0:T(8,128)(2,1)S(1)}, bf16[3,48,128]{2,1,0:T...) custom-call(f32[128,128]{1,0:T(8,128)S(1)} %get-tuple-element.29.bia, ...), custom_call_target="tpu_custom_call" | custom-call | tf_op jit(solution)/shard_map/temporal/pallas_call | solution.py:266
  27.3 2.6 %collective-permute-start.10 = (bf16[3,48,128]{2,1,0:T(8,128)(2,1)S(1)}, bf16[3,48,128]{2,1,0:T(8,128)(2,1)S(1)}, u32[]{:S(2)}, u32[]{:S(2)}) collective-permute-start(bf16[3,48,128]{2,1,0:T(8,128)(2,1)S(1)} %get-tuple-element.39), channel_id=1, source_target_pairs={{0,24},{4,28},{8,16},{12,20},{16,8},{20,12},{24,0},{28,4},{1,25},{... | collective-permute-start | bytes 110600 | tf_op jit(solution)/shard_map/ppermute | solution.py:234
  29.9 2.2 %collective-permute-start.11 = (bf16[3,48,128]{2,1,0:T(8,128)(2,1)S(1)}, bf16[3,48,128]{2,1,0:T(8,128)(2,1)S(1)}, u32[]{:S(2)}, u32[]{:S(2)}) collective-permute-start(bf16[3,48,128]{2,1,0:T(8,128)(2,1)S(1)} %get-tuple-element.40), channel_id=1, source_target_pairs={{0,28},{4,24},{8,20},{12,16},{16,12},{20,8},{24,4},{28,0},{1,29},{... | collective-permute-start | bytes 110600 | tf_op jit(solution)/shard_map/ppermute | solution.py:234
  32.1 3.1 %collective-permute-start.12 = (bf16[3,48,128]{2,1,0:T(8,128)(2,1)S(1)}, bf16[3,48,128]{2,1,0:T(8,128)(2,1)S(1)}, u32[]{:S(2)}, u32[]{:S(2)}) collective-permute-start(bf16[3,48,128]{2,1,0:T(8,128)(2,1)S(1)} %get-tuple-element.41), channel_id=1, source_target_pairs={{0,16},{4,20},{8,24},{12,28},{16,0},{20,4},{24,8},{28,12},{1,17},{... | collective-permute-start | bytes 110600 | tf_op jit(solution)/shard_map/ppermute | solution.py:234
  35.2 1.0 %collective-permute-start.13 = (bf16[3,48,128]{2,1,0:T(8,128)(2,1)S(1)}, bf16[3,48,128]{2,1,0:T(8,128)(2,1)S(1)}, u32[]{:S(2)}, u32[]{:S(2)}) collective-permute-start(bf16[3,48,128]{2,1,0:T(8,128)(2,1)S(1)} %get-tuple-element.42), channel_id=1, source_target_pairs={{0,20},{4,16},{8,28},{12,24},{16,4},{20,0},{24,12},{28,8},{1,21},{... | collective-permute-start | bytes 110600 | tf_op jit(solution)/shard_map/ppermute | solution.py:234
  36.1 1.5 %collective-permute-start.14 = (bf16[3,48,128]{2,1,0:T(8,128)(2,1)S(1)}, bf16[3,48,128]{2,1,0:T(8,128)(2,1)S(1)}, u32[]{:S(2)}, u32[]{:S(2)}) collective-permute-start(bf16[3,48,128]{2,1,0:T(8,128)(2,1)S(1)} %get-tuple-element.43), channel_id=1, source_target_pairs={{0,12},{4,8},{8,4},{12,0},{16,28},{20,24},{24,20},{28,16},{1,13},{... | collective-permute-start | bytes 110600 | tf_op jit(solution)/shard_map/ppermute | solution.py:234
  37.6 0.5 %collective-permute-start.15 = (bf16[3,48,128]{2,1,0:T(8,128)(2,1)S(1)}, bf16[3,48,128]{2,1,0:T(8,128)(2,1)S(1)}, u32[]{:S(2)}, u32[]{:S(2)}) collective-permute-start(bf16[3,48,128]{2,1,0:T(8,128)(2,1)S(1)} %get-tuple-element.44), channel_id=1, source_target_pairs={{0,8},{4,12},{8,0},{12,4},{16,24},{20,28},{24,16},{28,20},{1,9},{5... | collective-permute-start | bytes 110600 | tf_op jit(solution)/shard_map/ppermute | solution.py:234
  38.2 1.5 %collective-permute-start.16 = (bf16[3,48,128]{2,1,0:T(8,128)(2,1)S(1)}, bf16[3,48,128]{2,1,0:T(8,128)(2,1)S(1)}, u32[]{:S(2)}, u32[]{:S(2)}) collective-permute-start(bf16[3,48,128]{2,1,0:T(8,128)(2,1)S(1)} %get-tuple-element.45), channel_id=1, source_target_pairs={{0,4},{4,0},{8,12},{12,8},{16,20},{20,16},{24,28},{28,24},{1,5},{5... | collective-permute-start | bytes 110600 | tf_op jit(solution)/shard_map/ppermute | solution.py:234
  39.6 1.3 %collective-permute-done.13.refs_4_.rest_4_ = bf16[3,48,128]{2,1,0:T(8,128)(2,1)S(1)} collective-permute-done((bf16[3,48,128]{2,1,0:T(8,128)(2,1)S(1)}, bf16[3,48,128]{2,1,0:T(8,128)(2,1)S(1)}, u32[]{:S(2)}, u32[]{:S(2)}) %collective-permute-start.13) | collective-permute-done | bytes 36896 | tf_op jit(solution)/shard_map/ppermute | solution.py:234
  41.0 0.4 collective-permute-done.14.refs_5_.rest_5_
  41.4 0.2 collective-permute-done.15.refs_6_.rest_6_
  41.6 0.5 %collective-permute-done.16.refs_7_.rest_7_ = bf16[3,48,128]{2,1,0:T(8,128)(2,1)S(1)} collective-permute-done((bf16[3,48,128]{2,1,0:T(8,128)(2,1)S(1)}, bf16[3,48,128]{2,1,0:T(8,128)(2,1)S(1)}, u32[]{:S(2)}, u32[]{:S(2)}) %collective-permute-start.16) | collective-permute-done | bytes 36896 | tf_op jit(solution)/shard_map/ppermute | solution.py:234
  42.2 0.1 collective-permute-start.17
  42.2 1.7 %own.1.whole_ref = bf16[6,384,128]{2,1,0:T(8,128)(2,1)} custom-call(s32[24]{0:T(128)S(1)} %copy-done, bf16[6,384,128]{2,1,0:T(8,128)(2,1)S(1)} %get-tuple-element.46.spatial_ref, bf16[3,48,128]{2,1,0:T(8,128)(2,1)S(1)} %get-tuple-element.38.refs_0_.rest_0_, bf16[3,48,128]{2,1,0:T(8,128)(2,1)S(1)} %collective-permute-done.10.refs_1_.rest_1_, ...), custom_call_target="tpu_custom_call" | custom-call | tf_op jit(solution)/shard_map/own/pallas_call | solution.py:286
  43.9 0.6 %merge.1 = bf16[6,384,128]{2,1,0:T(8,128)(2,1)} custom-call(s32[24]{0:T(128)S(1)} %copy-done, bf16[2,384,128]{2,1,0:T(8,128)(2,1)S(1)} %collective-permute-done.17.given_ref, bf16[6,384,128]{2,1,0:T(8,128)(2,1)} %own.1.whole_ref), custom_call_target="tpu_custom_call", output_to_operand_aliasing={{}: (2, {})} | custom-call | tf_op jit(solution)/shard_map/merge/pallas_call | solution.py:295
  (15 shorter events, 0.1 us)
Async XLA Ops:
  0.0 3.3 %collective-permute-start = (bf16[6,384,128]{2,1,0:T(8,128)(2,1)}, bf16[6,384,128]{2,1,0:T(8,128)(2,1)S(1)}, u32[]{:S(2)}, u32[]{:S(2)}) collective-permute-start(bf16[6,384,128]{2,1,0:T(8,128)(2,1)} %bitcast.12), channel_id=1, source_target_pairs={{0,1},{1,0},{2,3},{3,2},{4,5},{5,4},{6,7},{7,6},{8,9},{9,8},{10,11... | collective-permute-start | bytes 1769480 | tf_op jit(solution)/shard_map/ppermute | solution.py:231
  0.5 0.7 %copy-start = (s32[24]{0:T(128)S(1)}, s32[24]{0:T(128)}, u32[]{:S(2)}) copy-start(s32[24]{0:T(128)} %class_ref.9) | copy-start | bytes 292
  0.5 2.9 %collective-permute-start.1 = (bf16[6,384,128]{2,1,0:T(8,128)(2,1)}, bf16[6,384,128]{2,1,0:T(8,128)(2,1)S(1)}, u32[]{:S(2)}, u32[]{:S(2)}) collective-permute-start(bf16[6,384,128]{2,1,0:T(8,128)(2,1)} %bitcast.14), channel_id=1, source_target_pairs={{0,1},{1,0},{2,3},{3,2},{4,5},{5,4},{6,7},{7,6},{8,9},{9,8},{10,11... | collective-permute-start | bytes 1769480 | tf_op jit(solution)/shard_map/ppermute | solution.py:231
  0.5 3.5 %collective-permute-start.2 = (bf16[6,384,128]{2,1,0:T(8,128)(2,1)}, bf16[6,384,128]{2,1,0:T(8,128)(2,1)S(1)}, u32[]{:S(2)}, u32[]{:S(2)}) collective-permute-start(bf16[6,384,128]{2,1,0:T(8,128)(2,1)} %bitcast.16), channel_id=1, source_target_pairs={{0,1},{1,0},{2,3},{3,2},{4,5},{5,4},{6,7},{7,6},{8,9},{9,8},{10,11... | collective-permute-start | bytes 1769480 | tf_op jit(solution)/shard_map/ppermute | solution.py:231
  4.7 9.9 %collective-permute-start.3 = (bf16[3,3,48,128]{3,2,1,0:T(8,128)(2,1)S(1)}, bf16[3,3,48,128]{3,2,1,0:T(8,128)(2,1)S(1)}, u32[]{:S(2)}, u32[]{:S(2)}) collective-permute-start(bf16[3,3,48,128]{3,2,1,0:T(8,128)(2,1)S(1)} %get-tuple-element.31), channel_id=1, source_target_pairs={{0,16},{4,20},{8,24},{12,28},{16,0},{20,4},{24,8},{28,12},{1,17},{... | collective-permute-start | bytes 331784 | tf_op jit(solution)/shard_map/ppermute | solution.py:234
  8.7 10.2 %collective-permute-start.4 = (bf16[3,3,48,128]{3,2,1,0:T(8,128)(2,1)S(1)}, bf16[3,3,48,128]{3,2,1,0:T(8,128)(2,1)S(1)}, u32[]{:S(2)}, u32[]{:S(2)}) collective-permute-start(bf16[3,3,48,128]{3,2,1,0:T(8,128)(2,1)S(1)} %get-tuple-element.32), channel_id=1, source_target_pairs={{0,8},{4,12},{8,0},{12,4},{16,24},{20,28},{24,16},{28,20},{1,9},{5... | collective-permute-start | bytes 331784 | tf_op jit(solution)/shard_map/ppermute | solution.py:234
  10.3 13.6 %collective-permute-start.5 = (bf16[3,3,48,128]{3,2,1,0:T(8,128)(2,1)S(1)}, bf16[3,3,48,128]{3,2,1,0:T(8,128)(2,1)S(1)}, u32[]{:S(2)}, u32[]{:S(2)}) collective-permute-start(bf16[3,3,48,128]{3,2,1,0:T(8,128)(2,1)S(1)} %get-tuple-element.33), channel_id=1, source_target_pairs={{0,20},{4,16},{8,28},{12,24},{16,4},{20,0},{24,12},{28,8},{1,21},{... | collective-permute-start | bytes 331784 | tf_op jit(solution)/shard_map/ppermute | solution.py:234
  11.5 12.3 %collective-permute-start.6 = (bf16[3,3,48,128]{3,2,1,0:T(8,128)(2,1)S(1)}, bf16[3,3,48,128]{3,2,1,0:T(8,128)(2,1)S(1)}, u32[]{:S(2)}, u32[]{:S(2)}) collective-permute-start(bf16[3,3,48,128]{3,2,1,0:T(8,128)(2,1)S(1)} %get-tuple-element.34), channel_id=1, source_target_pairs={{0,12},{4,8},{8,4},{12,0},{16,28},{20,24},{24,20},{28,16},{1,13},{... | collective-permute-start | bytes 331784 | tf_op jit(solution)/shard_map/ppermute | solution.py:234
  11.7 9.0 %copy-start.1 = (s32[4,4]{1,0:T(4,128)S(1)}, s32[4,4]{1,0:T(4,128)}, u32[]{:S(2)}) copy-start(s32[4,4]{1,0:T(4,128)} %mask_ref.1) | copy-start | bytes 196
  11.7 12.2 %collective-permute-start.7 = (bf16[3,3,48,128]{3,2,1,0:T(8,128)(2,1)S(1)}, bf16[3,3,48,128]{3,2,1,0:T(8,128)(2,1)S(1)}, u32[]{:S(2)}, u32[]{:S(2)}) collective-permute-start(bf16[3,3,48,128]{3,2,1,0:T(8,128)(2,1)S(1)} %get-tuple-element.35), channel_id=1, source_target_pairs={{0,4},{4,0},{8,12},{12,8},{16,20},{20,16},{24,28},{28,24},{1,5},{5... | collective-permute-start | bytes 331784 | tf_op jit(solution)/shard_map/ppermute | solution.py:234
  14.6 9.3 %collective-permute-start.8 = (bf16[3,3,48,128]{3,2,1,0:T(8,128)(2,1)S(1)}, bf16[3,3,48,128]{3,2,1,0:T(8,128)(2,1)S(1)}, u32[]{:S(2)}, u32[]{:S(2)}) collective-permute-start(bf16[3,3,48,128]{3,2,1,0:T(8,128)(2,1)S(1)} %get-tuple-element.36), channel_id=1, source_target_pairs={{0,24},{4,28},{8,16},{12,20},{16,8},{20,12},{24,0},{28,4},{1,25},{... | collective-permute-start | bytes 331784 | tf_op jit(solution)/shard_map/ppermute | solution.py:234
  18.8 7.5 %collective-permute-start.9 = (bf16[3,3,48,128]{3,2,1,0:T(8,128)(2,1)S(1)}, bf16[3,3,48,128]{3,2,1,0:T(8,128)(2,1)S(1)}, u32[]{:S(2)}, u32[]{:S(2)}) collective-permute-start(bf16[3,3,48,128]{3,2,1,0:T(8,128)(2,1)S(1)} %get-tuple-element.37), channel_id=1, source_target_pairs={{0,28},{4,24},{8,20},{12,16},{16,12},{20,8},{24,4},{28,0},{1,29},{... | collective-permute-start | bytes 331784 | tf_op jit(solution)/shard_map/ppermute | solution.py:234
  27.3 10.3 %collective-permute-start.10 = (bf16[3,48,128]{2,1,0:T(8,128)(2,1)S(1)}, bf16[3,48,128]{2,1,0:T(8,128)(2,1)S(1)}, u32[]{:S(2)}, u32[]{:S(2)}) collective-permute-start(bf16[3,48,128]{2,1,0:T(8,128)(2,1)S(1)} %get-tuple-element.39), channel_id=1, source_target_pairs={{0,24},{4,28},{8,16},{12,20},{16,8},{20,12},{24,0},{28,4},{1,25},{... | collective-permute-start | bytes 110600 | tf_op jit(solution)/shard_map/ppermute | solution.py:234
  29.9 8.3 %collective-permute-start.11 = (bf16[3,48,128]{2,1,0:T(8,128)(2,1)S(1)}, bf16[3,48,128]{2,1,0:T(8,128)(2,1)S(1)}, u32[]{:S(2)}, u32[]{:S(2)}) collective-permute-start(bf16[3,48,128]{2,1,0:T(8,128)(2,1)S(1)} %get-tuple-element.40), channel_id=1, source_target_pairs={{0,28},{4,24},{8,20},{12,16},{16,12},{20,8},{24,4},{28,0},{1,29},{... | collective-permute-start | bytes 110600 | tf_op jit(solution)/shard_map/ppermute | solution.py:234
  32.1 7.6 %collective-permute-start.12 = (bf16[3,48,128]{2,1,0:T(8,128)(2,1)S(1)}, bf16[3,48,128]{2,1,0:T(8,128)(2,1)S(1)}, u32[]{:S(2)}, u32[]{:S(2)}) collective-permute-start(bf16[3,48,128]{2,1,0:T(8,128)(2,1)S(1)} %get-tuple-element.41), channel_id=1, source_target_pairs={{0,16},{4,20},{8,24},{12,28},{16,0},{20,4},{24,8},{28,12},{1,17},{... | collective-permute-start | bytes 110600 | tf_op jit(solution)/shard_map/ppermute | solution.py:234
  35.2 5.8 %collective-permute-start.13 = (bf16[3,48,128]{2,1,0:T(8,128)(2,1)S(1)}, bf16[3,48,128]{2,1,0:T(8,128)(2,1)S(1)}, u32[]{:S(2)}, u32[]{:S(2)}) collective-permute-start(bf16[3,48,128]{2,1,0:T(8,128)(2,1)S(1)} %get-tuple-element.42), channel_id=1, source_target_pairs={{0,20},{4,16},{8,28},{12,24},{16,4},{20,0},{24,12},{28,8},{1,21},{... | collective-permute-start | bytes 110600 | tf_op jit(solution)/shard_map/ppermute | solution.py:234
  36.1 5.2 %collective-permute-start.14 = (bf16[3,48,128]{2,1,0:T(8,128)(2,1)S(1)}, bf16[3,48,128]{2,1,0:T(8,128)(2,1)S(1)}, u32[]{:S(2)}, u32[]{:S(2)}) collective-permute-start(bf16[3,48,128]{2,1,0:T(8,128)(2,1)S(1)} %get-tuple-element.43), channel_id=1, source_target_pairs={{0,12},{4,8},{8,4},{12,0},{16,28},{20,24},{24,20},{28,16},{1,13},{... | collective-permute-start | bytes 110600 | tf_op jit(solution)/shard_map/ppermute | solution.py:234
  37.6 4.0 %collective-permute-start.15 = (bf16[3,48,128]{2,1,0:T(8,128)(2,1)S(1)}, bf16[3,48,128]{2,1,0:T(8,128)(2,1)S(1)}, u32[]{:S(2)}, u32[]{:S(2)}) collective-permute-start(bf16[3,48,128]{2,1,0:T(8,128)(2,1)S(1)} %get-tuple-element.44), channel_id=1, source_target_pairs={{0,8},{4,12},{8,0},{12,4},{16,24},{20,28},{24,16},{28,20},{1,9},{5... | collective-permute-start | bytes 110600 | tf_op jit(solution)/shard_map/ppermute | solution.py:234
  38.2 4.0 %collective-permute-start.16 = (bf16[3,48,128]{2,1,0:T(8,128)(2,1)S(1)}, bf16[3,48,128]{2,1,0:T(8,128)(2,1)S(1)}, u32[]{:S(2)}, u32[]{:S(2)}) collective-permute-start(bf16[3,48,128]{2,1,0:T(8,128)(2,1)S(1)} %get-tuple-element.45), channel_id=1, source_target_pairs={{0,4},{4,0},{8,12},{12,8},{16,20},{20,16},{24,28},{28,24},{1,5},{5... | collective-permute-start | bytes 110600 | tf_op jit(solution)/shard_map/ppermute | solution.py:234
  42.2 1.7 %collective-permute-start.17 = (bf16[2,384,128]{2,1,0:T(8,128)(2,1)S(1)}, bf16[2,384,128]{2,1,0:T(8,128)(2,1)S(1)}, u32[]{:S(2)}, u32[]{:S(2)}) collective-permute-start(bf16[2,384,128]{2,1,0:T(8,128)(2,1)S(1)} %gather.1), channel_id=1, source_target_pairs={{0,1},{1,0},{2,3},{3,2},{4,5},{5,4},{6,7},{7,6},{8,9},{9,8},{10,11... | collective-permute-start | bytes 589832 | tf_op jit(solution)/shard_map/ppermute | solution.py:231

commit v7 on v6

--- a/solution.py
+++ b/solution.py
@@ -83,7 +83,7 @@
 
 def distances(ranks):
     far, near = list(range(ranks // 2, ranks)), list(range(1, ranks // 2))[::-1]
-    return [0, *far[:1], *near[-2:-1], *far[1:2], *near[:-2], *near[-1:], *far[2:]]
+    return [0, *far[:1], *near[-2:-1], *far[1:3], *near[:-2], *near[-1:], *far[3:]]
 
 
 def back_distances(ranks):

time: 45.3 us -> 45.3 us (level)
  starting transfers between devices: 28.3 us -> 29.3 us
  waiting for transfers between devices: 6.74 us -> 5.74 us
    ppermute x14, starting transfers between devices: 27.2 us -> 28.2 us  [send(): lax.ppermute(array, 'tm', [(rank, rank ^ step) for rank in range(ranks)])]
    ppermute x14, waiting for transfers between devices: 6.09 us -> 5.1 us  [send(): lax.ppermute(array, 'tm', [(rank, rank ^ step) for rank in range(ranks)])]
where the time goes in v7:
time: 45.3 us; the launch traced here: 44.5 us
  starting transfers between devices  29.3 us (65%)
  Pallas kernels  9.25 us (20%)
  waiting for transfers between devices  5.74 us (13%)
    ppermute x14, starting transfers between devices, send(): lax.ppermute(array, 'tm', [(rank, rank ^ step) for rank in range(ranks)])  28.2 us
    ppermute x14, waiting for transfers between devices, send(): lax.ppermute(array, 'tm', [(rank, rank ^ step) for rank in range(ranks)])  5.1 us
    pallas_call x1, Pallas kernels, per_device(): pl.pallas_call(functools.partial(spatial_kernel, (group_heads, ranks, blo...  3.17 us
    pallas_call x1, Pallas kernels, per_device(): pl.pallas_call(load_kernel, out_shape=[whole] * 3, in_specs=[smem] + [hbm...  2.21 us
    pallas_call x1, Pallas kernels, per_device(): pl.pallas_call(functools.partial(own_kernel, (group_heads, most, least, r...  1.65 us
    ppermute x4, starting transfers between devices, swap(): return lax.ppermute(array, 'head', pairs)  1.03 us
    pallas_call x1, Pallas kernels, per_device(): pl.pallas_call(functools.partial(temporal_kernel, (slots, ranks, share)),...  0.94 us
  transfers between devices with their start and end apart: 18, of which 7 were waited for; matrix products, arithmetic and copies ran while one was open for 0% of the time, Pallas kernels for 16%

profile of v7, /device:TPU:0, one launch (start us, length us, event | category | flops | bytes accessed | tf_op | source)
XLA Modules:
  0.0 44.5 jit_solution(156396967297699627)
XLA Ops:
  0.0 0.5 %collective-permute-start = (bf16[6,384,128]{2,1,0:T(8,128)(2,1)}, bf16[6,384,128]{2,1,0:T(8,128)(2,1)S(1)}, u32[]{:S(2)}, u32[]{:S(2)}) collective-permute-start(bf16[6,384,128]{2,1,0:T(8,128)(2,1)} %bitcast.12), channel_id=1, source_target_pairs={{0,1},{1,0},{2,3},{3,2},{4,5},{5,4},{6,7},{7,6},{8,9},{9,8},{10,11... | collective-permute-start | bytes 1769480 | tf_op jit(solution)/shard_map/ppermute | solution.py:231
  0.5 0.1 collective-permute-start.1
  0.5 0.4 %collective-permute-start.2 = (bf16[6,384,128]{2,1,0:T(8,128)(2,1)}, bf16[6,384,128]{2,1,0:T(8,128)(2,1)S(1)}, u32[]{:S(2)}, u32[]{:S(2)}) collective-permute-start(bf16[6,384,128]{2,1,0:T(8,128)(2,1)} %bitcast.16), channel_id=1, source_target_pairs={{0,1},{1,0},{2,3},{3,2},{4,5},{5,4},{6,7},{7,6},{8,9},{9,8},{10,11... | collective-permute-start | bytes 1769480 | tf_op jit(solution)/shard_map/ppermute | solution.py:231
  1.0 0.1 copy-done
  1.1 2.2 %load.1 = (bf16[6,384,128]{2,1,0:T(8,128)(2,1)S(1)}, bf16[6,384,128]{2,1,0:T(8,128)(2,1)S(1)}, bf16[6,384,128]{2,1,0:T(8,128)(2,1)S(1)}) custom-call(s32[24]{0:T(128)S(1)} %copy-done, bf16[6,384,128]{2,1,0:T(8,128)(2,1)} %bitcast.13, bf16[6,384,128]{2,1,0:T(8,128)(2,1)} %bitcast.15, bf16[6,384,128]{2,1,0:T(8,128)(2,1)} %bitcast.17), custom_call_target="tpu_custom_call" | custom-call | tf_op jit(solution)/shard_map/load/pallas_call | solution.py:237
  3.3 0.6 %collective-permute-done.2.refs_5_ = bf16[6,384,128]{2,1,0:T(8,128)(2,1)S(1)} collective-permute-done((bf16[6,384,128]{2,1,0:T(8,128)(2,1)}, bf16[6,384,128]{2,1,0:T(8,128)(2,1)S(1)}, u32[]{:S(2)}, u32[]{:S(2)}) %collective-permute-start.2) | collective-permute-done | bytes 589856 | tf_op jit(solution)/shard_map/ppermute | solution.py:231
  4.0 0.7 %pack.1 = (bf16[3,3,48,128]{3,2,1,0:T(8,128)(2,1)S(1)}, bf16[3,3,48,128]{3,2,1,0:T(8,128)(2,1)S(1)}, bf16[3,3,48,128]{3,2,1,0:T(8,128)(2,1)S(1)}, bf16[3,3,48,12...) custom-call(s32[24]{0:T(128)S(1)} %copy-done, ...), custom_call_target="tpu_custom_call" | custom-call | tf_op jit(solution)/shard_map/pack/pallas_call | solution.py:246
  4.7 4.0 %collective-permute-start.3 = (bf16[3,3,48,128]{3,2,1,0:T(8,128)(2,1)S(1)}, bf16[3,3,48,128]{3,2,1,0:T(8,128)(2,1)S(1)}, u32[]{:S(2)}, u32[]{:S(2)}) collective-permute-start(bf16[3,3,48,128]{3,2,1,0:T(8,128)(2,1)S(1)} %get-tuple-element.31), channel_id=1, source_target_pairs={{0,16},{4,20},{8,24},{12,28},{16,0},{20,4},{24,8},{28,12},{1,17},{... | collective-permute-start | bytes 331784 | tf_op jit(solution)/shard_map/ppermute | solution.py:234
  8.7 1.6 %collective-permute-start.4 = (bf16[3,3,48,128]{3,2,1,0:T(8,128)(2,1)S(1)}, bf16[3,3,48,128]{3,2,1,0:T(8,128)(2,1)S(1)}, u32[]{:S(2)}, u32[]{:S(2)}) collective-permute-start(bf16[3,3,48,128]{3,2,1,0:T(8,128)(2,1)S(1)} %get-tuple-element.32), channel_id=1, source_target_pairs={{0,8},{4,12},{8,0},{12,4},{16,24},{20,28},{24,16},{28,20},{1,9},{5... | collective-permute-start | bytes 331784 | tf_op jit(solution)/shard_map/ppermute | solution.py:234
  10.3 1.3 %collective-permute-start.5 = (bf16[3,3,48,128]{3,2,1,0:T(8,128)(2,1)S(1)}, bf16[3,3,48,128]{3,2,1,0:T(8,128)(2,1)S(1)}, u32[]{:S(2)}, u32[]{:S(2)}) collective-permute-start(bf16[3,3,48,128]{3,2,1,0:T(8,128)(2,1)S(1)} %get-tuple-element.33), channel_id=1, source_target_pairs={{0,20},{4,16},{8,28},{12,24},{16,4},{20,0},{24,12},{28,8},{1,21},{... | collective-permute-start | bytes 331784 | tf_op jit(solution)/shard_map/ppermute | solution.py:234
  11.5 2.5 %collective-permute-start.6 = (bf16[3,3,48,128]{3,2,1,0:T(8,128)(2,1)S(1)}, bf16[3,3,48,128]{3,2,1,0:T(8,128)(2,1)S(1)}, u32[]{:S(2)}, u32[]{:S(2)}) collective-permute-start(bf16[3,3,48,128]{3,2,1,0:T(8,128)(2,1)S(1)} %get-tuple-element.34), channel_id=1, source_target_pairs={{0,24},{4,28},{8,16},{12,20},{16,8},{20,12},{24,0},{28,4},{1,25},{... | collective-permute-start | bytes 331784 | tf_op jit(solution)/shard_map/ppermute | solution.py:234
  14.0 0.6 %collective-permute-start.7 = (bf16[3,3,48,128]{3,2,1,0:T(8,128)(2,1)S(1)}, bf16[3,3,48,128]{3,2,1,0:T(8,128)(2,1)S(1)}, u32[]{:S(2)}, u32[]{:S(2)}) collective-permute-start(bf16[3,3,48,128]{3,2,1,0:T(8,128)(2,1)S(1)} %get-tuple-element.35), channel_id=1, source_target_pairs={{0,12},{4,8},{8,4},{12,0},{16,28},{20,24},{24,20},{28,16},{1,13},{... | collective-permute-start | bytes 331784 | tf_op jit(solution)/shard_map/ppermute | solution.py:234
  14.6 2.7 %collective-permute-start.8 = (bf16[3,3,48,128]{3,2,1,0:T(8,128)(2,1)S(1)}, bf16[3,3,48,128]{3,2,1,0:T(8,128)(2,1)S(1)}, u32[]{:S(2)}, u32[]{:S(2)}) collective-permute-start(bf16[3,3,48,128]{3,2,1,0:T(8,128)(2,1)S(1)} %get-tuple-element.36), channel_id=1, source_target_pairs={{0,4},{4,0},{8,12},{12,8},{16,20},{20,16},{24,28},{28,24},{1,5},{5... | collective-permute-start | bytes 331784 | tf_op jit(solution)/shard_map/ppermute | solution.py:234
  17.4 2.9 %collective-permute-start.9 = (bf16[3,3,48,128]{3,2,1,0:T(8,128)(2,1)S(1)}, bf16[3,3,48,128]{3,2,1,0:T(8,128)(2,1)S(1)}, u32[]{:S(2)}, u32[]{:S(2)}) collective-permute-start(bf16[3,3,48,128]{3,2,1,0:T(8,128)(2,1)S(1)} %get-tuple-element.37), channel_id=1, source_target_pairs={{0,28},{4,24},{8,20},{12,16},{16,12},{20,8},{24,4},{28,0},{1,29},{... | collective-permute-start | bytes 331784 | tf_op jit(solution)/shard_map/ppermute | solution.py:234
  20.3 3.2 %spatial.1 = (bf16[6,384,128]{2,1,0:T(8,128)(2,1)S(1)}, f32[128,128]{1,0:T(8,128)S(1)}) custom-call(s32[24]{0:T(128)S(1)} %copy-done, s32[4,4]{1,0:T(4,128)S(1)} %copy-done.1, bf16[6,384,128]{2,1,0:T(8,128)(2,1)S(1)} %get-tuple-element.26.q_ref.refs_0_, bf16[6,384,128]{2,1,0:T(8,128)(2,1)S(1)} %get-tuple-element.27.k_ref.refs_1_, ...), custom_call_target="tpu_custom_call" | custom-call | flops 377487360 | bytes 2359296 | tf_op jit(solution)/shard_map/spatial/pallas_call | solution.py:256
  23.5 0.5 %collective-permute-done.5.rest_3_ = bf16[3,3,48,128]{3,2,1,0:T(8,128)(2,1)S(1)} collective-permute-done((bf16[3,3,48,128]{3,2,1,0:T(8,128)(2,1)S(1)}, bf16[3,3,48,128]{3,2,1,0:T(8,128)(2,1)S(1)}, u32[]{:S(2)}, u32[]{:S(2)}) %collective-permute-start.5) | collective-permute-done | bytes 110624 | tf_op jit(solution)/shard_map/ppermute | solution.py:234
  24.0 2.1 %collective-permute-done.9.rest_7_ = bf16[3,3,48,128]{3,2,1,0:T(8,128)(2,1)S(1)} collective-permute-done((bf16[3,3,48,128]{3,2,1,0:T(8,128)(2,1)S(1)}, bf16[3,3,48,128]{3,2,1,0:T(8,128)(2,1)S(1)}, u32[]{:S(2)}, u32[]{:S(2)}) %collective-permute-start.9) | collective-permute-done | bytes 110624 | tf_op jit(solution)/shard_map/ppermute | solution.py:234
  26.1 0.9 %temporal.1 = (bf16[3,48,128]{2,1,0:T(8,128)(2,1)S(1)}, bf16[3,48,128]{2,1,0:T(8,128)(2,1)S(1)}, bf16[3,48,128]{2,1,0:T(8,128)(2,1)S(1)}, bf16[3,48,128]{2,1,0:T...) custom-call(f32[128,128]{1,0:T(8,128)S(1)} %get-tuple-element.29.bia, ...), custom_call_target="tpu_custom_call" | custom-call | tf_op jit(solution)/shard_map/temporal/pallas_call | solution.py:266
  27.0 2.7 %collective-permute-start.10 = (bf16[3,48,128]{2,1,0:T(8,128)(2,1)S(1)}, bf16[3,48,128]{2,1,0:T(8,128)(2,1)S(1)}, u32[]{:S(2)}, u32[]{:S(2)}) collective-permute-start(bf16[3,48,128]{2,1,0:T(8,128)(2,1)S(1)} %get-tuple-element.39), channel_id=1, source_target_pairs={{0,24},{4,28},{8,16},{12,20},{16,8},{20,12},{24,0},{28,4},{1,25},{... | collective-permute-start | bytes 110600 | tf_op jit(solution)/shard_map/ppermute | solution.py:234
  29.8 1.1 %collective-permute-start.11 = (bf16[3,48,128]{2,1,0:T(8,128)(2,1)S(1)}, bf16[3,48,128]{2,1,0:T(8,128)(2,1)S(1)}, u32[]{:S(2)}, u32[]{:S(2)}) collective-permute-start(bf16[3,48,128]{2,1,0:T(8,128)(2,1)S(1)} %get-tuple-element.40), channel_id=1, source_target_pairs={{0,28},{4,24},{8,20},{12,16},{16,12},{20,8},{24,4},{28,0},{1,29},{... | collective-permute-start | bytes 110600 | tf_op jit(solution)/shard_map/ppermute | solution.py:234
  30.9 4.3 %collective-permute-start.12 = (bf16[3,48,128]{2,1,0:T(8,128)(2,1)S(1)}, bf16[3,48,128]{2,1,0:T(8,128)(2,1)S(1)}, u32[]{:S(2)}, u32[]{:S(2)}) collective-permute-start(bf16[3,48,128]{2,1,0:T(8,128)(2,1)S(1)} %get-tuple-element.41), channel_id=1, source_target_pairs={{0,16},{4,20},{8,24},{12,28},{16,0},{20,4},{24,8},{28,12},{1,17},{... | collective-permute-start | bytes 110600 | tf_op jit(solution)/shard_map/ppermute | solution.py:234
  35.2 1.0 %collective-permute-start.13 = (bf16[3,48,128]{2,1,0:T(8,128)(2,1)S(1)}, bf16[3,48,128]{2,1,0:T(8,128)(2,1)S(1)}, u32[]{:S(2)}, u32[]{:S(2)}) collective-permute-start(bf16[3,48,128]{2,1,0:T(8,128)(2,1)S(1)} %get-tuple-element.42), channel_id=1, source_target_pairs={{0,20},{4,16},{8,28},{12,24},{16,4},{20,0},{24,12},{28,8},{1,21},{... | collective-permute-start | bytes 110600 | tf_op jit(solution)/shard_map/ppermute | solution.py:234
  36.1 1.5 %collective-permute-start.14 = (bf16[3,48,128]{2,1,0:T(8,128)(2,1)S(1)}, bf16[3,48,128]{2,1,0:T(8,128)(2,1)S(1)}, u32[]{:S(2)}, u32[]{:S(2)}) collective-permute-start(bf16[3,48,128]{2,1,0:T(8,128)(2,1)S(1)} %get-tuple-element.43), channel_id=1, source_target_pairs={{0,12},{4,8},{8,4},{12,0},{16,28},{20,24},{24,20},{28,16},{1,13},{... | collective-permute-start | bytes 110600 | tf_op jit(solution)/shard_map/ppermute | solution.py:234
  37.6 0.5 %collective-permute-start.15 = (bf16[3,48,128]{2,1,0:T(8,128)(2,1)S(1)}, bf16[3,48,128]{2,1,0:T(8,128)(2,1)S(1)}, u32[]{:S(2)}, u32[]{:S(2)}) collective-permute-start(bf16[3,48,128]{2,1,0:T(8,128)(2,1)S(1)} %get-tuple-element.44), channel_id=1, source_target_pairs={{0,8},{4,12},{8,0},{12,4},{16,24},{20,28},{24,16},{28,20},{1,9},{5... | collective-permute-start | bytes 110600 | tf_op jit(solution)/shard_map/ppermute | solution.py:234
  38.2 1.5 %collective-permute-start.16 = (bf16[3,48,128]{2,1,0:T(8,128)(2,1)S(1)}, bf16[3,48,128]{2,1,0:T(8,128)(2,1)S(1)}, u32[]{:S(2)}, u32[]{:S(2)}) collective-permute-start(bf16[3,48,128]{2,1,0:T(8,128)(2,1)S(1)} %get-tuple-element.45), channel_id=1, source_target_pairs={{0,4},{4,0},{8,12},{12,8},{16,20},{20,16},{24,28},{28,24},{1,5},{5... | collective-permute-start | bytes 110600 | tf_op jit(solution)/shard_map/ppermute | solution.py:234
  39.6 1.3 %collective-permute-done.13.refs_4_.rest_4_ = bf16[3,48,128]{2,1,0:T(8,128)(2,1)S(1)} collective-permute-done((bf16[3,48,128]{2,1,0:T(8,128)(2,1)S(1)}, bf16[3,48,128]{2,1,0:T(8,128)(2,1)S(1)}, u32[]{:S(2)}, u32[]{:S(2)}) %collective-permute-start.13) | collective-permute-done | bytes 36896 | tf_op jit(solution)/shard_map/ppermute | solution.py:234
  41.0 0.4 collective-permute-done.14.refs_5_.rest_5_
  41.4 0.2 collective-permute-done.15.refs_6_.rest_6_
  41.6 0.5 %collective-permute-done.16.refs_7_.rest_7_ = bf16[3,48,128]{2,1,0:T(8,128)(2,1)S(1)} collective-permute-done((bf16[3,48,128]{2,1,0:T(8,128)(2,1)S(1)}, bf16[3,48,128]{2,1,0:T(8,128)(2,1)S(1)}, u32[]{:S(2)}, u32[]{:S(2)}) %collective-permute-start.16) | collective-permute-done | bytes 36896 | tf_op jit(solution)/shard_map/ppermute | solution.py:234
  42.2 0.1 collective-permute-start.17
  42.2 1.7 %own.1.whole_ref = bf16[6,384,128]{2,1,0:T(8,128)(2,1)} custom-call(s32[24]{0:T(128)S(1)} %copy-done, bf16[6,384,128]{2,1,0:T(8,128)(2,1)S(1)} %get-tuple-element.46.spatial_ref, bf16[3,48,128]{2,1,0:T(8,128)(2,1)S(1)} %get-tuple-element.38.refs_0_.rest_0_, bf16[3,48,128]{2,1,0:T(8,128)(2,1)S(1)} %collective-permute-done.10.refs_1_.rest_1_, ...), custom_call_target="tpu_custom_call" | custom-call | tf_op jit(solution)/shard_map/own/pallas_call | solution.py:286
  43.9 0.6 %merge.1 = bf16[6,384,128]{2,1,0:T(8,128)(2,1)} custom-call(s32[24]{0:T(128)S(1)} %copy-done, bf16[2,384,128]{2,1,0:T(8,128)(2,1)S(1)} %collective-permute-done.17.given_ref, bf16[6,384,128]{2,1,0:T(8,128)(2,1)} %own.1.whole_ref), custom_call_target="tpu_custom_call", output_to_operand_aliasing={{}: (2, {})} | custom-call | tf_op jit(solution)/shard_map/merge/pallas_call | solution.py:295
  (15 shorter events, 0.1 us)
Async XLA Ops:
  0.0 3.3 %collective-permute-start = (bf16[6,384,128]{2,1,0:T(8,128)(2,1)}, bf16[6,384,128]{2,1,0:T(8,128)(2,1)S(1)}, u32[]{:S(2)}, u32[]{:S(2)}) collective-permute-start(bf16[6,384,128]{2,1,0:T(8,128)(2,1)} %bitcast.12), channel_id=1, source_target_pairs={{0,1},{1,0},{2,3},{3,2},{4,5},{5,4},{6,7},{7,6},{8,9},{9,8},{10,11... | collective-permute-start | bytes 1769480 | tf_op jit(solution)/shard_map/ppermute | solution.py:231
  0.5 0.7 %copy-start = (s32[24]{0:T(128)S(1)}, s32[24]{0:T(128)}, u32[]{:S(2)}) copy-start(s32[24]{0:T(128)} %class_ref.9) | copy-start | bytes 292
  0.5 2.9 %collective-permute-start.1 = (bf16[6,384,128]{2,1,0:T(8,128)(2,1)}, bf16[6,384,128]{2,1,0:T(8,128)(2,1)S(1)}, u32[]{:S(2)}, u32[]{:S(2)}) collective-permute-start(bf16[6,384,128]{2,1,0:T(8,128)(2,1)} %bitcast.14), channel_id=1, source_target_pairs={{0,1},{1,0},{2,3},{3,2},{4,5},{5,4},{6,7},{7,6},{8,9},{9,8},{10,11... | collective-permute-start | bytes 1769480 | tf_op jit(solution)/shard_map/ppermute | solution.py:231
  0.5 3.5 %collective-permute-start.2 = (bf16[6,384,128]{2,1,0:T(8,128)(2,1)}, bf16[6,384,128]{2,1,0:T(8,128)(2,1)S(1)}, u32[]{:S(2)}, u32[]{:S(2)}) collective-permute-start(bf16[6,384,128]{2,1,0:T(8,128)(2,1)} %bitcast.16), channel_id=1, source_target_pairs={{0,1},{1,0},{2,3},{3,2},{4,5},{5,4},{6,7},{7,6},{8,9},{9,8},{10,11... | collective-permute-start | bytes 1769480 | tf_op jit(solution)/shard_map/ppermute | solution.py:231
  4.7 10.0 %collective-permute-start.3 = (bf16[3,3,48,128]{3,2,1,0:T(8,128)(2,1)S(1)}, bf16[3,3,48,128]{3,2,1,0:T(8,128)(2,1)S(1)}, u32[]{:S(2)}, u32[]{:S(2)}) collective-permute-start(bf16[3,3,48,128]{3,2,1,0:T(8,128)(2,1)S(1)} %get-tuple-element.31), channel_id=1, source_target_pairs={{0,16},{4,20},{8,24},{12,28},{16,0},{20,4},{24,8},{28,12},{1,17},{... | collective-permute-start | bytes 331784 | tf_op jit(solution)/shard_map/ppermute | solution.py:234
  8.7 8.7 %collective-permute-start.4 = (bf16[3,3,48,128]{3,2,1,0:T(8,128)(2,1)S(1)}, bf16[3,3,48,128]{3,2,1,0:T(8,128)(2,1)S(1)}, u32[]{:S(2)}, u32[]{:S(2)}) collective-permute-start(bf16[3,3,48,128]{3,2,1,0:T(8,128)(2,1)S(1)} %get-tuple-element.32), channel_id=1, source_target_pairs={{0,8},{4,12},{8,0},{12,4},{16,24},{20,28},{24,16},{28,20},{1,9},{5... | collective-permute-start | bytes 331784 | tf_op jit(solution)/shard_map/ppermute | solution.py:234
  10.3 13.7 %collective-permute-start.5 = (bf16[3,3,48,128]{3,2,1,0:T(8,128)(2,1)S(1)}, bf16[3,3,48,128]{3,2,1,0:T(8,128)(2,1)S(1)}, u32[]{:S(2)}, u32[]{:S(2)}) collective-permute-start(bf16[3,3,48,128]{3,2,1,0:T(8,128)(2,1)S(1)} %get-tuple-element.33), channel_id=1, source_target_pairs={{0,20},{4,16},{8,28},{12,24},{16,4},{20,0},{24,12},{28,8},{1,21},{... | collective-permute-start | bytes 331784 | tf_op jit(solution)/shard_map/ppermute | solution.py:234
  11.5 12.4 %collective-permute-start.6 = (bf16[3,3,48,128]{3,2,1,0:T(8,128)(2,1)S(1)}, bf16[3,3,48,128]{3,2,1,0:T(8,128)(2,1)S(1)}, u32[]{:S(2)}, u32[]{:S(2)}) collective-permute-start(bf16[3,3,48,128]{3,2,1,0:T(8,128)(2,1)S(1)} %get-tuple-element.34), channel_id=1, source_target_pairs={{0,24},{4,28},{8,16},{12,20},{16,8},{20,12},{24,0},{28,4},{1,25},{... | collective-permute-start | bytes 331784 | tf_op jit(solution)/shard_map/ppermute | solution.py:234
  14.0 6.3 %copy-start.1 = (s32[4,4]{1,0:T(4,128)S(1)}, s32[4,4]{1,0:T(4,128)}, u32[]{:S(2)}) copy-start(s32[4,4]{1,0:T(4,128)} %mask_ref.1) | copy-start | bytes 196
  14.0 9.9 %collective-permute-start.7 = (bf16[3,3,48,128]{3,2,1,0:T(8,128)(2,1)S(1)}, bf16[3,3,48,128]{3,2,1,0:T(8,128)(2,1)S(1)}, u32[]{:S(2)}, u32[]{:S(2)}) collective-permute-start(bf16[3,3,48,128]{3,2,1,0:T(8,128)(2,1)S(1)} %get-tuple-element.35), channel_id=1, source_target_pairs={{0,12},{4,8},{8,4},{12,0},{16,28},{20,24},{24,20},{28,16},{1,13},{... | collective-permute-start | bytes 331784 | tf_op jit(solution)/shard_map/ppermute | solution.py:234
  14.6 9.3 %collective-permute-start.8 = (bf16[3,3,48,128]{3,2,1,0:T(8,128)(2,1)S(1)}, bf16[3,3,48,128]{3,2,1,0:T(8,128)(2,1)S(1)}, u32[]{:S(2)}, u32[]{:S(2)}) collective-permute-start(bf16[3,3,48,128]{3,2,1,0:T(8,128)(2,1)S(1)} %get-tuple-element.36), channel_id=1, source_target_pairs={{0,4},{4,0},{8,12},{12,8},{16,20},{20,16},{24,28},{28,24},{1,5},{5... | collective-permute-start | bytes 331784 | tf_op jit(solution)/shard_map/ppermute | solution.py:234
  17.4 8.7 %collective-permute-start.9 = (bf16[3,3,48,128]{3,2,1,0:T(8,128)(2,1)S(1)}, bf16[3,3,48,128]{3,2,1,0:T(8,128)(2,1)S(1)}, u32[]{:S(2)}, u32[]{:S(2)}) collective-permute-start(bf16[3,3,48,128]{3,2,1,0:T(8,128)(2,1)S(1)} %get-tuple-element.37), channel_id=1, source_target_pairs={{0,28},{4,24},{8,20},{12,16},{16,12},{20,8},{24,4},{28,0},{1,29},{... | collective-permute-start | bytes 331784 | tf_op jit(solution)/shard_map/ppermute | solution.py:234
  27.0 10.6 %collective-permute-start.10 = (bf16[3,48,128]{2,1,0:T(8,128)(2,1)S(1)}, bf16[3,48,128]{2,1,0:T(8,128)(2,1)S(1)}, u32[]{:S(2)}, u32[]{:S(2)}) collective-permute-start(bf16[3,48,128]{2,1,0:T(8,128)(2,1)S(1)} %get-tuple-element.39), channel_id=1, source_target_pairs={{0,24},{4,28},{8,16},{12,20},{16,8},{20,12},{24,0},{28,4},{1,25},{... | collective-permute-start | bytes 110600 | tf_op jit(solution)/shard_map/ppermute | solution.py:234
  29.8 8.4 %collective-permute-start.11 = (bf16[3,48,128]{2,1,0:T(8,128)(2,1)S(1)}, bf16[3,48,128]{2,1,0:T(8,128)(2,1)S(1)}, u32[]{:S(2)}, u32[]{:S(2)}) collective-permute-start(bf16[3,48,128]{2,1,0:T(8,128)(2,1)S(1)} %get-tuple-element.40), channel_id=1, source_target_pairs={{0,28},{4,24},{8,20},{12,16},{16,12},{20,8},{24,4},{28,0},{1,29},{... | collective-permute-start | bytes 110600 | tf_op jit(solution)/shard_map/ppermute | solution.py:234
  30.9 8.8 %collective-permute-start.12 = (bf16[3,48,128]{2,1,0:T(8,128)(2,1)S(1)}, bf16[3,48,128]{2,1,0:T(8,128)(2,1)S(1)}, u32[]{:S(2)}, u32[]{:S(2)}) collective-permute-start(bf16[3,48,128]{2,1,0:T(8,128)(2,1)S(1)} %get-tuple-element.41), channel_id=1, source_target_pairs={{0,16},{4,20},{8,24},{12,28},{16,0},{20,4},{24,8},{28,12},{1,17},{... | collective-permute-start | bytes 110600 | tf_op jit(solution)/shard_map/ppermute | solution.py:234
  35.2 5.8 %collective-permute-start.13 = (bf16[3,48,128]{2,1,0:T(8,128)(2,1)S(1)}, bf16[3,48,128]{2,1,0:T(8,128)(2,1)S(1)}, u32[]{:S(2)}, u32[]{:S(2)}) collective-permute-start(bf16[3,48,128]{2,1,0:T(8,128)(2,1)S(1)} %get-tuple-element.42), channel_id=1, source_target_pairs={{0,20},{4,16},{8,28},{12,24},{16,4},{20,0},{24,12},{28,8},{1,21},{... | collective-permute-start | bytes 110600 | tf_op jit(solution)/shard_map/ppermute | solution.py:234
  36.1 5.2 %collective-permute-start.14 = (bf16[3,48,128]{2,1,0:T(8,128)(2,1)S(1)}, bf16[3,48,128]{2,1,0:T(8,128)(2,1)S(1)}, u32[]{:S(2)}, u32[]{:S(2)}) collective-permute-start(bf16[3,48,128]{2,1,0:T(8,128)(2,1)S(1)} %get-tuple-element.43), channel_id=1, source_target_pairs={{0,12},{4,8},{8,4},{12,0},{16,28},{20,24},{24,20},{28,16},{1,13},{... | collective-permute-start | bytes 110600 | tf_op jit(solution)/shard_map/ppermute | solution.py:234
  37.6 4.0 %collective-permute-start.15 = (bf16[3,48,128]{2,1,0:T(8,128)(2,1)S(1)}, bf16[3,48,128]{2,1,0:T(8,128)(2,1)S(1)}, u32[]{:S(2)}, u32[]{:S(2)}) collective-permute-start(bf16[3,48,128]{2,1,0:T(8,128)(2,1)S(1)} %get-tuple-element.44), channel_id=1, source_target_pairs={{0,8},{4,12},{8,0},{12,4},{16,24},{20,28},{24,16},{28,20},{1,9},{5... | collective-permute-start | bytes 110600 | tf_op jit(solution)/shard_map/ppermute | solution.py:234
  38.2 4.0 %collective-permute-start.16 = (bf16[3,48,128]{2,1,0:T(8,128)(2,1)S(1)}, bf16[3,48,128]{2,1,0:T(8,128)(2,1)S(1)}, u32[]{:S(2)}, u32[]{:S(2)}) collective-permute-start(bf16[3,48,128]{2,1,0:T(8,128)(2,1)S(1)} %get-tuple-element.45), channel_id=1, source_target_pairs={{0,4},{4,0},{8,12},{12,8},{16,20},{20,16},{24,28},{28,24},{1,5},{5... | collective-permute-start | bytes 110600 | tf_op jit(solution)/shard_map/ppermute | solution.py:234
  42.2 1.7 %collective-permute-start.17 = (bf16[2,384,128]{2,1,0:T(8,128)(2,1)S(1)}, bf16[2,384,128]{2,1,0:T(8,128)(2,1)S(1)}, u32[]{:S(2)}, u32[]{:S(2)}) collective-permute-start(bf16[2,384,128]{2,1,0:T(8,128)(2,1)S(1)} %gather.1), channel_id=1, source_target_pairs={{0,1},{1,0},{2,3},{3,2},{4,5},{5,4},{6,7},{7,6},{8,9},{9,8},{10,11... | collective-permute-start | bytes 589832 | tf_op jit(solution)/shard_map/ppermute | solution.py:231
